TPU v7x, 32 devices: a whole 2x2x4 slice. The times are simulated.
32 devices in a mesh: groups: 2 (over y), chan: 4 (over z), rows: 2 (over x), cols: 2 (over core).
Axes of the slice: x: 2, y: 2, z: 4, core: 2. Of those that a mesh axis runs over, the one named last changes fastest.
Arguments:
- image: bfloat16 [1536, 16, 256], P('chan', ('groups', 'rows'), 'cols'), parts along dimension 1, may hold values from -40 to 40
- kernel: float32 [1536, 49], P('chan'), may hold values from -0.875 to 0.875
- layer_norm_weight: float32 [1536], P('chan'), may hold values from 0.1 to 1.9
- w_expand: bfloat16 [6144, 1536], P('chan'), may hold values from -0.21875 to 0.21875
- bias_expand: float32 [6144], P('chan'), may hold values from -3 to 3
- w_reduce: bfloat16 [1536, 6144], P(None, 'chan'), may hold values from -0.109375 to 0.109375
- layer_scale: float32 [1536], P('chan'), may hold values from 0.5 to 2
- cotangent: bfloat16 [1536, 16, 256], P('chan', ('groups', 'rows'), 'cols'), parts along dimension 1, may hold values from -6 to 6
Outputs:
- output: bfloat16 [1536, 16, 256], P('chan', ('groups', 'rows'), 'cols'), parts along dimension 1
- grad_input: bfloat16 [1536, 16, 256], P('chan', ('groups', 'rows'), 'cols'), parts along dimension 1
- grad_expand: bfloat16 [12288, 1536], P(('groups', 'chan')), parts along dimension 0
- grad_reduce: bfloat16 [3072, 6144], P('groups', 'chan'), parts along dimension 0
- grad_kernel: float32 [3072, 49], P(('groups', 'chan')), parts along dimension 0
There are 2 independent parts, one for each index of `groups`. A program takes and returns all parts, laid end to end along the dimension named above; an argument that names none is the same for every part. Nothing has to cross between parts.
All inputs are finite; a program needn't handle non-finite values.
Results may differ from a plain program's by a relative error of at most 0.015.
Values may be sent and summed in bfloat16 or wider, within the bound.
No kernel may reach another device: no remote copies, remote signals or barrier semaphores. Data moves between devices by JAX's collectives and lax.ppermute only.
A program may use at most 128 MiB of HBM per device.

v0:
```python
import jax
import jax.numpy as jnp
from jax import lax
from jax.sharding import PartitionSpec as P

KS = 7


epsilon = 1e-06


def extended(block, sides, width):
    for axis, dim in sides:
        count = lax.axis_size(axis)
        forward = [(i, i + 1) for i in range(count - 1)]
        backward = [(target, source) for source, target in forward]
        low = lax.ppermute(
            lax.slice_in_dim(block, block.shape[dim] - width, None, axis=dim), axis, forward
        )
        high = lax.ppermute(lax.slice_in_dim(block, 0, width, axis=dim), axis, backward)
        block = jnp.concatenate([low, block, high], axis=dim)
    return block


def gelu_exact(values):
    return 0.5 * values * (1.0 + lax.erf(values * 0.7071067811865476))


def gelu_slope(values):
    return (
        0.5 * (1.0 + lax.erf(values * 0.7071067811865476))
        + values * jnp.exp(-0.5 * values * values) * 0.3989422804014327
    )


def on_device(
    image, kernel, layer_norm_weight, w_expand, bias_expand, w_reduce, layer_scale, cotangent
):
    channel_slice, tile_rows, tile_cols = image.shape
    pixel_count = tile_rows * tile_cols
    every_channel = w_reduce.shape[0]
    half_side = KS // 2
    padded = extended(image, (("rows", 1), ("cols", 2)), half_side)
    padded_wide = padded.astype(jnp.float32)
    conv = jnp.zeros((channel_slice, tile_rows, tile_cols), jnp.float32)
    for tap_row in range(KS):
        for tap_col in range(KS):
            weight = kernel[:, tap_row * KS + tap_col][:, None, None]
            conv = (
                conv
                + weight
                * padded_wide[:, tap_row : tap_row + tile_rows, tap_col : tap_col + tile_cols]
            )
    mean_map = lax.psum(jnp.sum(conv, axis=0), "chan") / every_channel
    mean_removed = conv - mean_map
    var_map = lax.psum(jnp.sum(mean_removed * mean_removed, axis=0), "chan") / every_channel
    inverse_deviation = lax.rsqrt(var_map + epsilon)
    normalized_input = mean_removed * inverse_deviation
    norm_output = (
        (normalized_input * layer_norm_weight[:, None, None])
        .astype(jnp.bfloat16)
        .reshape(channel_slice, pixel_count)
    )
    normed_full = lax.all_gather(norm_output, "chan", axis=0, tiled=True)
    pre_act = jnp.dot(w_expand, normed_full, preferred_element_type=jnp.float32)
    pre_act = pre_act + bias_expand[:, None]
    hidden = gelu_exact(pre_act).astype(jnp.bfloat16)
    weight_rows = w_reduce
    reduced = lax.psum_scatter(
        jnp.dot(weight_rows, hidden, preferred_element_type=jnp.float32).astype(jnp.bfloat16),
        "chan",
        scatter_dimension=0,
        tiled=True,
    ).astype(jnp.float32)
    image_flat = image.reshape(channel_slice, pixel_count).astype(jnp.float32)
    output = (
        (image_flat + layer_scale[:, None] * reduced)
        .astype(jnp.bfloat16)
        .reshape(channel_slice, tile_rows, tile_cols)
    )
    scaled_cot = (
        layer_scale[:, None] * cotangent.reshape(channel_slice, pixel_count).astype(jnp.float32)
    ).astype(jnp.bfloat16)
    block_rows = lax.all_gather(scaled_cot, "chan", axis=0, tiled=True)
    weight_rows = w_reduce
    grad_hidden = lax.dot_general(
        weight_rows, block_rows, (((0,), (0,)), ((), ())), preferred_element_type=jnp.float32
    )
    outer = lax.dot_general(
        block_rows, hidden, (((1,), (1,)), ((), ())), preferred_element_type=jnp.float32
    )
    grad_reduce = outer
    grad_hidden, grad_reduce = (grad_hidden, grad_reduce)
    grad_pre = (grad_hidden * gelu_slope(pre_act)).astype(jnp.bfloat16)
    grad_expand = lax.dot_general(
        grad_pre, normed_full, (((1,), (1,)), ((), ())), preferred_element_type=jnp.float32
    )
    grad_normed = (
        lax.psum_scatter(
            lax.dot_general(
                w_expand, grad_pre, (((0,), (0,)), ((), ())), preferred_element_type=jnp.float32
            ).astype(jnp.bfloat16),
            "chan",
            scatter_dimension=0,
            tiled=True,
        )
        .astype(jnp.float32)
        .reshape(channel_slice, tile_rows, tile_cols)
    )
    normalized_gradient = grad_normed * layer_norm_weight[:, None, None]
    first_gradient, cross_gradient = lax.psum(
        (
            jnp.sum(normalized_gradient, axis=0),
            jnp.sum(normalized_gradient * normalized_input, axis=0),
        ),
        "chan",
    )
    convolution_gradient = (
        normalized_gradient
        - first_gradient / every_channel
        - normalized_input * (cross_gradient / every_channel)
    ) * inverse_deviation
    grad_padded = extended(
        convolution_gradient.astype(jnp.bfloat16), (("rows", 1), ("cols", 2)), half_side
    ).astype(convolution_gradient.dtype)
    back_conv = jnp.zeros((channel_slice, tile_rows, tile_cols), jnp.float32)
    kernel_terms = []
    for tap_row in range(KS):
        for tap_col in range(KS):
            weight = kernel[:, tap_row * KS + tap_col][:, None, None]
            row_first = 2 * half_side - tap_row
            col_first = 2 * half_side - tap_col
            back_conv = (
                back_conv
                + weight
                * grad_padded[
                    :, row_first : row_first + tile_rows, col_first : col_first + tile_cols
                ]
            )
            product = (
                convolution_gradient
                * padded_wide[:, tap_row : tap_row + tile_rows, tap_col : tap_col + tile_cols]
            )
            kernel_terms.append(jnp.sum(product, axis=(1, 2)))
    kernel_local = jnp.stack(kernel_terms, axis=1)
    grad_input = (cotangent.astype(jnp.float32) + back_conv).astype(jnp.bfloat16)
    grad_expand, grad_reduce, grad_kernel = (
        lax.psum(grad_expand.astype(jnp.bfloat16), ("rows", "cols")).astype(jnp.float32),
        lax.psum(grad_reduce.astype(jnp.bfloat16), ("rows", "cols")).astype(jnp.float32),
        lax.psum(kernel_local.astype(jnp.bfloat16), ("rows", "cols")).astype(jnp.float32),
    )
    return (
        output,
        grad_input,
        grad_expand.astype(jnp.bfloat16),
        grad_reduce.astype(jnp.bfloat16),
        grad_kernel,
    )


def solution(mesh):
    placed = (
        P("chan", ("groups", "rows"), "cols"),
        P("chan", None),
        P("chan"),
        P("chan", None),
        P("chan"),
        P(None, "chan"),
        P("chan"),
        P("chan", ("groups", "rows"), "cols"),
    )
    return jax.shard_map(
        on_device,
        mesh=mesh,
        in_specs=placed,
        out_specs=(
            P("chan", ("groups", "rows"), "cols"),
            P("chan", ("groups", "rows"), "cols"),
            P(("groups", "chan"), None),
            P("groups", "chan"),
            P(("groups", "chan"), None),
        ),
        check_vma=False,
    )
```

profile of v0, /device:TPU:0, one launch (start us, length us, event | category | flops | bytes accessed | tf_op | source)
XLA Modules:
  0.0 431.5 jit_solution(10395118376842621070)
XLA Ops:
  7.2 1.4 copy.35
  8.9 4.9 %collective-permute-start = (bf16[384,3,128]{0,1,2:T(4,128)(2,1)S(1)}, bf16[384,3,128]{0,1,2:T(4,128)(2,1)S(1)}, u32[]{:S(2)}, u32[]{:S(2)}) collective-permute-start(bf16[384,3,128]{0,1,2:T(4,128)(2,1)S(1)} %get-tuple-element.132), channel_id=1, source_target_pairs={{0,2},{1,3},{4,6},{5,7},{8,10},{9,11},{12,14},{13,15},{16,18},{17,... | collective-permute-start | bytes 884744 | tf_op jit(solution)/shard_map/ppermute | solution.py:17
  13.7 1.3 collective-permute-start.1
  15.3 6.8 %collective-permute-done = bf16[384,3,128]{0,1,2:T(4,128)(2,1)S(1)} collective-permute-done((bf16[384,3,128]{0,1,2:T(4,128)(2,1)S(1)}, bf16[384,3,128]{0,1,2:T(4,128)(2,1)S(1)}, u32[]{:S(2)}, u32[]{:S(2)}) %collective-permute-start) | collective-permute-done | bytes 294944 | tf_op jit(solution)/shard_map/ppermute | solution.py:17
  22.1 4.1 collective-permute-done.1
  26.2 1.0 pad_maximum_fusion
  27.2 1.3 collective-permute-start.2
  28.5 1.3 collective-permute-start.3
  30.2 1.5 collective-permute-done.3
  31.9 5.7 %fusion.61 = (f32[4,128]{1,0:T(4,128)S(1)}, f32[384,4,128]{0,2,1:T(8,128)S(1)}) fusion(f32[384,10,134]{0,2,1:T(8,128)S(1)} %maximum_convert_fusion, f32[384]{0:T(512)S(1)} %get-tuple-element.116, f32[384]{0:T(512)S(1)} %get-tuple-element.117, f32[384]{0:T(512)S(1)} %get-tuple-element.70, f32[384]{0:T(512)S(1)} %get-tuple-element.71, ...), kind=kLoop, calls=%fused_computation.236 | loop fusion | flops 19267072 | bytes 39398912 | tf_op jit(solution)/shard_map/reduce_sum | solution.py:54
  37.7 12.0 %psum.49 = f32[4,128]{1,0:T(4,128)S(1)} all-reduce(f32[4,128]{1,0:T(4,128)S(1)} %get-tuple-element.123), channel_id=1, replica_groups=mesh['groups'=2,'chan'=4,'rows'=2,'cols'=2] {'chan'}, use_global_device_ids=true, to_apply=%region_1.0 | all-reduce | flops 512 | bytes 4096 | tf_op jit(solution)/shard_map/psum | solution.py:54
  49.9 8.4 %psum.50 = f32[4,128]{1,0:T(4,128)S(1)} all-reduce(f32[4,128]{1,0:T(4,128)S(1)} %multiply_reduce_fusion.51), channel_id=1, replica_groups=mesh['groups'=2,'chan'=4,'rows'=2,'cols'=2] {'chan'}, use_global_device_ids=true, to_apply=%region_3.0 | all-reduce | flops 512 | bytes 4096 | tf_op jit(solution)/shard_map/psum | solution.py:56
  58.3 1.0 multiply_convert_fusion.1
  59.3 35.9 %all-gather.3.cloned.1.call-done = bf16[1536,512]{0,1:T(8,128)(2,1)} async-done(((bf16[384,512]{0,1:T(8,128)(2,1)}), bf16[1536,512]{0,1:T(8,128)(2,1)}) %all-gather.3.cloned.1.call-update) | async-done | bytes 1572880 | tf_op jit(solution)/shard_map/all_gather | solution.py:64
  95.2 7.3 %multiply_convert_fusion = (bf16[1536,512]{0,1:T(8,128)(2,1)S(1)}, f32[1536,512]{0,1:T(8,128)}) fusion(f32[1536]{0:T(1024)S(1)} %copy-done.15, bf16[1536,512]{0,1:T(8,128)(2,1)} %all-gather.3.cloned.1.call-done, bf16[1536,1536]{1,0:T(8,128)(2,1)} %param.11), kind=kOutput, calls=%fused_computation.11 | convolution fusion | flops 2420637696 | bytes 11016192 | tf_op jit(solution)/shard_map/dot_general | solution.py:65
  102.5 1.1 copy-done.16
  103.7 6.1 %fusion.7 = bf16[1536,512]{0,1:T(8,128)(2,1)} fusion(bf16[1536,512]{0,1:T(8,128)(2,1)S(1)} %get-tuple-element.136, bf16[1536,1536]{1,0:T(8,128)(2,1)} %param.13), kind=kOutput, calls=%fused_computation.16 | convolution fusion | flops 2416705536 | bytes 7864320 | tf_op jit(solution)/shard_map/dot_general | solution.py:70
  109.8 2.6 copy.48
  112.5 1.1 copy.34
  113.6 1.2 copy.41
  114.9 31.9 %reduce-scatter.7.cloned.1.call-done = bf16[384,512]{1,0:T(8,128)(2,1)} async-done(((bf16[1536,512]{1,0:T(8,128)(2,1)}), bf16[384,512]{1,0:T(8,128)(2,1)}) %reduce-scatter.7.cloned.1.call-update) | async-done | bytes 393232
  146.8 1.9 copy.49
  148.7 2.3 fusion.59
  151.3 36.0 %all-gather.5.cloned.1.call-done = bf16[1536,512]{0,1:T(8,128)(2,1)} async-done(((bf16[384,512]{0,1:T(8,128)(2,1)}), bf16[1536,512]{0,1:T(8,128)(2,1)}) %all-gather.5.cloned.1.call-update) | async-done | bytes 1572880 | tf_op jit(solution)/shard_map/all_gather | solution.py:84
  187.3 6.9 %fusion.6 = bf16[1536,512]{0,1:T(8,128)(2,1)S(1)} fusion(f32[1536,512]{0,1:T(8,128)} %get-tuple-element.137, bf16[1536,512]{0,1:T(8,128)(2,1)} %all-gather.5.cloned.1.call-done, bf16[1536,1536]{1,0:T(8,128)(2,1)} %param.13), kind=kOutput, calls=%fused_computation.13 | convolution fusion | flops 2423783424 | bytes 11010048 | tf_op jit(solution)/shard_map/dot_general | solution.py:86
  194.3 1.1 copy-done.17
  195.4 6.0 %fusion.8 = bf16[1536,512]{0,1:T(8,128)(2,1)} fusion(bf16[1536,512]{0,1:T(8,128)(2,1)S(1)} %fusion.6, bf16[1536,1536]{1,0:T(8,128)(2,1)} %param.11), kind=kOutput, calls=%fused_computation.17 | convolution fusion | flops 2416705536 | bytes 7864320 | tf_op jit(solution)/shard_map/dot_general | solution.py:100
  201.4 2.6 copy.50
  204.1 6.9 %convolution_convert_fusion = bf16[1536,1536]{1,0:T(8,128)(2,1)} fusion(bf16[1536,512]{0,1:T(8,128)(2,1)} %all-gather.5.cloned.1.call-done, bf16[1536,512]{0,1:T(8,128)(2,1)} %copy-done.16), kind=kOutput, calls=%fused_computation | convolution fusion | flops 2418278400 | bytes 7864320 | tf_op jit(solution)/shard_map/dot_general | solution.py:89
  211.0 4.3 convolution_convert_fusion.1
  215.3 1.0 copy-done.4
  216.3 1.0 copy.46
  217.3 21.2 %reduce-scatter.9.cloned.1.call-done = bf16[384,512]{1,0:T(8,128)(2,1)} async-done(((bf16[1536,512]{1,0:T(8,128)(2,1)}), bf16[384,512]{1,0:T(8,128)(2,1)}) %reduce-scatter.9.cloned.1.call-update) | async-done | bytes 393232
  238.5 1.2 copy.51
  240.2 9.8 %all-reduce = (f32[4,128]{1,0:T(4,128)S(1)}, f32[4,128]{1,0:T(4,128)S(1)}) all-reduce(f32[4,128]{1,0:T(4,128)S(1)} %multiply_reduce_fusion.49, f32[4,128]{1,0:T(4,128)S(1)} %bitcast.43), channel_id=1, replica_groups=mesh['groups'=2,'chan'=4,'rows'=2,'cols'=2] {'chan'}, use_global_device_ids=true, to_apply=%region_9.0 | all-reduce | flops 1024 | bytes 8192 | tf_op jit(solution)/shard_map/psum | solution.py:111
  250.0 2.2 multiply_reduce_fusion
  252.2 0.6 stack.248
  255.0 0.6 stack.243
  255.6 0.6 stack.242
  256.1 0.6 stack.241
  256.7 0.6 stack.240
  258.4 0.6 stack.237
  259.0 0.6 stack.236
  259.6 0.6 stack.235
  260.1 0.6 stack.234
  260.7 0.6 stack.233
  261.3 0.6 stack.232
  262.5 1.8 multiply_reduce_fusion.18
  264.3 0.8 fusion.63
  265.1 3.3 collective-permute-start.4
  268.4 1.5 collective-permute-start.5
  269.9 1.1 multiply_reduce_fusion.36
  271.4 3.0 stack.249
  274.5 7.1 %collective-permute-done.4 = bf16[384,3,128]{0,2,1:T(8,128)(2,1)S(1)} collective-permute-done((bf16[384,3,128]{0,2,1:T(8,128)(2,1)}, bf16[384,3,128]{0,2,1:T(8,128)(2,1)S(1)}, u32[]{:S(2)}, u32[]{:S(2)}) %collective-permute-start.4) | collective-permute-done | bytes 294944 | tf_op jit(solution)/shard_map/ppermute | solution.py:17
  281.5 4.0 collective-permute-done.5
  285.6 1.3 collective-permute-start.7
  286.9 3.0 collective-permute-start.6
  290.0 12.2 %psum.55 = bf16[384,49]{0,1:T(8,128)(2,1)S(1)} all-reduce(bf16[384,49]{0,1:T(8,128)(2,1)S(1)} %stack.249), channel_id=1, replica_groups=mesh['groups'=2,'chan'=4,'rows'=2,'cols'=2] {'rows','cols'}, use_global_device_ids=true, to_apply=%region_61.0 | all-reduce | flops 18816 | bytes 75264 | tf_op jit(solution)/shard_map/psum | solution.py:150
  302.2 0.6 convert_element_type.96
  303.1 5.8 %fusion.11 = bf16[384,4,128]{0,2,1:T(8,128)(2,1)S(1)} fusion(f32[384,10,134]{0,2,1:T(8,128)S(1)} %maximum_convert_fusion.1, f32[384]{0:T(512)S(1)} %copy-done.10, f32[384]{0:T(512)S(1)} %copy-done.12, f32[384]{0:T(512)S(1)} %get-tuple-element.70, f32[384]{0:T(512)S(1)} %get-tuple-element.71, f32[384]{0:T(512)S(1)} %get-tuple-element.72, ...), kind=kLoop, calls=%fused_computation.24 | loop fusion | flops 19660800 | bytes 39396864 | tf_op jit(solution)/shard_map/convert_element_type | solution.py:146
  308.9 1.0 copy.47
  309.9 107.9 %all-reduce.4.cloned.1.call-done = (bf16[1536,1536]{1,0:T(8,128)(2,1)}, bf16[1536,1536]{1,0:T(8,128)(2,1)}) async-done(((bf16[1536,1536]{1,0:T(8,128)(2,1)}, bf16[1536,1536]{1,0:T(8,128)(2,1)}), (bf16[1536,1536]{1,0:T(8,128)(2,1)}, bf16[1536,1536]{1,0:T(8,128)(2,1)})) %all-reduce.4.cloned.1.call-update) | async-done | bytes 9437200 | tf_op jit(solution)/shard_map/psum | solution.py:148
  417.8 5.0 %copy.54 = bf16[1536,1536]{1,0:T(8,128)(2,1)} copy(bf16[1536,1536]{1,0:T(8,128)(2,1)} %get-tuple-element.142) | data formatting | bytes 9437184
  422.8 2.2 copy.55
  (108 shorter events, 6.6 us)
Async XLA Ops:
  7.2 7.9 %copy-start.5 = (f32[384,49]{0,1:T(8,128)S(1)}, f32[384,49]{0,1:T(8,128)}, u32[]{:S(2)}) copy-start(f32[384,49]{0,1:T(8,128)} %param.9) | copy-start | bytes 225796
  7.2 88.1 %all-gather.3.cloned.1.call-start = ((), (), s32[]{:S(2)}) async-start(), calls=%async_computation.2 | async-start | bytes 1966080 | tf_op jit(solution)/shard_map/all_gather | solution.py:64
  8.9 13.2 %collective-permute-start = (bf16[384,3,128]{0,1,2:T(4,128)(2,1)S(1)}, bf16[384,3,128]{0,1,2:T(4,128)(2,1)S(1)}, u32[]{:S(2)}, u32[]{:S(2)}) collective-permute-start(bf16[384,3,128]{0,1,2:T(4,128)(2,1)S(1)} %get-tuple-element.132), channel_id=1, source_target_pairs={{0,2},{1,3},{4,6},{5,7},{8,10},{9,11},{12,14},{13,15},{16,18},{17,... | collective-permute-start | bytes 884744 | tf_op jit(solution)/shard_map/ppermute | solution.py:17
  13.7 12.5 %collective-permute-start.1 = (bf16[384,3,128]{0,1,2:T(4,128)(2,1)S(1)}, bf16[384,3,128]{0,1,2:T(4,128)(2,1)S(1)}, u32[]{:S(2)}, u32[]{:S(2)}) collective-permute-start(bf16[384,3,128]{0,1,2:T(4,128)(2,1)S(1)} %get-tuple-element.133), channel_id=1, source_target_pairs={{2,0},{3,1},{6,4},{7,5},{10,8},{11,9},{14,12},{15,13},{18,16},{19,... | collective-permute-start | bytes 884744 | tf_op jit(solution)/shard_map/ppermute | solution.py:20
  27.2 2.9 collective-permute-start.2
  28.5 3.1 collective-permute-start.3
  29.9 2.0 copy-start.7
  29.9 2.0 copy-start.9
  29.9 2.0 copy-start.11
  31.9 26.4 %copy-start.6 = (f32[384]{0:T(512)S(1)}, f32[384]{0:T(512)}, u32[]{:S(2)}) copy-start(f32[384]{0:T(512)} %param.10) | copy-start | bytes 4612
  37.7 57.6 %copy-start.15 = (f32[1536]{0:T(1024)S(1)}, f32[1536]{0:T(1024)}, u32[]{:S(2)}) copy-start(f32[1536]{0:T(1024)} %param.12) | copy-start | bytes 18436
  59.3 87.5 %reduce-scatter.7.cloned.1.call-start = ((), (), s32[]{:S(2)}) async-start(), calls=%async_computation.4 | async-start | bytes 1966080
  102.5 1.1 copy-start.16
  109.8 2.7 copy-start.3
  112.4 36.3 %copy-start.13 = (f32[384]{0:T(512)S(1)}, f32[384]{0:T(512)}, u32[]{:S(2)}) copy-start(f32[384]{0:T(512)} %param.14) | copy-start | bytes 4612
  112.4 74.8 %all-gather.5.cloned.1.call-start = ((), (), s32[]{:S(2)}) async-start(), calls=%async_computation.3 | async-start | bytes 1966080 | tf_op jit(solution)/shard_map/all_gather | solution.py:84
  114.9 79.4 %copy-start.1 = (bf16[384,4,128]{0,2,1:T(8,128)(2,1)}, bf16[384,4,128]{0,2,1:T(8,128)(2,1)S(1)}, u32[]{:S(2)}) copy-start(bf16[384,4,128]{0,2,1:T(8,128)(2,1)S(1)} %copy.41) | copy-start | bytes 1179652
  151.1 87.4 %reduce-scatter.9.cloned.1.call-start = ((), (), s32[]{:S(2)}) async-start(), calls=%async_computation.5 | async-start | bytes 1966080
  194.3 1.1 copy-start.17
  204.1 213.7 %all-reduce.4.cloned.1.call-start = ((), (), s32[]{:S(2)}) async-start(), calls=%async_computation.6 | async-start | bytes 18874368 | tf_op jit(solution)/shard_map/psum | solution.py:148
  204.1 6.9 %copy-start.14 = (bf16[1536,512]{0,1:T(8,128)(2,1)S(1)}, bf16[1536,512]{0,1:T(8,128)(2,1)}, u32[]{:S(2)}) copy-start(bf16[1536,512]{0,1:T(8,128)(2,1)} %all-gather.3.cloned.1.call-done) | copy-start | bytes 4718596
  204.1 6.9 %copy-start.18 = (bf16[1536,512]{0,1:T(8,128)(2,1)S(1)}, bf16[1536,512]{0,1:T(8,128)(2,1)}, u32[]{:S(2)}) copy-start(bf16[1536,512]{0,1:T(8,128)(2,1)} %copy-done.17) | copy-start | bytes 4718596
  215.3 1.0 copy-start.4
  265.1 16.5 %collective-permute-start.4 = (bf16[384,3,128]{0,2,1:T(8,128)(2,1)}, bf16[384,3,128]{0,2,1:T(8,128)(2,1)S(1)}, u32[]{:S(2)}, u32[]{:S(2)}) collective-permute-start(bf16[384,3,128]{0,2,1:T(8,128)(2,1)} %get-tuple-element.130), channel_id=1, source_target_pairs={{0,2},{1,3},{4,6},{5,7},{8,10},{9,11},{12,14},{13,15},{16,18},{17,... | collective-permute-start | bytes 884744 | tf_op jit(solution)/shard_map/ppermute | solution.py:17
  268.4 17.1 %collective-permute-start.5 = (bf16[384,3,128]{0,2,1:T(8,128)(2,1)S(1)}, bf16[384,3,128]{0,2,1:T(8,128)(2,1)S(1)}, u32[]{:S(2)}, u32[]{:S(2)}) collective-permute-start(bf16[384,3,128]{0,2,1:T(8,128)(2,1)S(1)} %get-tuple-element.131), channel_id=1, source_target_pairs={{2,0},{3,1},{6,4},{7,5},{10,8},{11,9},{14,12},{15,13},{18,16},{19,... | collective-permute-start | bytes 884744 | tf_op jit(solution)/shard_map/ppermute | solution.py:20
  274.4 28.7 %copy-start.2 = (bf16[384,4,128]{0,2,1:T(8,128)(2,1)S(1)}, bf16[384,4,128]{0,2,1:T(8,128)(2,1)}, u32[]{:S(2)}) copy-start(bf16[384,4,128]{0,2,1:T(8,128)(2,1)} %copy-done.1) | copy-start | bytes 1179652
  274.4 28.7 %copy-start.8 = (f32[384]{0:T(512)S(1)}, f32[384]{0:T(512)}, u32[]{:S(2)}) copy-start(f32[384]{0:T(512)} %copy-done.7) | copy-start | bytes 4612
  274.4 28.7 %copy-start.10 = (f32[384]{0:T(512)S(1)}, f32[384]{0:T(512)}, u32[]{:S(2)}) copy-start(f32[384]{0:T(512)} %copy-done.9) | copy-start | bytes 4612
  274.4 28.7 %copy-start.12 = (f32[384]{0:T(512)S(1)}, f32[384]{0:T(512)}, u32[]{:S(2)}) copy-start(f32[384]{0:T(512)} %copy-done.11) | copy-start | bytes 4612
  285.6 17.2 %collective-permute-start.7 = (bf16[384,10,3]{0,1,2:T(8,128)(2,1)S(1)}, bf16[384,10,3]{0,1,2:T(8,128)(2,1)S(1)}, u32[]{:S(2)}, u32[]{:S(2)}) collective-permute-start(bf16[384,10,3]{0,1,2:T(8,128)(2,1)S(1)} %copy.43), channel_id=1, source_target_pairs={{1,0},{3,2},{5,4},{7,6},{9,8},{11,10},{13,12},{15,14},{17,16},{19,... | collective-permute-start | bytes 69128 | tf_op jit(solution)/shard_map/ppermute | solution.py:20
  286.9 15.9 %collective-permute-start.6 = (bf16[384,10,3]{0,1,2:T(8,128)(2,1)S(1)}, bf16[384,10,3]{0,1,2:T(8,128)(2,1)S(1)}, u32[]{:S(2)}, u32[]{:S(2)}) collective-permute-start(bf16[384,10,3]{0,1,2:T(8,128)(2,1)S(1)} %copy.42), channel_id=1, source_target_pairs={{0,1},{2,3},{4,5},{6,7},{8,9},{10,11},{12,13},{14,15},{16,17},{18,... | collective-permute-start | bytes 69128 | tf_op jit(solution)/shard_map/ppermute | solution.py:17
  417.8 5.0 %copy-start = (bf16[1536,1536]{1,0:T(8,128)(2,1)S(1)}, bf16[1536,1536]{1,0:T(8,128)(2,1)}, u32[]{:S(2)}) copy-start(bf16[1536,1536]{1,0:T(8,128)(2,1)} %get-tuple-element.143) | copy-start | bytes 14155780
Sparse Core Ops, SparseCore 0:
  59.4 35.7 all-gather.2
  112.6 34.2 reduce-scatter.6
  151.2 36.0 all-gather.4
  204.2 34.2 reduce-scatter.8
  241.5 176.2 all-reduce.3
where the time goes:
time: 432 us; the launch traced here: 431 us
  waiting for transfers between devices  257 us (59%)
  blocking collectives  42.3 us (10%)
  local copies, waits for them, and re-layouts  39.6 us (9%)
  matrix products  37.5 us (9%)
  other arithmetic  22.8 us (5%)
  starting transfers between devices  18.3 us (4%)
  between operations  14.4 us (3%)
    psum x1, waiting for transfers between devices, on_device(): lax.psum(grad_expand.astype(jnp.bfloat16), ('rows', 'cols'))  108 us
    unnamed x7, waiting for transfers between devices  53.2 us
    all_gather x1, waiting for transfers between devices, on_device(): block_rows = lax.all_gather(scaled_cot, 'chan', axis=0, tiled=True)  36 us
    all_gather x1, waiting for transfers between devices, on_device(): normed_full = lax.all_gather(norm_output, 'chan', axis=0, tiled=True)  35.9 us
    unnamed x48, local copies, waits for them, and re-layouts  23.4 us
    ppermute x4, waiting for transfers between devices, extended(): lax.ppermute(lax.slice_in_dim(block, block.shape[dim] - width, None, axis...  13.9 us
    another operation x50, local copies, waits for them, and re-layouts, on_device(): kernel_local = jnp.stack(kernel_terms, axis=1)  13.5 us
    ppermute x4, starting transfers between devices, extended(): lax.ppermute(lax.slice_in_dim(block, block.shape[dim] - width, None, axis...  12.5 us
  transfers between devices with their start and end apart: 13, of which 10 were waited for; matrix products, arithmetic and copies ran while one was open for 10% of the time, Pallas kernels for 0%

commit v1 on v0

v1 whole, which is shorter than its diff:
```python
import functools

import jax
import jax.numpy as jnp
from jax import lax
from jax.experimental import pallas as pl
from jax.experimental.pallas import tpu as pltpu
from jax.sharding import PartitionSpec as P

KS = 7
HALF = KS // 2
PAD = 16
EPSILON = 1e-06
MIB = 1024 * 1024
F32 = jnp.float32
BF16 = jnp.bfloat16

whole = pl.BlockSpec(memory_space=pltpu.VMEM)


def params(mib):
    return pltpu.CompilerParams(vmem_limit_bytes=mib * MIB)


def shape(dims, dtype):
    return jax.ShapeDtypeStruct(dims, dtype)


def pieces(values):
    high = values.astype(BF16)
    rest = values - high.astype(F32)
    middle = rest.astype(BF16)
    low = (rest - middle.astype(F32)).astype(BF16)
    return high, middle, low


def stacked_rows(values):
    width = values.shape[1]
    row = lax.broadcasted_iota(jnp.int32, (PAD, width), 0)
    block = jnp.zeros((PAD, width), F32)
    for index, part in enumerate(pieces(values)):
        block = jnp.where(row == index, part.astype(F32), block)
    return block.astype(BF16)


def from_sides(low_source, high_source, axis):
    count = lax.axis_size(axis)
    if count == 2:
        index = lax.axis_index(axis)
        sent = jnp.where(index == 0, low_source, high_source)
        got = lax.ppermute(sent, axis, [(0, 1), (1, 0)])
        return got, got
    forward = [(i, i + 1) for i in range(count - 1)]
    backward = [(i + 1, i) for i in range(count - 1)]
    return lax.ppermute(low_source, axis, forward), lax.ppermute(high_source, axis, backward)


def edges(block, axis):
    count = lax.axis_size(axis)
    if count == 2:
        return lax.ppermute(block, axis, [(0, 1), (1, 0)])
    low, high = from_sides(block, block, axis)
    width = block.shape[-1]
    lane = lax.broadcasted_iota(jnp.int32, block.shape, block.ndim - 1)
    return jnp.where(lane < width // 2, high, low)


def surroundings(block):
    rows = block.shape[0]
    above, below = from_sides(block[rows - HALF :], block[:HALF], "rows")
    side = edges(block, "cols")
    if lax.axis_size("rows") == 2:
        corner = edges(above, "cols")
        return block, above, below, side, corner, corner
    return block, above, below, side, edges(above, "cols"), edges(below, "cols")


def border_flags(width):
    row, col = lax.axis_index("rows"), lax.axis_index("cols")
    one = lambda test: jnp.where(test, 1.0, 0.0).astype(F32)
    has_above = one(row > 0)
    has_below = one(row < lax.axis_size("rows") - 1)
    lane = lax.broadcasted_iota(jnp.int32, (1, width), 1)
    seam = jnp.where(lane < width // 2, one(col < lax.axis_size("cols") - 1), one(col > 0))
    return has_above, has_below, seam


def window_rows(refs, flags, at, count):
    block, above, below, side, above_side, below_side = refs
    has_above, has_below, seam = flags
    rows = block.shape[0]
    cut = pl.ds(at, count)
    found = []
    for k in range(HALF):
        found.append((above[k, cut].astype(F32) * has_above, above_side[k, cut].astype(F32) * (has_above * seam)))
    for k in range(rows):
        found.append((block[k, cut].astype(F32), side[k, cut].astype(F32) * seam))
    for k in range(HALF):
        found.append((below[k, cut].astype(F32) * has_below, below_side[k, cut].astype(F32) * (has_below * seam)))
    return found


def moved(pair, offset, lane):
    own, edge = pair
    width = own.shape[1]
    if offset == 0:
        return own
    if offset > 0:
        return pltpu.roll(jnp.where(lane < offset, edge, own), width - offset, 1)
    return pltpu.roll(jnp.where(lane >= width + offset, edge, own), -offset, 1)


def convolve(refs, flags, taps, at, count, flipped):
    rows = refs[0].shape[0]
    width = refs[0].shape[2]
    found = window_rows(refs, flags, at, count)
    lane = lax.broadcasted_iota(jnp.int32, (count, width), 1)
    sums = [None] * rows
    for tap_col in range(KS):
        shifted = [moved(pair, tap_col - HALF, lane) for pair in found]
        for tap_row in range(KS):
            tap = tap_row * KS + tap_col
            tap = KS * KS - 1 - tap if flipped else tap
            weight = jnp.broadcast_to(taps[:, tap : tap + 1], (count, width))
            for k in range(rows):
                term = weight * shifted[k + tap_row]
                sums[k] = term if sums[k] is None else sums[k] + term
    return sums


def forward_conv_kernel(block, above, below, side, above_side, below_side, kernel, packed, centered, local):
    refs = (block, above, below, side, above_side, below_side)
    rows, channels, width = block.shape
    flags = border_flags(width)

    def step(index, totals):
        at = pl.multiple_of(index * PAD, PAD)
        sums = convolve(refs, flags, kernel[pl.ds(at, PAD), :], at, PAD, False)
        for k in range(rows):
            centered[pl.ds(at, PAD), k * width : (k + 1) * width] = sums[k]
        return tuple(total + value[:8] + value[8:] for total, value in zip(totals, sums))

    totals = lax.fori_loop(
        0, channels // PAD, step, tuple(jnp.zeros((8, width), F32) for _ in range(rows))
    )
    mean = jnp.concatenate([jnp.sum(total, axis=0, keepdims=True) for total in totals], axis=1) / channels
    local[...] = jnp.broadcast_to(mean, local.shape)

    def finish(index, carry):
        at = pl.multiple_of(index * PAD, PAD)
        value = centered[pl.ds(at, PAD), :] - mean
        centered[pl.ds(at, PAD), :] = value
        packed[pl.ds(at, PAD), :] = value.astype(BF16)
        return carry

    lax.fori_loop(0, channels // PAD, finish, 0)
    packed[channels:, :] = stacked_rows(mean)


def forward_conv(around, kernel):
    rows, channels, width = around[0].shape
    pixels = rows * width
    return pl.pallas_call(
        forward_conv_kernel,
        out_shape=(
            shape((channels + PAD, pixels), BF16),
            shape((channels, pixels), F32),
            shape((8, pixels), F32),
        ),
        in_specs=[whole] * 7,
        out_specs=(whole,) * 3,
        compiler_params=params(32),
        cost_estimate=pl.CostEstimate(flops=20_000_000, bytes_accessed=4_000_000, transcendentals=0),
        name="conv_forward",
    )(*around, kernel)


def backward_conv_kernel(block, above, below, side, above_side, below_side, kernel, cotangent, result):
    refs = (block, above, below, side, above_side, below_side)
    rows, channels, width = block.shape
    flags = border_flags(width)

    def step(index, carry):
        at = pl.multiple_of(index * PAD, PAD)
        sums = convolve(refs, flags, kernel[pl.ds(at, PAD), :], at, PAD, True)
        for k in range(rows):
            result[k, pl.ds(at, PAD)] = (sums[k] + cotangent[k, pl.ds(at, PAD)].astype(F32)).astype(BF16)
        return carry

    lax.fori_loop(0, channels // PAD, step, 0)


def backward_conv(around, kernel, cotangent):
    return pl.pallas_call(
        backward_conv_kernel,
        out_shape=shape(cotangent.shape, BF16),
        in_specs=[whole] * 8,
        out_specs=whole,
        compiler_params=params(32),
        cost_estimate=pl.CostEstimate(flops=20_000_000, bytes_accessed=4_000_000, transcendentals=0),
        name="conv_backward",
    )(*around, kernel, cotangent)


def kernel_gradient_kernel(block, above, below, side, above_side, below_side, gradient, result):
    refs = (block, above, below, side, above_side, below_side)
    rows, channels, width = block.shape
    flags = border_flags(width)

    def step(index, carry):
        at = pl.multiple_of(index * PAD, PAD)
        found = window_rows(refs, flags, at, PAD)
        lane = lax.broadcasted_iota(jnp.int32, (PAD, width), 1)
        grads = [gradient[k, pl.ds(at, PAD)].astype(F32) for k in range(rows)]
        sums = jnp.zeros((PAD, width), F32)
        for tap_col in range(KS):
            shifted = [moved(pair, tap_col - HALF, lane) for pair in found]
            for tap_row in range(KS):
                total = grads[0] * shifted[tap_row]
                for k in range(1, rows):
                    total = total + grads[k] * shifted[k + tap_row]
                tap = tap_row * KS + tap_col
                sums = jnp.where(lane == tap, jnp.sum(total, axis=1, keepdims=True), sums)
        result[pl.ds(at, PAD), :] = sums
        return carry

    lax.fori_loop(0, channels // PAD, step, 0)


def kernel_gradient(around, gradient):
    rows, channels, width = gradient.shape
    return pl.pallas_call(
        kernel_gradient_kernel,
        out_shape=shape((channels, width), F32),
        in_specs=[whole] * 7,
        out_specs=whole,
        compiler_params=params(32),
        cost_estimate=pl.CostEstimate(flops=20_000_000, bytes_accessed=4_000_000, transcendentals=0),
        name="kernel_gradient",
    )(*around, gradient)


def pack_kernel(cotangent, scale, gain, packed):
    rows, channels, width = cotangent.shape
    for k in range(rows):
        packed[:channels, k * width : (k + 1) * width] = (
            cotangent[k].astype(F32) * scale[...]
        ).astype(BF16)
    packed[channels:, :] = jnp.zeros((PAD, rows * width), BF16)
    packed[channels:, :channels] = stacked_rows(gain[...])


def pack_cotangent(cotangent, scale, gain):
    rows, channels, width = cotangent.shape
    return pl.pallas_call(
        pack_kernel,
        out_shape=shape((channels + PAD, rows * width), BF16),
        in_specs=[whole] * 3,
        out_specs=whole,
        compiler_params=params(32),
        name="pack_cotangent",
    )(cotangent, scale, gain)


def gelu_parts(values):
    cdf = 0.5 * (1.0 + lax.erf(values * 0.7071067811865476))
    slope = cdf + values * jnp.exp(-0.5 * values * values) * 0.3989422804014327
    return values * cdf, slope


ROWS_BY_COLS = (((1,), (0,)), ((), ()))
COLS_BY_COLS = (((0,), (0,)), ((), ()))
ROWS_BY_ROWS = (((1,), (1,)), ((), ()))


def dot(left, right, dims):
    return lax.dot_general(left, right, dims, preferred_element_type=F32)


def unpack_matrix(gathered, target, channels):
    for k in range(gathered.shape[0]):
        target[k * channels : (k + 1) * channels, :] = gathered[k, :channels, :]


def block_kernel(
    steps, conv_all, cot_all, gain, w_expand, bias, w_reduce,
    normed, hidden, grad_pre, reduced, grad_normed, stats, moments,
    cot, reduce_sum, normed_sum,
):
    count = conv_all.shape[0]
    channels = conv_all.shape[1] - PAD
    every = count * channels
    at = pl.program_id(0)

    @pl.when(at == 0)
    def _():
        means = [
            jnp.sum(conv_all[k, channels:, :].astype(F32), axis=0, keepdims=True) for k in range(count)
        ]
        mean = means[0]
        for k in range(1, count):
            mean = mean + means[k]
        mean = mean / count
        squares = jnp.zeros_like(mean)
        for k in range(count):
            value = conv_all[k, :channels, :].astype(F32) + (means[k] - mean)
            squares = squares + jnp.sum(value * value, axis=0, keepdims=True)
        deviation = lax.rsqrt(squares / every + EPSILON)
        for k in range(count):
            value = conv_all[k, :channels, :].astype(F32) + (means[k] - mean)
            cut = slice(k * channels, (k + 1) * channels)
            normed[cut, :] = (value * deviation * gain[cut, :]).astype(BF16)
        row = lax.broadcasted_iota(jnp.int32, stats.shape, 0)
        stats[...] = jnp.where(row == 0, mean, jnp.where(row == 1, deviation, 0.0))
        unpack_matrix(cot_all, cot, channels)
        reduce_sum[...] = jnp.zeros_like(reduce_sum)
        normed_sum[...] = jnp.zeros_like(normed_sum)

    pre = dot(w_expand[...], normed[...], ROWS_BY_COLS) + bias[...]
    active, slope = gelu_parts(pre)
    active = active.astype(BF16)
    hidden[...] = active
    back = dot(w_reduce[...], cot[...], COLS_BY_COLS)
    back = (back * slope).astype(BF16)
    grad_pre[...] = back
    normed_sum[...] += dot(w_expand[...], back, COLS_BY_COLS)
    reduce_sum[...] += dot(w_reduce[...], active, ROWS_BY_COLS)

    @pl.when(at == steps - 1)
    def _():
        reduced[...] = reduce_sum[...].astype(BF16)
        total = normed_sum[...]
        grad_normed[...] = total.astype(BF16)
        first = jnp.sum(total * gain[...], axis=0, keepdims=True)
        cross = jnp.sum(total * normed[...].astype(F32), axis=0, keepdims=True)
        row = lax.broadcasted_iota(jnp.int32, moments.shape, 0)
        moments[...] = jnp.where(row == 0, first, jnp.where(row == 1, cross, 0.0))


def tile_of(hidden_units):
    for size in (256, 128):
        if hidden_units % size == 0:
            return size
    return hidden_units


def fixed(dims):
    return pl.BlockSpec(dims, lambda t: (0,) * len(dims))


def block_forward(conv_all, cot_all, gain, w_expand, bias, w_reduce):
    count, padded, pixels = conv_all.shape
    every = gain.shape[0]
    units = w_expand.shape[0]
    tile = tile_of(units)
    steps = units // tile
    return pl.pallas_call(
        functools.partial(block_kernel, steps),
        grid=(steps,),
        out_shape=(
            shape((every, pixels), BF16),
            shape((units, pixels), BF16),
            shape((units, pixels), BF16),
            shape((every, pixels), BF16),
            shape((every, pixels), BF16),
            shape((8, pixels), F32),
            shape((8, pixels), F32),
        ),
        in_specs=[
            fixed(conv_all.shape),
            fixed(cot_all.shape),
            fixed(gain.shape),
            pl.BlockSpec((tile, every), lambda t: (t, 0)),
            pl.BlockSpec((tile, 1), lambda t: (t, 0)),
            pl.BlockSpec((every, tile), lambda t: (0, t)),
        ],
        out_specs=(
            fixed((every, pixels)),
            pl.BlockSpec((tile, pixels), lambda t: (t, 0)),
            pl.BlockSpec((tile, pixels), lambda t: (t, 0)),
            fixed((every, pixels)),
            fixed((every, pixels)),
            fixed((8, pixels)),
            fixed((8, pixels)),
        ),
        scratch_shapes=[
            pltpu.VMEM((every, pixels), BF16),
            pltpu.VMEM((every, pixels), F32),
            pltpu.VMEM((every, pixels), F32),
        ],
        compiler_params=params(48),
        cost_estimate=pl.CostEstimate(
            flops=8 * units * every * pixels, bytes_accessed=18_000_000, transcendentals=0
        ),
        name="pointwise_block",
    )(conv_all, cot_all, gain, w_expand, bias, w_reduce)


def weight_kernel(
    channels, normed_own, normed_other, cot_own, cot_other, hidden_own, pre_own,
    w_expand, bias, w_reduce, grad_reduce, grad_expand, normed, cot, hidden, grad_pre,
):
    pixels = normed_own.shape[1]
    index = lax.axis_index("rows")
    own = pl.ds(pl.multiple_of(index * pixels, pixels), pixels)
    other = pl.ds(pl.multiple_of((1 - index) * pixels, pixels), pixels)

    @pl.when(pl.program_id(0) == 0)
    def _():
        normed[:, own] = normed_own[...]
        normed[:, other] = normed_other[...]
        for k in range(cot_own.shape[0]):
            cut = slice(k * channels, (k + 1) * channels)
            cot[cut, own] = cot_own[k, :channels, :]
            cot[cut, other] = cot_other[k, :channels, :]

    pre = dot(w_expand[...], normed_other[...], ROWS_BY_COLS) + bias[...]
    active, slope = gelu_parts(pre)
    hidden[:, own] = hidden_own[...]
    hidden[:, other] = active.astype(BF16)
    back = dot(w_reduce[...], cot[:, other], COLS_BY_COLS)
    grad_pre[:, own] = pre_own[...]
    grad_pre[:, other] = (back * slope).astype(BF16)
    grad_reduce[...] = dot(cot[...], hidden[...], ROWS_BY_ROWS).astype(BF16)
    grad_expand[...] = dot(grad_pre[...], normed[...], ROWS_BY_ROWS).astype(BF16)


def weight_gradients(part, parts, normed_own, normed_other, cot_own, cot_other, hidden, grad_pre, w_expand, bias, w_reduce):
    every, pixels = normed_own.shape
    units = w_expand.shape[0]
    tile = tile_of(units)
    steps = units // tile // parts
    first = part * steps
    return pl.pallas_call(
        functools.partial(weight_kernel, cot_own.shape[1] - PAD),
        grid=(steps,),
        out_shape=(shape((every, steps * tile), BF16), shape((steps * tile, every), BF16)),
        in_specs=[
            fixed(normed_own.shape),
            fixed(normed_other.shape),
            fixed(cot_own.shape),
            fixed(cot_other.shape),
            pl.BlockSpec((tile, pixels), lambda t: (t + first, 0)),
            pl.BlockSpec((tile, pixels), lambda t: (t + first, 0)),
            pl.BlockSpec((tile, every), lambda t: (t + first, 0)),
            pl.BlockSpec((tile, 1), lambda t: (t + first, 0)),
            pl.BlockSpec((every, tile), lambda t: (0, t + first)),
        ],
        out_specs=(
            pl.BlockSpec((every, tile), lambda t: (0, t)),
            pl.BlockSpec((tile, every), lambda t: (t, 0)),
        ),
        scratch_shapes=[
            pltpu.VMEM((every, 2 * pixels), BF16),
            pltpu.VMEM((every, 2 * pixels), BF16),
            pltpu.VMEM((tile, 2 * pixels), BF16),
            pltpu.VMEM((tile, 2 * pixels), BF16),
        ],
        compiler_params=params(48),
        cost_estimate=pl.CostEstimate(
            flops=12 * steps * tile * every * pixels, bytes_accessed=18_000_000, transcendentals=0
        ),
        name="weight_gradients",
    )(normed_own, normed_other, cot_own, cot_other, hidden, grad_pre, w_expand, bias, w_reduce)


def norm_gradient_kernel(every, grad_normed, centered, local, stats, moments, gain, result):
    rows, channels, width = result.shape
    mean, deviation = stats[0:1, :], stats[1:2, :]
    first, cross = moments[0:1, :] / every, moments[1:2, :] / every
    shift = local[0:1, :] - mean

    def step(index, carry):
        at = pl.multiple_of(index * PAD, PAD)
        cut = pl.ds(at, PAD)
        hat = (centered[cut, :] + shift) * deviation
        value = grad_normed[cut, :].astype(F32) * gain[cut, :]
        value = ((value - first - hat * cross) * deviation).astype(BF16)
        for k in range(rows):
            result[k, cut] = value[:, k * width : (k + 1) * width]
        return carry

    lax.fori_loop(0, channels // PAD, step, 0)


def norm_gradient(every, dims, grad_normed, centered, local, stats, moments, gain):
    return pl.pallas_call(
        functools.partial(norm_gradient_kernel, every),
        out_shape=shape(dims, BF16),
        in_specs=[whole] * 6,
        out_specs=whole,
        compiler_params=params(32),
        name="norm_gradient",
    )(grad_normed, centered, local, stats, moments, gain)


def swap(values, axis):
    return lax.ppermute(values, axis, [(0, 1), (1, 0)])


def on_device(
    image, kernel, layer_norm_weight, w_expand, bias_expand, w_reduce, layer_scale, cotangent
):
    channels, tile_rows, tile_cols = image.shape
    pixels = tile_rows * tile_cols
    every = w_reduce.shape[0]
    two_tiles = lax.axis_size("rows") == 2 and lax.axis_size("cols") == 2

    cot_rows = jnp.transpose(cotangent, (1, 0, 2))
    packed_cot = pack_cotangent(cot_rows, layer_scale[:, None], layer_norm_weight[None, :])
    cot_all = lax.all_gather(packed_cot, "chan")
    gain_rows = cot_all[:, channels : channels + 3, :channels].astype(F32)
    gain_all = jnp.sum(gain_rows, axis=1).reshape(every, 1)

    image_rows = jnp.transpose(image, (1, 0, 2))
    around = surroundings(image_rows)
    packed_conv, centered, local = forward_conv(around, kernel)
    conv_all = lax.all_gather(packed_conv, "chan")

    bias = bias_expand[:, None]
    normed, hidden, grad_pre, reduced, grad_normed, stats, moments = block_forward(
        conv_all, cot_all, gain_all, w_expand, bias, w_reduce
    )
    grad_normed = lax.psum_scatter(grad_normed, "chan", scatter_dimension=0, tiled=True)
    moments = lax.psum(moments, "chan")
    reduced = lax.psum_scatter(reduced, "chan", scatter_dimension=0, tiled=True)

    if two_tiles:
        cot_other = swap(cot_all, "rows")
        normed_other = swap(normed, "rows")
        parts = 2
        reduce_parts, expand_parts = [], []
        for part in range(parts):
            of_reduce, of_expand = weight_gradients(
                part, parts, normed, normed_other, cot_all, cot_other, hidden, grad_pre,
                w_expand, bias, w_reduce,
            )
            reduce_parts.append(of_reduce.astype(F32) + swap(of_reduce, "cols").astype(F32))
            expand_parts.append(of_expand.astype(F32) + swap(of_expand, "cols").astype(F32))
        grad_reduce = jnp.concatenate(reduce_parts, axis=1).astype(BF16)
        grad_expand = jnp.concatenate(expand_parts, axis=0).astype(BF16)
    else:
        cot_full = cot_all[:, :channels, :].reshape(every, pixels)
        grad_reduce = dot(cot_full, hidden, ROWS_BY_ROWS).astype(BF16)
        grad_expand = dot(grad_pre, normed, ROWS_BY_ROWS).astype(BF16)
        grad_reduce, grad_expand = lax.psum((grad_reduce, grad_expand), ("rows", "cols"))

    gradient = norm_gradient(
        every, image_rows.shape, grad_normed, centered, local, stats, moments,
        layer_norm_weight[:, None],
    )
    grad_around = surroundings(gradient)
    taps = kernel_gradient(around, gradient)[:, : KS * KS]
    if two_tiles:
        taps = taps + swap(taps, "cols")
        taps = taps + swap(taps, "rows")
    else:
        taps = lax.psum(taps, ("rows", "cols"))
    grad_input = jnp.transpose(backward_conv(grad_around, kernel, cot_rows), (1, 0, 2))

    output = (
        image.reshape(channels, pixels).astype(F32)
        + layer_scale[:, None] * reduced.astype(F32)
    ).astype(BF16).reshape(image.shape)
    return output, grad_input, grad_expand, grad_reduce, taps


def solution(mesh):
    placed = (
        P("chan", ("groups", "rows"), "cols"),
        P("chan", None),
        P("chan"),
        P("chan", None),
        P("chan"),
        P(None, "chan"),
        P("chan"),
        P("chan", ("groups", "rows"), "cols"),
    )
    return jax.shard_map(
        on_device,
        mesh=mesh,
        in_specs=placed,
        out_specs=(
            P("chan", ("groups", "rows"), "cols"),
            P("chan", ("groups", "rows"), "cols"),
            P(("groups", "chan"), None),
            P("groups", "chan"),
            P(("groups", "chan"), None),
        ),
        check_vma=False,
    )
```

time: 432 us -> 301 us (0.70)
  waiting for transfers between devices: 257 us -> 144 us
  Pallas kernels: 0 us -> 81.7 us
  matrix products: 37.5 us -> 0 us
  blocking collectives: 42.3 us -> 17 us
  local copies, waits for them, and re-layouts: 39.6 us -> 18.4 us
  starting transfers between devices: 18.3 us -> 9.37 us
  other arithmetic: 22.8 us -> 16.4 us
    psum x1 -> x0, waiting for transfers between devices: 108 us -> none  [on_device(): lax.psum(grad_expand.astype(jnp.bfloat16), ('rows', 'cols'))]
    pallas_call x0 -> x8, Pallas kernels: none -> 81.7 us  [the longest x2 26.7 us: weight_gradients(): pl.pallas_call(functools.partial(weight_kernel, cot_own.shape[1] - PAD),...]
    ppermute x8 -> x14, waiting for transfers between devices: 23.5 us -> 88.7 us  [the longest x8 80.2 us: swap(): return lax.ppermute(values, axis, [(0, 1), (1, 0)])]
    unnamed x7 -> x4, waiting for transfers between devices: 53.2 us -> 0.07 us
    dot_general x6 -> x0, matrix products: 37.5 us -> none  [the longest x1 7.28 us: on_device(): pre_act = jnp.dot(w_expand, normed_full, preferred_element_type=jnp.float32)]
    psum x4 -> x1, blocking collectives: 42.3 us -> 17 us  [on_device(): moments = lax.psum(moments, 'chan')]
    all_gather x2, waiting for transfers between devices: 71.9 us -> 55.2 us  [the longest x1 37.2 us: on_device(): conv_all = lax.all_gather(packed_conv, 'chan')]
    another operation x50 -> x0, local copies, waits for them, and re-layouts: 13.5 us -> none  [on_device(): kernel_local = jnp.stack(kernel_terms, axis=1)]
  transfers between devices with their start and end apart: 13 -> 18, of which waited for: 10 -> 7; matrix products, arithmetic and copies ran while one was open for 10% -> 6% of each run, Pallas kernels for 0% -> 21%
where the time goes in v1:
time: 301 us
  waiting for transfers between devices  144 us (48%)
  Pallas kernels  81.7 us (27%)
  local copies, waits for them, and re-layouts  18.4 us (6%)
  blocking collectives  17 us (6%)
  other arithmetic  16.4 us (5%)
  between operations  14 us (5%)
  starting transfers between devices  9.37 us (3%)
    ppermute x8, waiting for transfers between devices, swap(): return lax.ppermute(values, axis, [(0, 1), (1, 0)])  80.2 us
    all_gather x1, waiting for transfers between devices, on_device(): conv_all = lax.all_gather(packed_conv, 'chan')  37.2 us
    pallas_call x2, Pallas kernels, weight_gradients(): pl.pallas_call(functools.partial(weight_kernel, cot_own.shape[1] - PAD),...  26.7 us
    pallas_call x1, Pallas kernels, block_forward(): pl.pallas_call(functools.partial(block_kernel, steps), grid=(steps,), out...  18.6 us
    all_gather x1, waiting for transfers between devices, on_device(): cot_all = lax.all_gather(packed_cot, 'chan')  18 us
    psum x1, blocking collectives, on_device(): moments = lax.psum(moments, 'chan')  17 us
    pallas_call x1, Pallas kernels, kernel_gradient(): pl.pallas_call(kernel_gradient_kernel, out_shape=shape((channels, width),...  14.2 us
    unnamed x41, local copies, waits for them, and re-layouts  13.8 us
  transfers between devices with their start and end apart: 18, of which 7 were waited for; matrix products, arithmetic and copies ran while one was open for 6% of the time, Pallas kernels for 21%

profile of v1, /device:TPU:0, one launch (start us, length us, event | category | flops | bytes accessed | tf_op | source)
XLA Modules:
  0.0 300.8 jit_solution(8900042771354892729)
XLA Ops:
  7.2 0.0 copy-start.11
  7.2 0.0 all-gather.7.cloned.1.call-start
  7.2 0.7 broadcast_in_dim.14.gain
  8.0 0.8 broadcast_in_dim.17.scale
  8.8 1.1 copy.37
  9.8 1.0 pack_cotangent.1
  10.8 0.0 all-gather.7.cloned.1.call-update
  10.9 0.0 copy-start.14
  10.9 0.0 all-gather.5.cloned.1.call-start
  10.9 0.1 copy.38
  11.0 3.0 collective-permute-start
  14.0 7.0 %collective-permute-done.above.below = bf16[3,384,128]{2,1,0:T(8,128)(2,1)S(1)} collective-permute-done((bf16[3,384,128]{2,1,0:T(8,128)(2,1)S(1)}, bf16[3,384,128]{2,1,0:T(8,128)(2,1)S(1)}, u32[]{:S(2)}, u32[]{:S(2)}) %collective-permute-start) | collective-permute-done | bytes 294944 | tf_op jit(solution)/shard_map/ppermute | solution.py:51
  21.1 0.1 copy.20.kernel
  21.2 1.4 collective-permute-done.2.above_side.below_side
  22.6 10.1 %conv_forward.1 = (bf16[400,512]{1,0:T(8,128)(2,1)}, f32[384,512]{1,0:T(8,128)S(1)}, f32[8,512]{1,0:T(8,128)S(1)}) custom-call(bf16[4,384,128]{2,1,0:T(8,128)(2,1)S(1)} %bitcast.22, bf16[3,384,128]{2,1,0:T(8,128)(2,1)S(1)} %collective-permute-done.above.below, bf16[3,384,128]{2,1,0:T(8,128)(2,1)S(1)} %collective-permute-done.above.below, ...), custom_call_target="tpu_custom_call" | custom-call | flops 20000000 | bytes 4000000 | tf_op jit(solution)/shard_map/conv_forward/pallas_call | solution.py:163
  32.7 0.0 all-gather.5.cloned.1.call-update
  32.7 0.0 reduce-scatter.5.cloned.1.call-start
  32.8 1.1 broadcast_in_dim.18.bias
  33.9 18.0 %all-gather.7.cloned.1.call-done = bf16[1600,512]{1,0:T(8,128)(2,1)} async-done(((bf16[400,512]{1,0:T(8,128)(2,1)}), bf16[1600,512]{1,0:T(8,128)(2,1)}) %all-gather.7.cloned.1.call-update) | async-done | bytes 1638416 | tf_op jit(solution)/shard_map/all_gather | solution.py:511
  51.9 0.8 convert_reduce_fusion
  52.7 1.2 copy.33
  53.9 37.2 %all-gather.5.cloned.1.call-done = bf16[1600,512]{1,0:T(8,128)(2,1)} async-done(((bf16[400,512]{1,0:T(8,128)(2,1)}), bf16[1600,512]{1,0:T(8,128)(2,1)}) %all-gather.5.cloned.1.call-update) | async-done | bytes 1638416 | tf_op jit(solution)/shard_map/all_gather | solution.py:518
  91.1 1.1 copy-done
  92.2 1.1 copy-done.2
  93.3 18.6 %pointwise_block.1 = (bf16[1536,512]{1,0:T(8,128)(2,1)S(1)}, bf16[1536,512]{1,0:T(8,128)(2,1)S(1)}, bf16[1536,512]{1,0:T(8,128)(2,1)}, bf16[1536,512]{1,0:T(8,12...) custom-call(bf16[4,400,512]{2,1,0:T(8,128)(2,1)} %bitcast.37, ...), custom_call_target="tpu_custom_call" | custom-call | flops 9663676416 | bytes 18000000 | tf_op jit(solution)/shard_map/pointwise_block/pallas_call | solution.py:357
  112.0 1.1 copy-done.4
  113.1 1.1 copy-done.6
  114.3 0.0 reduce-scatter.5.cloned.1.call-update
  114.3 0.2 reduce-scatter.3.cloned.1.call-start
  114.5 1.5 collective-permute-start.7
  116.0 0.6 collective-permute-start.6
  116.6 0.0 reduce-scatter.3.cloned.1.call-update
  116.6 37.0 %collective-permute-done.7.cot_other = bf16[4,400,512]{2,1,0:T(8,128)(2,1)} collective-permute-done((bf16[4,400,512]{2,1,0:T(8,128)(2,1)}, bf16[4,400,512]{2,1,0:T(8,128)(2,1)}, u32[]{:S(2)}, u32[]{:S(2)}) %collective-permute-start.7) | collective-permute-done | bytes 1638432 | tf_op jit(solution)/shard_map/ppermute | solution.py:498
  153.6 32.5 %collective-permute-done.6.normed_other = bf16[1536,512]{1,0:T(8,128)(2,1)} collective-permute-done((bf16[1536,512]{1,0:T(8,128)(2,1)}, bf16[1536,512]{1,0:T(8,128)(2,1)}, u32[]{:S(2)}, u32[]{:S(2)}) %collective-permute-start.6) | collective-permute-done | bytes 1572896 | tf_op jit(solution)/shard_map/ppermute | solution.py:498
  186.1 1.1 copy-done.1
  187.2 1.4 copy-done.5
  188.6 1.4 copy-done.7
  190.0 13.3 %weight_gradients.3 = (bf16[1536,768]{1,0:T(8,128)(2,1)}, bf16[768,1536]{1,0:T(8,128)(2,1)}) custom-call(bf16[1536,512]{1,0:T(8,128)(2,1)S(1)} %copy-done.5, bf16[1536,512]{1,0:T(8,128)(2,1)} %collective-permute-done.6.normed_other, bf16[4,400,512]{2,1,0:T(8,128)(2,1)} %bitcast.35, bf16[4,400,512]{2,1,0:T(8,128)(2,1)} %collective-permute-done.7.cot_other, ...), custom_call_target="tpu_custom_call" | custom-call | flops 7247757312 | bytes 18000000 | tf_op jit(solution)/shard_map/weight_gradients/pallas_call | solution.py:434
  203.3 13.4 %weight_gradients.2 = (bf16[1536,768]{1,0:T(8,128)(2,1)}, bf16[768,1536]{1,0:T(8,128)(2,1)}) custom-call(bf16[1536,512]{1,0:T(8,128)(2,1)S(1)} %copy-done.5, bf16[1536,512]{1,0:T(8,128)(2,1)} %collective-permute-done.6.normed_other, bf16[4,400,512]{2,1,0:T(8,128)(2,1)} %bitcast.36, bf16[4,400,512]{2,1,0:T(8,128)(2,1)} %collective-permute-done.7.cot_other, ...), custom_call_target="tpu_custom_call" | custom-call | flops 7247757312 | bytes 18000000 | tf_op jit(solution)/shard_map/weight_gradients/pallas_call | solution.py:434
  216.7 0.5 collective-permute-start.8
  217.2 0.1 broadcast_in_dim.19.gain
  217.3 17.0 %psum.7.moments = f32[8,512]{1,0:T(8,128)S(1)} all-reduce(f32[8,512]{1,0:T(8,128)S(1)} %get-tuple-element.25), channel_id=1, replica_groups=mesh['groups'=2,'chan'=4,'rows'=2,'cols'=2] {'chan'}, use_global_device_ids=true, to_apply=%region_3.4 | all-reduce | flops 4096 | bytes 32768 | tf_op jit(solution)/shard_map/psum | solution.py:525
  234.3 1.0 copy-done.3
  235.3 1.9 norm_gradient.1.block.gradient
  237.1 14.2 %kernel_gradient.1 = f32[384,128]{1,0:T(8,128)S(1)} custom-call(bf16[4,384,128]{2,1,0:T(8,128)(2,1)S(1)} %bitcast.23, bf16[3,384,128]{2,1,0:T(8,128)(2,1)S(1)} %collective-permute-done.above.below, bf16[3,384,128]{2,1,0:T(8,128)(2,1)S(1)} %collective-permute-done.above.below, bf16[4,384,128]{2,1,0:T(8,128)(2,1)S(1)} %collective-permute-done.1.side, ...), custom_call_target="tpu_custom_call" | custom-call | flops 20000000 | bytes 4000000 | tf_op jit(solution)/shard_map/kernel_gradient/pallas_call | solution.py:232
  251.3 0.1 collective-permute-start.12
  251.4 1.5 collective-permute-start.3
  252.9 1.4 collective-permute-start.13
  254.3 10.8 %collective-permute-done.13 = f32[384,49]{1,0:T(8,128)S(1)} collective-permute-done((f32[384,49]{1,0:T(8,128)S(1)}, f32[384,49]{1,0:T(8,128)S(1)}, u32[]{:S(2)}, u32[]{:S(2)}) %collective-permute-start.13) | collective-permute-done | bytes 75296 | tf_op jit(solution)/shard_map/ppermute | solution.py:498
  265.1 0.5 collective-permute-start.5
  265.6 0.1 convert.21
  265.7 0.0 reduce-scatter.3.cloned.1.call-done
  265.8 1.9 fusion
  267.7 1.8 reshape.21
  269.5 0.8 copy.30
  270.3 0.0 collective-permute-start.10
  270.3 9.3 %conv_backward.1 = bf16[4,384,128]{2,1,0:T(8,128)(2,1)S(1)} custom-call(bf16[4,384,128]{2,1,0:T(8,128)(2,1)S(1)} %norm_gradient.1.block.gradient, bf16[3,384,128]{2,1,0:T(8,128)(2,1)S(1)} %collective-permute-done.3.above.below, bf16[3,384,128]{2,1,0:T(8,128)(2,1)S(1)} %collective-permute-done.3.above.below, ...), custom_call_target="tpu_custom_call" | custom-call | flops 20000000 | bytes 4000000 | tf_op jit(solution)/shard_map/conv_backward/pallas_call | solution.py:194
  279.6 1.1 copy.29
  280.7 2.4 add_convert_fusion.2
  283.1 2.3 add_convert_fusion.3
  285.4 2.5 pad_maximum_fusion
  287.9 3.1 %add_convert_fusion = bf16[1536,768]{1,0:T(8,128)(2,1)S(1)} fusion(bf16[1536,768]{1,0:T(8,128)(2,1)} %collective-permute-done.11, bf16[1536,768]{1,0:T(8,128)(2,1)} %get-tuple-element.32), kind=kLoop, calls=%fused_computation.2 | loop fusion | flops 4718592 | bytes 7077888 | tf_op jit(solution)/shard_map/convert.2
  291.0 0.7 add_convert_fusion.1
  291.7 2.6 pad_maximum_fusion.1
  (44 shorter events, 0.2 us)
Async XLA Ops:
  7.2 3.8 %copy-start.11 = (bf16[384,4,128]{2,1,0:T(4,128)(2,1)S(1)}, bf16[384,4,128]{2,1,0:T(4,128)(2,1)}, u32[]{:S(2)}) copy-start(bf16[384,4,128]{2,1,0:T(4,128)(2,1)} %param.8) | copy-start | bytes 1179652
  7.2 13.9 %copy-start.13 = (f32[384,49]{0,1:T(8,128)S(1)}, f32[384,49]{0,1:T(8,128)}, u32[]{:S(2)}) copy-start(f32[384,49]{0,1:T(8,128)} %param.9) | copy-start | bytes 225796
  7.2 44.7 %all-gather.7.cloned.1.call-start = ((), (), s32[]{:S(2)}) async-start(), calls=%async_computation.5 | async-start | bytes 2048000 | tf_op jit(solution)/shard_map/all_gather | solution.py:511
  10.9 21.9 %copy-start.14 = (f32[1536]{0:T(1024)S(1)}, f32[1536]{0:T(1024)}, u32[]{:S(2)}) copy-start(f32[1536]{0:T(1024)} %param.12) | copy-start | bytes 18436
  10.9 80.2 %all-gather.5.cloned.1.call-start = ((), (), s32[]{:S(2)}) async-start(), calls=%async_computation.4 | async-start | bytes 2048000 | tf_op jit(solution)/shard_map/all_gather | solution.py:518
  11.0 10.0 %collective-permute-start = (bf16[3,384,128]{2,1,0:T(8,128)(2,1)S(1)}, bf16[3,384,128]{2,1,0:T(8,128)(2,1)S(1)}, u32[]{:S(2)}, u32[]{:S(2)}) collective-permute-start(bf16[3,384,128]{2,1,0:T(8,128)(2,1)S(1)} %slice_select_fusion.1), channel_id=1, source_target_pairs={{0,2},{2,0},{1,3},{3,1},{4,6},{6,4},{5,7},{7,5},{8,10},{10,8},{9,1... | collective-permute-start | bytes 884744 | tf_op jit(solution)/shard_map/ppermute | solution.py:51
  14.0 7.2 %collective-permute-start.1 = (bf16[4,384,128]{2,1,0:T(8,128)(2,1)S(1)}, bf16[4,384,128]{2,1,0:T(8,128)(2,1)S(1)}, u32[]{:S(2)}, u32[]{:S(2)}) collective-permute-start(bf16[4,384,128]{2,1,0:T(8,128)(2,1)S(1)} %bitcast.21), channel_id=1, source_target_pairs={{0,1},{1,0},{2,3},{3,2},{4,5},{5,4},{6,7},{7,6},{8,9},{9,8},{10,11... | collective-permute-start | bytes 1179656 | tf_op jit(solution)/shard_map/ppermute | solution.py:61
  21.1 1.6 collective-permute-start.2
  32.7 201.5 %reduce-scatter.5.cloned.1.call-start = ((), (), s32[]{:S(2)}) async-start(), calls=%async_computation.3 | async-start | bytes 1966080 | tf_op jit(solution)/shard_map/reduce_scatter | solution.py:524
  91.1 1.1 copy-start
  92.2 1.1 copy-start.2
  112.0 1.1 copy-start.4
  113.1 1.1 copy-start.6
  114.3 151.5 %reduce-scatter.3.cloned.1.call-start = ((), (), s32[]{:S(2)}) async-start(), calls=%async_computation.2 | async-start | bytes 1966080 | tf_op jit(solution)/shard_map/reduce_scatter | solution.py:526
  114.5 39.1 %collective-permute-start.7 = (bf16[4,400,512]{2,1,0:T(8,128)(2,1)}, bf16[4,400,512]{2,1,0:T(8,128)(2,1)}, u32[]{:S(2)}, u32[]{:S(2)}) collective-permute-start(bf16[4,400,512]{2,1,0:T(8,128)(2,1)} %bitcast.34), channel_id=1, source_target_pairs={{0,2},{2,0},{1,3},{3,1},{4,6},{6,4},{5,7},{7,5},{8,10},{10,8},{9,1... | collective-permute-start | bytes 4915208 | tf_op jit(solution)/shard_map/ppermute | solution.py:498
  116.0 70.0 %collective-permute-start.6 = (bf16[1536,512]{1,0:T(8,128)(2,1)}, bf16[1536,512]{1,0:T(8,128)(2,1)}, u32[]{:S(2)}, u32[]{:S(2)}) collective-permute-start(bf16[1536,512]{1,0:T(8,128)(2,1)} %copy-done.4), channel_id=1, source_target_pairs={{0,2},{2,0},{1,3},{3,1},{4,6},{6,4},{5,7},{7,5},{8,10},{10,8},{9,1... | collective-permute-start | bytes 4718600 | tf_op jit(solution)/shard_map/ppermute | solution.py:498
  186.1 1.1 copy-start.1
  187.2 1.4 copy-start.5
  188.6 1.4 copy-start.7
  203.3 13.9 %copy-start.16 = (f32[384]{0:T(512)S(1)}, f32[384]{0:T(512)}, u32[]{:S(2)}) copy-start(f32[384]{0:T(512)} %param.10) | copy-start | bytes 4612
  203.3 77.4 %collective-permute-start.9 = (bf16[768,1536]{1,0:T(8,128)(2,1)}, bf16[768,1536]{1,0:T(8,128)(2,1)}, u32[]{:S(2)}, u32[]{:S(2)}) collective-permute-start(bf16[768,1536]{1,0:T(8,128)(2,1)} %get-tuple-element.30), channel_id=1, source_target_pairs={{0,1},{1,0},{2,3},{3,2},{4,5},{5,4},{6,7},{7,6},{8,9},{9,8},{10,11... | collective-permute-start | bytes 7077896 | tf_op jit(solution)/shard_map/ppermute | solution.py:498
  216.7 66.4 %collective-permute-start.8 = (bf16[768,1536]{1,0:T(8,128)(2,1)}, bf16[768,1536]{1,0:T(8,128)(2,1)}, u32[]{:S(2)}, u32[]{:S(2)}) collective-permute-start(bf16[768,1536]{1,0:T(8,128)(2,1)} %get-tuple-element.29), channel_id=1, source_target_pairs={{0,1},{1,0},{2,3},{3,2},{4,5},{5,4},{6,7},{7,6},{8,9},{9,8},{10,11... | collective-permute-start | bytes 7077896 | tf_op jit(solution)/shard_map/ppermute | solution.py:498
  234.3 1.0 copy-start.3
  237.1 28.5 %copy-start.12 = (bf16[384,4,128]{2,1,0:T(4,128)(2,1)S(1)}, bf16[384,4,128]{2,1,0:T(4,128)(2,1)}, u32[]{:S(2)}) copy-start(bf16[384,4,128]{2,1,0:T(4,128)(2,1)} %param.8) | copy-start | bytes 1179652
  237.1 28.6 %copy-start.15 = (f32[384]{0:T(512)S(1)}, f32[384]{0:T(512)}, u32[]{:S(2)}) copy-start(f32[384]{0:T(512)} %param.14) | copy-start | bytes 4612
  251.3 1.6 collective-permute-start.12
  251.4 13.7 %collective-permute-start.3 = (bf16[3,384,128]{2,1,0:T(8,128)(2,1)S(1)}, bf16[3,384,128]{2,1,0:T(8,128)(2,1)S(1)}, u32[]{:S(2)}, u32[]{:S(2)}) collective-permute-start(bf16[3,384,128]{2,1,0:T(8,128)(2,1)S(1)} %slice_select_fusion), channel_id=1, source_target_pairs={{0,2},{2,0},{1,3},{3,1},{4,6},{6,4},{5,7},{7,5},{8,10},{10,8},{9,1... | collective-permute-start | bytes 884744 | tf_op jit(solution)/shard_map/ppermute | solution.py:51
  252.9 12.2 %collective-permute-start.13 = (f32[384,49]{1,0:T(8,128)S(1)}, f32[384,49]{1,0:T(8,128)S(1)}, u32[]{:S(2)}, u32[]{:S(2)}) collective-permute-start(f32[384,49]{1,0:T(8,128)S(1)} %slice_add_fusion), channel_id=1, source_target_pairs={{0,2},{2,0},{1,3},{3,1},{4,6},{6,4},{5,7},{7,5},{8,10},{10,8},{9,1... | collective-permute-start | bytes 225800 | tf_op jit(solution)/shard_map/ppermute | solution.py:498
  254.3 16.0 %collective-permute-start.4 = (bf16[4,384,128]{2,1,0:T(8,128)(2,1)S(1)}, bf16[4,384,128]{2,1,0:T(8,128)(2,1)S(1)}, u32[]{:S(2)}, u32[]{:S(2)}) collective-permute-start(bf16[4,384,128]{2,1,0:T(8,128)(2,1)S(1)} %norm_gradient.1.block.gradient), channel_id=1, source_target_pairs={{0,1},{1,0},{2,3},{3,2},{4,5},{5,4},{6,7},{7,6},{8,9},{9,8},{10,11... | collective-permute-start | bytes 1179656 | tf_op jit(solution)/shard_map/ppermute | solution.py:61
  265.1 22.8 %collective-permute-start.11 = (bf16[1536,768]{1,0:T(8,128)(2,1)}, bf16[1536,768]{1,0:T(8,128)(2,1)}, u32[]{:S(2)}, u32[]{:S(2)}) collective-permute-start(bf16[1536,768]{1,0:T(8,128)(2,1)} %get-tuple-element.32), channel_id=1, source_target_pairs={{0,1},{1,0},{2,3},{3,2},{4,5},{5,4},{6,7},{7,6},{8,9},{9,8},{10,11... | collective-permute-start | bytes 7077896 | tf_op jit(solution)/shard_map/ppermute | solution.py:498
  265.1 5.2 %collective-permute-start.5 = (bf16[3,384,128]{2,1,0:T(8,128)(2,1)S(1)}, bf16[3,384,128]{2,1,0:T(8,128)(2,1)S(1)}, u32[]{:S(2)}, u32[]{:S(2)}) collective-permute-start(bf16[3,384,128]{2,1,0:T(8,128)(2,1)S(1)} %collective-permute-done.3.above.below), channel_id=1, source_target_pairs={{0,1},{1,0},{2,3},{3,2},{4,5},{5,4},{6,7},{7,6},{8,9},{9,8},{10,11... | collective-permute-start | bytes 884744 | tf_op jit(solution)/shard_map/ppermute | solution.py:61
  270.3 10.4 %copy-start.9 = (bf16[768,1536]{1,0:T(8,128)(2,1)S(1)}, bf16[768,1536]{1,0:T(8,128)(2,1)}, u32[]{:S(2)}) copy-start(bf16[768,1536]{1,0:T(8,128)(2,1)} %get-tuple-element.30) | copy-start | bytes 7077892
  270.3 20.7 %collective-permute-start.10 = (bf16[1536,768]{1,0:T(8,128)(2,1)}, bf16[1536,768]{1,0:T(8,128)(2,1)S(1)}, u32[]{:S(2)}, u32[]{:S(2)}) collective-permute-start(bf16[1536,768]{1,0:T(8,128)(2,1)} %get-tuple-element.31), channel_id=1, source_target_pairs={{0,1},{1,0},{2,3},{3,2},{4,5},{5,4},{6,7},{7,6},{8,9},{9,8},{10,11... | collective-permute-start | bytes 7077896 | tf_op jit(solution)/shard_map/ppermute | solution.py:498
  280.7 2.4 copy-start.10
  287.9 3.1 %copy-start.8 = (bf16[1536,768]{1,0:T(8,128)(2,1)S(1)}, bf16[1536,768]{1,0:T(8,128)(2,1)}, u32[]{:S(2)}) copy-start(bf16[1536,768]{1,0:T(8,128)(2,1)} %get-tuple-element.31) | copy-start | bytes 7077892
Sparse Core Ops, SparseCore 0:
  11.0 40.8 all-gather.6
  54.0 37.0 all-gather.4
  114.4 34.1 reduce-scatter.4
  150.7 34.2 reduce-scatter.2

commit v2 on v1

v2 whole, which is shorter than its diff:
```python
import functools

import jax
import jax.numpy as jnp
from jax import lax
from jax.experimental import pallas as pl
from jax.experimental.pallas import tpu as pltpu
from jax.sharding import PartitionSpec as P

KS = 7
HALF = KS // 2
PAD = 16
EPSILON = 1e-06
MIB = 1024 * 1024
F32 = jnp.float32
BF16 = jnp.bfloat16

whole = pl.BlockSpec(memory_space=pltpu.VMEM)
anywhere = pl.BlockSpec(memory_space=pl.ANY)
LIGHT = pl.CostEstimate(flops=1000, bytes_accessed=1000, transcendentals=0)


def params(mib):
    return pltpu.CompilerParams(vmem_limit_bytes=mib * MIB)


def shape(dims, dtype):
    return jax.ShapeDtypeStruct(dims, dtype)


def pieces(values):
    high = values.astype(BF16)
    rest = values - high.astype(F32)
    middle = rest.astype(BF16)
    low = (rest - middle.astype(F32)).astype(BF16)
    return high, middle, low


def stacked_rows(*rows):
    width = rows[0].shape[1]
    row = lax.broadcasted_iota(jnp.int32, (PAD, width), 0)
    block = jnp.zeros((PAD, width), F32)
    for first, values in enumerate(rows):
        for index, part in enumerate(pieces(values)):
            block = jnp.where(row == 3 * first + index, part.astype(F32), block)
    return block.astype(BF16)


def unstacked(block, first):
    return jnp.sum(block[3 * first : 3 * first + 3, :].astype(F32), axis=0, keepdims=True)


def from_sides(low_source, high_source, axis):
    count = lax.axis_size(axis)
    if count == 2:
        index = lax.axis_index(axis)
        sent = jnp.where(index == 0, low_source, high_source)
        got = lax.ppermute(sent, axis, [(0, 1), (1, 0)])
        return got, got
    forward = [(i, i + 1) for i in range(count - 1)]
    backward = [(i + 1, i) for i in range(count - 1)]
    return lax.ppermute(low_source, axis, forward), lax.ppermute(high_source, axis, backward)


def edges(block, axis):
    count = lax.axis_size(axis)
    if count == 2:
        return lax.ppermute(block, axis, [(0, 1), (1, 0)])
    low, high = from_sides(block, block, axis)
    width = block.shape[-1]
    lane = lax.broadcasted_iota(jnp.int32, block.shape, block.ndim - 1)
    return jnp.where(lane < width // 2, high, low)


def surroundings(block):
    rows = block.shape[0]
    above, below = from_sides(block[rows - HALF :], block[:HALF], "rows")
    side = edges(block, "cols")
    if lax.axis_size("rows") == 2:
        corner = edges(above, "cols")
        return block, above, below, side, corner, corner
    return block, above, below, side, edges(above, "cols"), edges(below, "cols")


def flag(test):
    return jnp.where(test, 1.0, 0.0).astype(F32)


def fill_shifts(shifts):
    width = shifts.shape[0] // 2
    col = lax.axis_index("cols")
    has_right, has_left = flag(col < lax.axis_size("cols") - 1), flag(col > 0)
    source = lax.broadcasted_iota(jnp.int32, (width, width), 0)
    target = lax.broadcasted_iota(jnp.int32, (width, width), 1)
    for tap in range(KS):
        cut = slice(tap * width, (tap + 1) * width)
        wanted = target + (tap - HALF)
        shifts[:width, cut] = jnp.where(source == wanted, 1.0, 0.0).astype(BF16)
        right = jnp.where(source + width == wanted, has_right, 0.0)
        left = jnp.where(source - width == wanted, has_left, 0.0)
        shifts[width:, cut] = (right + left).astype(BF16)


def shifted_rows(refs, shifts, at, count):
    block, above, below, side, above_side, below_side = refs
    row = lax.axis_index("rows")
    has_above = flag(row > 0).astype(BF16)
    has_below = flag(row < lax.axis_size("rows") - 1).astype(BF16)
    rows = block.shape[0]
    cut = pl.ds(at, count)
    found = [jnp.concatenate([above[k, cut], above_side[k, cut]], axis=1) * has_above for k in range(HALF)]
    found += [jnp.concatenate([block[k, cut], side[k, cut]], axis=1) for k in range(rows)]
    found += [jnp.concatenate([below[k, cut], below_side[k, cut]], axis=1) * has_below for k in range(HALF)]
    return dot(jnp.concatenate(found, axis=0), shifts[...], ROWS_BY_COLS)


def convolve(refs, shifts, taps, at, count, flipped):
    rows, _, width = refs[0].shape
    moved = shifted_rows(refs, shifts, at, count)
    sums = [None] * rows
    for tap_col in range(KS):
        near = [
            moved[k * count : (k + 1) * count, tap_col * width : (tap_col + 1) * width]
            for k in range(rows + KS - 1)
        ]
        for tap_row in range(KS):
            tap = tap_row * KS + tap_col
            tap = KS * KS - 1 - tap if flipped else tap
            weight = jnp.broadcast_to(taps[:, tap : tap + 1], (count, width))
            for k in range(rows):
                term = weight * near[k + tap_row]
                sums[k] = term if sums[k] is None else sums[k] + term
    return sums


def forward_conv_kernel(block, above, below, side, above_side, below_side, kernel, packed, centered, local, shifts):
    refs = (block, above, below, side, above_side, below_side)
    rows, channels, width = block.shape
    fill_shifts(shifts)

    def step(index, totals):
        at = pl.multiple_of(index * PAD, PAD)
        sums = convolve(refs, shifts, kernel[pl.ds(at, PAD), :], at, PAD, False)
        for k in range(rows):
            centered[pl.ds(at, PAD), k * width : (k + 1) * width] = sums[k]
        return tuple(total + value[:8] + value[8:] for total, value in zip(totals, sums))

    totals = lax.fori_loop(
        0, channels // PAD, step, tuple(jnp.zeros((8, width), F32) for _ in range(rows)), unroll=2
    )
    mean = jnp.concatenate([jnp.sum(total, axis=0, keepdims=True) for total in totals], axis=1) / channels
    local[...] = jnp.broadcast_to(mean, local.shape)

    def finish(index, carry):
        at = pl.multiple_of(index * PAD, PAD)
        value = centered[pl.ds(at, PAD), :] - mean
        centered[pl.ds(at, PAD), :] = value
        packed[pl.ds(at, PAD), :] = value.astype(BF16)
        return carry

    lax.fori_loop(0, channels // PAD, finish, 0, unroll=2)
    packed[channels:, :] = stacked_rows(mean)


def shift_scratch(width):
    return [pltpu.VMEM((2 * width, KS * width), BF16)]


def forward_conv(around, kernel):
    rows, channels, width = around[0].shape
    pixels = rows * width
    return pl.pallas_call(
        forward_conv_kernel,
        out_shape=(
            shape((channels + PAD, pixels), BF16),
            shape((channels, pixels), F32),
            shape((8, pixels), F32),
        ),
        in_specs=[whole] * 7,
        out_specs=(whole,) * 3,
        scratch_shapes=shift_scratch(width),
        compiler_params=params(32),
        cost_estimate=LIGHT,
        name="conv_forward",
    )(*around, kernel)


def backward_conv_kernel(block, above, below, side, above_side, below_side, kernel, cotangent, result, shifts):
    refs = (block, above, below, side, above_side, below_side)
    rows, channels, width = block.shape
    fill_shifts(shifts)

    def step(index, carry):
        at = pl.multiple_of(index * PAD, PAD)
        sums = convolve(refs, shifts, kernel[pl.ds(at, PAD), :], at, PAD, True)
        for k in range(rows):
            result[k, pl.ds(at, PAD)] = (sums[k] + cotangent[k, pl.ds(at, PAD)].astype(F32)).astype(BF16)
        return carry

    lax.fori_loop(0, channels // PAD, step, 0, unroll=2)


def backward_conv(around, kernel, cotangent):
    return pl.pallas_call(
        backward_conv_kernel,
        out_shape=shape(cotangent.shape, BF16),
        in_specs=[whole] * 8,
        out_specs=whole,
        scratch_shapes=shift_scratch(cotangent.shape[2]),
        compiler_params=params(32),
        cost_estimate=LIGHT,
        name="conv_backward",
    )(*around, kernel, cotangent)


def kernel_gradient_kernel(block, above, below, side, above_side, below_side, gradient, result, shifts):
    refs = (block, above, below, side, above_side, below_side)
    rows, channels, width = block.shape
    fill_shifts(shifts)

    def step(index, carry):
        at = pl.multiple_of(index * PAD, PAD)
        moved = shifted_rows(refs, shifts, at, PAD)
        lane = lax.broadcasted_iota(jnp.int32, (PAD, width), 1)
        grads = [gradient[k, pl.ds(at, PAD)].astype(F32) for k in range(rows)]
        sums = jnp.zeros((PAD, width), F32)
        for tap_col in range(KS):
            near = [
                moved[k * PAD : (k + 1) * PAD, tap_col * width : (tap_col + 1) * width]
                for k in range(rows + KS - 1)
            ]
            for tap_row in range(KS):
                total = grads[0] * near[tap_row]
                for k in range(1, rows):
                    total = total + grads[k] * near[k + tap_row]
                tap = tap_row * KS + tap_col
                sums = jnp.where(lane == tap, jnp.sum(total, axis=1, keepdims=True), sums)
        result[pl.ds(at, PAD), :] = sums
        return carry

    lax.fori_loop(0, channels // PAD, step, 0, unroll=2)


def kernel_gradient(around, gradient):
    rows, channels, width = gradient.shape
    return pl.pallas_call(
        kernel_gradient_kernel,
        out_shape=shape((channels, width), F32),
        in_specs=[whole] * 7,
        out_specs=whole,
        scratch_shapes=shift_scratch(width),
        compiler_params=params(32),
        cost_estimate=LIGHT,
        name="kernel_gradient",
    )(*around, gradient)


def pack_kernel(cotangent, scale, gain, packed):
    rows, channels, width = cotangent.shape
    for k in range(rows):
        packed[:channels, k * width : (k + 1) * width] = (
            cotangent[k].astype(F32) * scale[...]
        ).astype(BF16)
    packed[channels:, :] = jnp.zeros((PAD, rows * width), BF16)
    packed[channels:, :channels] = stacked_rows(gain[...])


def pack_cotangent(cotangent, scale, gain):
    rows, channels, width = cotangent.shape
    return pl.pallas_call(
        pack_kernel,
        out_shape=shape((channels + PAD, rows * width), BF16),
        in_specs=[whole] * 3,
        out_specs=whole,
        compiler_params=params(32),
        name="pack_cotangent",
    )(cotangent, scale, gain)


def gelu_parts(values):
    cdf = 0.5 * (1.0 + lax.erf(values * 0.7071067811865476))
    slope = cdf + values * jnp.exp(-0.5 * values * values) * 0.3989422804014327
    return values * cdf, slope


ROWS_BY_COLS = (((1,), (0,)), ((), ()))
COLS_BY_COLS = (((0,), (0,)), ((), ()))
ROWS_BY_ROWS = (((1,), (1,)), ((), ()))


def dot(left, right, dims):
    return lax.dot_general(left, right, dims, preferred_element_type=F32)


def tile_of(hidden_units):
    for size in (256, 128):
        if hidden_units % size == 0:
            return size
    return hidden_units


def fixed(dims):
    return pl.BlockSpec(dims, lambda t: (0,) * len(dims))


def rows_of(tile, width, first=0):
    return pl.BlockSpec((tile, width), lambda t: (t + first, 0))


def columns_of(height, tile, first=0):
    return pl.BlockSpec((height, tile), lambda t: (0, t + first))


def rotated(block):
    count = lax.axis_size("chan")
    return [block] + [
        lax.ppermute(block, "chan", [(i, (i + k) % count) for i in range(count)])
        for k in range(1, count)
    ]


def gain_kernel(cot_all, gain, tails, sem):
    count, padded, pixels = cot_all.shape
    channels = padded - PAD
    copy = pltpu.make_async_copy(cot_all.at[:, channels:, :], tails, sem)
    copy.start()
    copy.wait()
    ones = jnp.ones((PAD, gain.shape[1]), BF16)
    for k in range(count):
        gain[k * channels : (k + 1) * channels, :] = dot(tails[k], ones, COLS_BY_COLS)[:channels, :]


def gain_stage(cot_all):
    count, padded, pixels = cot_all.shape
    return pl.pallas_call(
        gain_kernel,
        out_shape=shape((count * (padded - PAD), 128), F32),
        in_specs=[anywhere],
        out_specs=whole,
        scratch_shapes=[pltpu.VMEM((count, PAD, pixels), BF16), pltpu.SemaphoreType.DMA],
        compiler_params=params(60),
        cost_estimate=LIGHT,
        name="gains",
    )(cot_all)


def normalise(conv_all, gain, normed):
    count, padded, pixels = conv_all.shape
    channels = padded - PAD
    every = count * channels
    means = [jnp.sum(conv_all[k, channels:, :].astype(F32), axis=0, keepdims=True) for k in range(count)]
    mean = means[0]
    for k in range(1, count):
        mean = mean + means[k]
    mean = mean / count
    squares = jnp.zeros((8, pixels), F32)
    for k in range(count):
        moved = means[k] - mean

        def gather(index, total):
            at = pl.multiple_of(index * PAD, PAD)
            value = conv_all[k, pl.ds(at, PAD), :].astype(F32) + moved
            value = value * value
            return total + value[:8] + value[8:]

        squares = lax.fori_loop(0, channels // PAD, gather, squares, unroll=2)
    deviation = lax.rsqrt(jnp.sum(squares, axis=0, keepdims=True) / every + EPSILON)
    for k in range(count):
        moved = means[k] - mean

        def write(index, carry):
            at = pl.multiple_of(index * PAD, PAD)
            to = pl.multiple_of(k * channels + at, PAD)
            value = (conv_all[k, pl.ds(at, PAD), :].astype(F32) + moved) * deviation
            scale = gain[pl.ds(to, PAD), :]
            for p in range(pixels // 128):
                cut = slice(p * 128, (p + 1) * 128)
                normed[pl.ds(to, PAD), cut] = (value[:, cut] * scale).astype(BF16)
            return carry

        lax.fori_loop(0, channels // PAD, write, 0, unroll=2)
    return mean, deviation


def norm_kernel(conv_all, gain, normed, stats):
    mean, deviation = normalise(conv_all, gain, normed)
    row = lax.broadcasted_iota(jnp.int32, stats.shape, 0)
    stats[...] = jnp.where(row == 0, mean, jnp.where(row == 1, deviation, 0.0))


def norm_stage(conv_all, gain):
    pixels = conv_all.shape[2]
    return pl.pallas_call(
        norm_kernel,
        out_shape=(shape((gain.shape[0], pixels), BF16), shape((8, pixels), F32)),
        in_specs=[whole] * 2,
        out_specs=(whole, whole),
        compiler_params=params(32),
        cost_estimate=LIGHT,
        name="norm",
    )(conv_all, gain)


def block_kernel(steps, normed, cot_all, gain, w_expand, bias, w_reduce, hidden, grad_pre, reduced, *refs):
    blocks, (cot, reduce_sum, normed_sum) = refs[:-3], refs[-3:]
    at = pl.program_id(0)

    @pl.when(at == 0)
    def _():
        channels = cot_all.shape[1] - PAD
        for k in range(cot_all.shape[0]):
            cot[k * channels : (k + 1) * channels, :] = cot_all[k, :channels, :]
        reduce_sum[...] = jnp.zeros_like(reduce_sum)
        normed_sum[...] = jnp.zeros_like(normed_sum)

    pre = dot(w_expand[...], normed[...], ROWS_BY_COLS) + bias[...]
    back = dot(w_reduce[...], cot[...], COLS_BY_COLS)
    active, slope = gelu_parts(pre)
    active = active.astype(BF16)
    hidden[...] = active
    grad = (back * slope).astype(BF16)
    grad_pre[...] = grad
    reduce_sum[...] += dot(w_reduce[...], active, ROWS_BY_COLS)
    normed_sum[...] += dot(w_expand[...], grad, COLS_BY_COLS)

    @pl.when(at == steps - 1)
    def _():
        every, pixels = normed.shape
        reduced[...] = reduce_sum[...].astype(BF16)

        def step(index, totals):
            cut = pl.ds(pl.multiple_of(index * PAD, PAD), PAD)
            value = normed_sum[cut, :]
            first = value * jnp.concatenate([gain[cut, :]] * (pixels // gain.shape[1]), axis=1)
            cross = value * normed[cut, :].astype(F32)
            return totals[0] + first[:8] + first[8:], totals[1] + cross[:8] + cross[8:]

        totals = lax.fori_loop(0, every // PAD, step, (jnp.zeros((8, pixels), F32),) * 2, unroll=2)
        moments = stacked_rows(*[jnp.sum(total, axis=0, keepdims=True) for total in totals])
        for k, block in enumerate(blocks):
            height = block.shape[0] - PAD
            place = lax.rem(lax.axis_index("chan") + k, len(blocks)) if len(blocks) > 1 else 0
            block[:height, :] = normed_sum[pl.ds(pl.multiple_of(place * height, PAD), height), :].astype(BF16)
            block[height:, :] = moments


def block_stage(normed, cot_all, gain, w_expand, bias, w_reduce):
    count = lax.axis_size("chan")
    units, every = w_expand.shape
    pixels = normed.shape[1]
    tile = tile_of(units)
    steps = units // tile
    blocks = count if count <= 4 else 1
    return pl.pallas_call(
        functools.partial(block_kernel, steps),
        grid=(steps,),
        out_shape=(shape((units, pixels), BF16),) * 2
        + (shape((every, pixels), BF16),)
        + (shape((every // blocks + PAD, pixels), BF16),) * blocks,
        in_specs=[
            fixed(normed.shape),
            fixed(cot_all.shape),
            fixed(gain.shape),
            rows_of(tile, every),
            rows_of(tile, 1),
            columns_of(every, tile),
        ],
        out_specs=(rows_of(tile, pixels),) * 2
        + (fixed((every, pixels)),)
        + (fixed((every // blocks + PAD, pixels)),) * blocks,
        scratch_shapes=[
            pltpu.VMEM((every, pixels), BF16),
            pltpu.VMEM((every, pixels), F32),
            pltpu.VMEM((every, pixels), F32),
        ],
        compiler_params=params(60),
        cost_estimate=LIGHT,
        name="pointwise_block",
    )(normed, cot_all, gain, w_expand, bias, w_reduce)


def side_by_side(pixels):
    index = lax.axis_index("rows")
    own = pl.ds(pl.multiple_of(index * pixels, pixels), pixels)
    other = pl.ds(pl.multiple_of((1 - index) * pixels, pixels), pixels)
    return own, other


def weight_kernel(
    normed_own, normed_other, cot_own, cot_other, hidden_own, pre_own, w_expand, bias, w_reduce,
    grad_reduce, grad_expand, normed, cot, hidden, grad_pre, sems,
):
    pixels = normed_own.shape[1]
    own, other = side_by_side(pixels)

    @pl.when(pl.program_id(0) == 0)
    def _():
        copies = [
            pltpu.make_async_copy(normed_other, normed.at[:, other], sems.at[0]),
            pltpu.make_async_copy(normed_own, normed.at[:, own], sems.at[1]),
        ]
        count, padded, _ = cot_own.shape
        channels = padded - PAD
        for k in range(count):
            rows = slice(k * channels, (k + 1) * channels)
            for x, (source, cut) in enumerate(((cot_own, own), (cot_other, other))):
                copies.append(
                    pltpu.make_async_copy(source.at[k, :channels, :], cot.at[rows, cut], sems.at[2 + 2 * k + x])
                )
        for copy in copies:
            copy.start()
        for copy in copies:
            copy.wait()

    pre = dot(w_expand[...], normed[:, other], ROWS_BY_COLS) + bias[...]
    back = dot(w_reduce[...], cot[:, other], COLS_BY_COLS)
    active, slope = gelu_parts(pre)
    hidden[:, own] = hidden_own[...]
    hidden[:, other] = active.astype(BF16)
    grad_pre[:, own] = pre_own[...]
    grad_pre[:, other] = (back * slope).astype(BF16)
    grad_reduce[...] = dot(cot[...], hidden[...], ROWS_BY_ROWS).astype(BF16)
    grad_expand[...] = dot(grad_pre[...], normed[...], ROWS_BY_ROWS).astype(BF16)


def weight_gradients(part, parts, normed_own, normed_other, cot_own, cot_other, hidden, grad_pre, w_expand, bias, w_reduce):
    every, pixels = normed_own.shape
    units = w_expand.shape[0]
    tile = tile_of(units)
    steps = units // tile // parts
    first = part * steps
    return pl.pallas_call(
        weight_kernel,
        grid=(steps,),
        out_shape=(shape((every, steps * tile), BF16), shape((steps * tile, every), BF16)),
        in_specs=[anywhere] * 4
        + [
            rows_of(tile, pixels, first),
            rows_of(tile, pixels, first),
            rows_of(tile, every, first),
            rows_of(tile, 1, first),
            columns_of(every, tile, first),
        ],
        out_specs=(columns_of(every, tile), rows_of(tile, every)),
        scratch_shapes=[
            pltpu.VMEM((every, 2 * pixels), BF16),
            pltpu.VMEM((every, 2 * pixels), BF16),
            pltpu.VMEM((tile, 2 * pixels), BF16),
            pltpu.VMEM((tile, 2 * pixels), BF16),
            pltpu.SemaphoreType.DMA((2 + 2 * cot_own.shape[0],)),
        ],
        compiler_params=params(60),
        cost_estimate=LIGHT,
        name="weight_gradients",
    )(normed_own, normed_other, cot_own, cot_other, hidden, grad_pre, w_expand, bias, w_reduce)


def pair_kernel(*refs):
    mine, theirs, result = refs[0], refs[1], refs[-1]
    result[...] = (mine[...].astype(F32) + theirs[...].astype(F32)).astype(BF16)


def add_pair(part, parts, axis, mine, theirs, target):
    height, width = mine.shape
    if axis == 0:
        tile = 384 if height % 384 == 0 else tile_of(height)
        steps = height // tile
        block, dims = rows_of(tile, width), (height * parts, width)
        placed = rows_of(tile, width, part * steps)
    else:
        tile = 384 if height % 384 == 0 else tile_of(height)
        steps = height // tile
        block, dims = rows_of(tile, width), (height, width * parts)
        placed = pl.BlockSpec((tile, width), lambda t: (t, part))
    known = () if target is None else (target,)
    return pl.pallas_call(
        pair_kernel,
        grid=(steps,),
        out_shape=shape(dims, BF16),
        in_specs=[block, block] + [anywhere] * len(known),
        out_specs=placed,
        input_output_aliases={2: 0} if known else {},
        compiler_params=params(60),
        cost_estimate=LIGHT,
        name="add_pair",
    )(mine, theirs, *known)


def norm_gradient_kernel(every, centered, local, stats, gain, *refs):
    blocks, result = refs[:-1], refs[-1]
    rows, channels, width = result.shape
    mean, deviation = stats[0:1, :], stats[1:2, :]
    first = cross = 0.0
    for block in blocks:
        tail = block[channels:, :]
        first = first + unstacked(tail, 0)
        cross = cross + unstacked(tail, 1)
    first, cross = first / every, cross / every
    shift = local[0:1, :] - mean

    def step(index, carry):
        at = pl.multiple_of(index * PAD, PAD)
        cut = pl.ds(at, PAD)
        hat = (centered[cut, :] + shift) * deviation
        value = blocks[0][cut, :].astype(F32)
        for block in blocks[1:]:
            value = value + block[cut, :].astype(F32)
        value = value * gain[cut, :]
        value = ((value - first - hat * cross) * deviation).astype(BF16)
        for k in range(rows):
            result[k, cut] = value[:, k * width : (k + 1) * width]
        return carry

    lax.fori_loop(0, channels // PAD, step, 0)


def norm_gradient(every, dims, blocks, centered, local, stats, gain):
    return pl.pallas_call(
        functools.partial(norm_gradient_kernel, every),
        out_shape=shape(dims, BF16),
        in_specs=[whole] * (4 + len(blocks)),
        out_specs=whole,
        compiler_params=params(32),
        cost_estimate=LIGHT,
        name="norm_gradient",
    )(centered, local, stats, gain, *blocks)


def scattered(blocks):
    count = lax.axis_size("chan")
    if len(blocks) == 1:
        height = blocks[0].shape[0] - PAD
        total = lax.psum_scatter(blocks[0][:height], "chan", scatter_dimension=0, tiled=True)
        tail = blocks[0][height:].astype(F32)
        sums = jnp.stack([jnp.sum(tail[:3], axis=0), jnp.sum(tail[3:6], axis=0)])
        sums = lax.psum(sums, "chan")
        parts = [part for row in sums for part in pieces(row)]
        tail = jnp.zeros(tail.shape, BF16).at[:6].set(jnp.stack(parts))
        return [jnp.concatenate([total, tail])]
    return [blocks[0]] + [
        lax.ppermute(blocks[k], "chan", [(i, (i + k) % count) for i in range(count)])
        for k in range(1, count)
    ]


def after(values, *others):
    return lax.optimization_barrier((values, others))[0]


def swap(values, axis):
    return lax.ppermute(values, axis, [(0, 1), (1, 0)])


def on_device(
    image, kernel, layer_norm_weight, w_expand, bias_expand, w_reduce, layer_scale, cotangent
):
    channels, tile_rows, tile_cols = image.shape
    pixels = tile_rows * tile_cols
    every = w_reduce.shape[0]
    two_tiles = lax.axis_size("rows") == 2 and lax.axis_size("cols") == 2

    image_rows = jnp.transpose(image, (1, 0, 2))
    around = surroundings(image_rows)
    cot_rows = jnp.transpose(cotangent, (1, 0, 2))
    packed_cot = pack_cotangent(cot_rows, layer_scale[:, None], layer_norm_weight[None, :])
    cot_all = lax.all_gather(packed_cot, "chan")

    bias = bias_expand[:, None]
    packed_conv, centered, local = forward_conv(around, kernel)
    conv_all = lax.all_gather(packed_conv, "chan")
    cot_all = after(cot_all, packed_conv)
    gain = gain_stage(cot_all)
    normed, stats = norm_stage(conv_all, gain)
    ready = normed
    if two_tiles:
        cot_other = swap(cot_all, "rows")
        normed_other = swap(normed, "rows")
        ready = after(normed, cot_other)
    hidden, grad_pre, reduced, *blocks = block_stage(ready, cot_all, gain, w_expand, bias, w_reduce)
    norm_inputs = (scattered(blocks), centered, local, stats)

    if two_tiles:
        weight_inputs = (normed, normed_other, cot_all, cot_other, hidden, grad_pre, w_expand, bias, w_reduce)
        found = weight_gradients(0, 1, *weight_inputs)
        norm_inputs = after(norm_inputs, found)
    reduced = lax.psum_scatter(reduced, "chan", scatter_dimension=0, tiled=True).astype(F32)
    gradient = norm_gradient(every, image_rows.shape, *norm_inputs, layer_norm_weight[:, None])
    grad_around = surroundings(gradient)
    taps = kernel_gradient(around, gradient)
    if two_tiles:
        grad_around = after(grad_around, reduced)
    grad_rows = backward_conv(grad_around, kernel, cot_rows)
    grad_input = jnp.transpose(grad_rows, (1, 0, 2))
    if two_tiles:
        taps = after(taps, grad_rows)
        taps = taps + swap(taps, "cols")
        taps = taps + swap(taps, "rows")
        theirs = [swap(after(mine, gradient), "cols") for mine in found]
        grad_reduce, grad_expand = [add_pair(0, 1, 0, *pair, None) for pair in zip(found, theirs)]
    else:
        taps = lax.psum(taps, ("rows", "cols"))
        cot = cot_all[:, :channels, :].reshape(every, pixels)
        grad_reduce = dot(cot, hidden, ROWS_BY_ROWS).astype(BF16)
        grad_expand = dot(grad_pre, normed, ROWS_BY_ROWS).astype(BF16)
        grad_reduce, grad_expand = lax.psum((grad_reduce, grad_expand), ("rows", "cols"))
    taps = taps[:, : KS * KS]

    output = (
        image.reshape(channels, pixels).astype(F32) + layer_scale[:, None] * reduced
    ).astype(BF16).reshape(image.shape)
    return output, grad_input, grad_expand, grad_reduce, taps


def solution(mesh):
    placed = (
        P("chan", ("groups", "rows"), "cols"),
        P("chan", None),
        P("chan"),
        P("chan", None),
        P("chan"),
        P(None, "chan"),
        P("chan"),
        P("chan", ("groups", "rows"), "cols"),
    )
    return jax.shard_map(
        on_device,
        mesh=mesh,
        in_specs=placed,
        out_specs=(
            P("chan", ("groups", "rows"), "cols"),
            P("chan", ("groups", "rows"), "cols"),
            P(("groups", "chan"), None),
            P("groups", "chan"),
            P(("groups", "chan"), None),
        ),
        check_vma=False,
    )
```

time: 301 us -> 216 us (0.72)
  waiting for transfers between devices: 144 us -> 92 us
  blocking collectives: 17 us -> 0 us
  other arithmetic: 16.4 us -> 1.33 us
  starting transfers between devices: 9.37 us -> 14.4 us
  local copies, waits for them, and re-layouts: 18.4 us -> 13.7 us
    ppermute x8 -> x6, waiting for transfers between devices: 80.2 us -> 16.8 us  [swap(): return lax.ppermute(values, axis, [(0, 1), (1, 0)])]
    psum x1 -> x0, blocking collectives: 17 us -> none  [on_device(): moments = lax.psum(moments, 'chan')]
    pallas_call x3 -> x6, Pallas kernels: 45.3 us -> 57 us  [the longest x1 23.2 us: weight_gradients(): pl.pallas_call(weight_kernel, grid=(steps,), out_shape=(shape((every, ste...]
    another operation x4 -> x0, other arithmetic: 8.51 us -> none
    pallas_call x1, Pallas kernels: 14.2 us -> 6.22 us  [kernel_gradient(): pl.pallas_call(kernel_gradient_kernel, out_shape=shape((channels, width),...]
    ppermute x2, waiting for transfers between devices: 7.01 us -> 14.6 us  [from_sides(): got = lax.ppermute(sent, axis, [(0, 1), (1, 0)])]
    concatenate x2 -> x0, other arithmetic: 5.05 us -> none  [the longest x1 2.56 us: on_device(): grad_reduce = jnp.concatenate(reduce_parts, axis=1).astype(BF16)]
    unnamed x41 -> x23, local copies, waits for them, and re-layouts: 13.8 us -> 9.42 us
  transfers between devices with their start and end apart: 18 -> 18, of which waited for: 7 -> 9; matrix products, arithmetic and copies ran while one was open for 6% -> 4% of each run, Pallas kernels for 21% -> 32%
where the time goes in v2:
time: 216 us; the launch traced here: 215 us
  waiting for transfers between devices  92 us (43%)
  Pallas kernels  79.8 us (37%)
  starting transfers between devices  14.4 us (7%)
  between operations  14 us (6%)
  local copies, waits for them, and re-layouts  13.7 us (6%)
    all_gather x1, waiting for transfers between devices, on_device(): conv_all = lax.all_gather(packed_conv, 'chan')  35.6 us
    pallas_call x1, Pallas kernels, weight_gradients(): pl.pallas_call(weight_kernel, grid=(steps,), out_shape=(shape((every, ste...  23.2 us
    all_gather x1, waiting for transfers between devices, on_device(): cot_all = lax.all_gather(packed_cot, 'chan')  20.7 us
    pallas_call x1, Pallas kernels, block_stage(): pl.pallas_call(functools.partial(block_kernel, steps), grid=(steps,), out...  17.4 us
    ppermute x6, waiting for transfers between devices, swap(): return lax.ppermute(values, axis, [(0, 1), (1, 0)])  16.8 us
    ppermute x2, waiting for transfers between devices, from_sides(): got = lax.ppermute(sent, axis, [(0, 1), (1, 0)])  14.6 us
    pallas_call x2, Pallas kernels, add_pair(): pl.pallas_call(pair_kernel, grid=(steps,), out_shape=shape(dims, BF16), i...  12.9 us
    unnamed x23, local copies, waits for them, and re-layouts  9.42 us
  transfers between devices with their start and end apart: 18, of which 9 were waited for; matrix products, arithmetic and copies ran while one was open for 4% of the time, Pallas kernels for 32%

profile of v2, /device:TPU:0, one launch (start us, length us, event | category | flops | bytes accessed | tf_op | source)
XLA Modules:
  0.0 215.2 jit_solution(9225402972129850688)
XLA Ops:
  7.2 0.0 all-gather.7.cloned.1.call-start
  7.2 1.0 copy.33
  8.3 0.8 broadcast_in_dim.17.scale
  9.1 0.7 broadcast_in_dim.14.gain
  9.7 1.0 pack_cotangent.1
  10.8 0.0 all-gather.7.cloned.1.call-update
  10.8 0.0 all-gather.5.cloned.1.call-start
  10.9 1.1 copy.34
  11.9 3.0 %collective-permute-start = (bf16[3,384,128]{2,1,0:T(8,128)(2,1)S(1)}, bf16[3,384,128]{2,1,0:T(8,128)(2,1)S(1)}, u32[]{:S(2)}, u32[]{:S(2)}) collective-permute-start(bf16[3,384,128]{2,1,0:T(8,128)(2,1)S(1)} %slice_select_fusion.1), channel_id=1, source_target_pairs={{0,2},{2,0},{1,3},{3,1},{4,6},{6,4},{5,7},{7,5},{8,10},{10,8},{9,1... | collective-permute-start | bytes 884744 | tf_op jit(solution)/shard_map/ppermute | solution.py:58
  14.9 0.0 collective-permute-start.1
  15.0 7.0 %collective-permute-done.above.below = bf16[3,384,128]{2,1,0:T(8,128)(2,1)S(1)} collective-permute-done((bf16[3,384,128]{2,1,0:T(8,128)(2,1)S(1)}, bf16[3,384,128]{2,1,0:T(8,128)(2,1)S(1)}, u32[]{:S(2)}, u32[]{:S(2)}) %collective-permute-start) | collective-permute-done | bytes 294944 | tf_op jit(solution)/shard_map/ppermute | solution.py:58
  22.0 0.0 collective-permute-start.2
  22.0 1.0 copy.20.kernel
  23.0 0.5 collective-permute-done.2.above_side.below_side
  23.5 6.6 %conv_forward.1 = (bf16[400,512]{1,0:T(8,128)(2,1)}, f32[384,512]{1,0:T(8,128)S(1)}, f32[8,512]{1,0:T(8,128)S(1)}) custom-call(bf16[4,384,128]{2,1,0:T(8,128)(2,1)S(1)} %bitcast.17, bf16[3,384,128]{2,1,0:T(8,128)(2,1)S(1)} %collective-permute-done.above.below, bf16[3,384,128]{2,1,0:T(8,128)(2,1)S(1)} %collective-permute-done.above.below, ...), custom_call_target="tpu_custom_call" | custom-call | flops 1000 | bytes 1000 | tf_op jit(solution)/shard_map/conv_forward/pallas_call | solution.py:172
  30.2 0.9 copy-done.3
  31.1 0.0 all-gather.5.cloned.1.call-update
  31.1 0.0 reduce-scatter.2.cloned.1.call-start
  31.2 20.7 %all-gather.7.cloned.1.call-done = bf16[1600,512]{1,0:T(8,128)(2,1)} async-done(((bf16[400,512]{1,0:T(8,128)(2,1)}), bf16[1600,512]{1,0:T(8,128)(2,1)}) %all-gather.7.cloned.1.call-update) | async-done | bytes 1638416 | tf_op jit(solution)/shard_map/all_gather | solution.py:666
  51.8 1.5 collective-permute-start.3
  53.3 2.1 gains.1.gain
  55.4 35.6 %all-gather.5.cloned.1.call-done = bf16[1600,512]{1,0:T(8,128)(2,1)} async-done(((bf16[400,512]{1,0:T(8,128)(2,1)}), bf16[1600,512]{1,0:T(8,128)(2,1)}) %all-gather.5.cloned.1.call-update) | async-done | bytes 1638416 | tf_op jit(solution)/shard_map/all_gather | solution.py:670
  91.0 1.1 copy-done
  92.2 1.4 copy-done.2
  93.6 1.5 norm.1
  95.1 0.0 copy-start.1
  95.1 1.5 collective-permute-start.7
  96.6 1.9 broadcast_in_dim.18.bias
  98.5 17.4 %pointwise_block.1 = (bf16[1536,512]{1,0:T(8,128)(2,1)}, bf16[1536,512]{1,0:T(8,128)(2,1)}, bf16[1536,512]{1,0:T(8,128)(2,1)}, bf16[400,512]{1,0:T(8,128)(2,1)},...) custom-call(bf16[1536,512]{1,0:T(8,128)(2,1)} %copy-done.1, ...), custom_call_target="tpu_custom_call" | custom-call | flops 1000 | bytes 1000 | tf_op jit(solution)/shard_map/pointwise_block/pallas_call | solution.py:454
  115.9 0.5 collective-permute-start.4
  116.3 1.4 collective-permute-start.5
  117.7 2.4 %collective-permute-start.6 = (bf16[400,512]{1,0:T(8,128)(2,1)}, bf16[400,512]{1,0:T(8,128)(2,1)}, u32[]{:S(2)}, u32[]{:S(2)}) collective-permute-start(bf16[400,512]{1,0:T(8,128)(2,1)} %get-tuple-element.45), channel_id=1, source_target_pairs={{0,12},{4,0},{8,4},{12,8},{1,13},{5,1},{9,5},{13,9},{2,14},{6,2},{... | collective-permute-start | bytes 1228808 | tf_op jit(solution)/shard_map/ppermute | solution.py:641
  120.1 0.1 broadcast_in_dim.19.gain
  120.2 11.1 %collective-permute-done.7.normed_other = bf16[1536,512]{1,0:T(8,128)(2,1)} collective-permute-done((bf16[1536,512]{1,0:T(8,128)(2,1)S(1)}, bf16[1536,512]{1,0:T(8,128)(2,1)}, u32[]{:S(2)}, u32[]{:S(2)}) %collective-permute-start.7) | collective-permute-done | bytes 1572896 | tf_op jit(solution)/shard_map/ppermute | solution.py:651
  131.3 23.2 %weight_gradients.1 = (bf16[1536,1536]{1,0:T(8,128)(2,1)}, bf16[1536,1536]{1,0:T(8,128)(2,1)}) custom-call(bf16[1536,512]{1,0:T(8,128)(2,1)} %copy-done.1, bf16[1536,512]{1,0:T(8,128)(2,1)} %collective-permute-done.7.normed_other, bf16[4,400,512]{2,1,0:T(8,128)(2,1)} %bitcast.26, bf16[4,400,512]{2,1,0:T(8,128)(2,1)} %collective-permute-done.3.cot_other, ...), custom_call_target="tpu_custom_call" | custom-call | flops 1000 | bytes 1000 | tf_op jit(solution)/shard_map/weight_gradients/pallas_call | solution.py:532
  154.5 0.0 collective-permute-done.4.refs_1_
  154.5 0.0 collective-permute-done.5.refs_2_
  154.6 1.0 copy-done.5
  155.6 3.1 %norm_gradient.1.block.gradient = bf16[4,384,128]{2,1,0:T(8,128)(2,1)S(1)} custom-call(f32[384,512]{1,0:T(8,128)S(1)} %copy-done.4, f32[8,512]{1,0:T(8,128)S(1)} %get-tuple-element.54.local, f32[8,512]{1,0:T(8,128)S(1)} %get-tuple-element.55.stats, f32[384,1]{1,0:T(8,128)S(1)} %broadcast_in_dim.19.gain, bf16[400,512]{1,0:T(8,128)(2,1)S(1)} %copy-done.5, ...), custom_call_target="tpu_custom_call" | custom-call | flops 1000 | bytes 1000 | tf_op jit(solution)/shard_map/norm_gradient/pallas_call | solution.py:618
  158.7 0.1 collective-permute-start.11
  158.8 0.5 collective-permute-start.12
  159.3 0.0 reduce-scatter.2.cloned.1.call-update
  159.3 0.0 copy-start.7
  159.4 1.4 collective-permute-start.8
  160.8 7.6 %collective-permute-done.8.above.below = bf16[3,384,128]{2,1,0:T(8,128)(2,1)S(1)} collective-permute-done((bf16[3,384,128]{2,1,0:T(8,128)(2,1)S(1)}, bf16[3,384,128]{2,1,0:T(8,128)(2,1)S(1)}, u32[]{:S(2)}, u32[]{:S(2)}) %collective-permute-start.8) | collective-permute-done | bytes 294944 | tf_op jit(solution)/shard_map/ppermute | solution.py:58
  168.4 0.0 collective-permute-start.10
  168.4 6.2 %kernel_gradient.1 = f32[384,128]{1,0:T(8,128)S(1)} custom-call(bf16[4,384,128]{2,1,0:T(8,128)(2,1)S(1)} %bitcast.18, bf16[3,384,128]{2,1,0:T(8,128)(2,1)S(1)} %collective-permute-done.above.below, bf16[3,384,128]{2,1,0:T(8,128)(2,1)S(1)} %collective-permute-done.above.below, bf16[4,384,128]{2,1,0:T(8,128)(2,1)S(1)} %collective-permute-done.1.side, ...), custom_call_target="tpu_custom_call" | custom-call | flops 1000 | bytes 1000 | tf_op jit(solution)/shard_map/kernel_gradient/pallas_call | solution.py:246
  174.7 0.0 collective-permute-done.9.side
  174.7 0.0 collective-permute-done.10.above_side.below_side
  174.7 5.7 %conv_backward.1 = bf16[4,384,128]{2,1,0:T(8,128)(2,1)S(1)} custom-call(bf16[4,384,128]{2,1,0:T(8,128)(2,1)S(1)} %norm_gradient.1.block.gradient, bf16[3,384,128]{2,1,0:T(8,128)(2,1)S(1)} %collective-permute-done.8.above.below, bf16[3,384,128]{2,1,0:T(8,128)(2,1)S(1)} %collective-permute-done.8.above.below, ...), custom_call_target="tpu_custom_call" | custom-call | flops 1000 | bytes 1000 | tf_op jit(solution)/shard_map/conv_backward/pallas_call | solution.py:204
  180.4 0.6 collective-permute-start.13
  181.0 1.1 collective-permute-done.13
  182.1 1.5 collective-permute-start.14
  183.5 0.1 convert.1
  183.6 1.1 copy.27
  184.7 4.6 %collective-permute-done.14 = f32[384,128]{1,0:T(8,128)S(1)} collective-permute-done((f32[384,128]{1,0:T(8,128)S(1)}, f32[384,128]{1,0:T(8,128)S(1)}, u32[]{:S(2)}, u32[]{:S(2)}) %collective-permute-start.14) | collective-permute-done | bytes 196640 | tf_op jit(solution)/shard_map/ppermute | solution.py:651
  189.4 0.8 copy.28
  190.1 3.6 %reduce-scatter.2.cloned.1.call-done = bf16[384,512]{1,0:T(8,128)(2,1)} async-done(((bf16[1536,512]{1,0:T(8,128)(2,1)}), bf16[384,512]{1,0:T(8,128)(2,1)}) %reduce-scatter.2.cloned.1.call-update) | async-done | bytes 393232 | tf_op jit(solution)/shard_map/reduce_scatter | solution.py:686
  193.7 1.1 fusion
  194.9 0.8 reshape.17
  195.7 0.0 collective-permute-done.11.refs_1_
  195.7 6.4 %add_pair.2 = bf16[1536,1536]{1,0:T(8,128)(2,1)} custom-call(bf16[1536,1536]{1,0:T(8,128)(2,1)} %get-tuple-element.66.refs_0_, bf16[1536,1536]{1,0:T(8,128)(2,1)} %collective-permute-done.11.refs_1_), custom_call_target="tpu_custom_call" | custom-call | flops 1000 | bytes 1000 | tf_op jit(solution)/shard_map/add_pair/pallas_call | solution.py:576
  202.2 0.0 collective-permute-done.12.refs_1_
  202.2 6.5 %add_pair.3 = bf16[1536,1536]{1,0:T(8,128)(2,1)} custom-call(bf16[1536,1536]{1,0:T(8,128)(2,1)} %get-tuple-element.67.refs_0_, bf16[1536,1536]{1,0:T(8,128)(2,1)} %collective-permute-done.12.refs_1_), custom_call_target="tpu_custom_call" | custom-call | flops 1000 | bytes 1000 | tf_op jit(solution)/shard_map/add_pair/pallas_call | solution.py:576
  (20 shorter events, 0.1 us)
Async XLA Ops:
  7.2 44.7 %all-gather.7.cloned.1.call-start = ((), (), s32[]{:S(2)}) async-start(), calls=%async_computation.3 | async-start | bytes 2048000 | tf_op jit(solution)/shard_map/all_gather | solution.py:666
  10.8 80.2 %all-gather.5.cloned.1.call-start = ((), (), s32[]{:S(2)}) async-start(), calls=%async_computation.2 | async-start | bytes 2048000 | tf_op jit(solution)/shard_map/all_gather | solution.py:670
  11.9 10.0 %collective-permute-start = (bf16[3,384,128]{2,1,0:T(8,128)(2,1)S(1)}, bf16[3,384,128]{2,1,0:T(8,128)(2,1)S(1)}, u32[]{:S(2)}, u32[]{:S(2)}) collective-permute-start(bf16[3,384,128]{2,1,0:T(8,128)(2,1)S(1)} %slice_select_fusion.1), channel_id=1, source_target_pairs={{0,2},{2,0},{1,3},{3,1},{4,6},{6,4},{5,7},{7,5},{8,10},{10,8},{9,1... | collective-permute-start | bytes 884744 | tf_op jit(solution)/shard_map/ppermute | solution.py:58
  14.9 8.0 %collective-permute-start.1 = (bf16[4,384,128]{2,1,0:T(8,128)(2,1)S(1)}, bf16[4,384,128]{2,1,0:T(8,128)(2,1)S(1)}, u32[]{:S(2)}, u32[]{:S(2)}) collective-permute-start(bf16[4,384,128]{2,1,0:T(8,128)(2,1)S(1)} %bitcast.16), channel_id=1, source_target_pairs={{0,1},{1,0},{2,3},{3,2},{4,5},{5,4},{6,7},{7,6},{8,9},{9,8},{10,11... | collective-permute-start | bytes 1179656 | tf_op jit(solution)/shard_map/ppermute | solution.py:68
  22.0 1.6 collective-permute-start.2
  30.2 0.9 copy-start.3
  31.1 162.6 %reduce-scatter.2.cloned.1.call-start = ((), (), s32[]{:S(2)}) async-start(), calls=%async_computation.1 | async-start | bytes 1966080 | tf_op jit(solution)/shard_map/reduce_scatter | solution.py:686
  51.8 46.7 %collective-permute-start.3 = (bf16[4,400,512]{2,1,0:T(8,128)(2,1)}, bf16[4,400,512]{2,1,0:T(8,128)(2,1)}, u32[]{:S(2)}, u32[]{:S(2)}) collective-permute-start(bf16[4,400,512]{2,1,0:T(8,128)(2,1)} %bitcast.23), channel_id=1, source_target_pairs={{0,2},{2,0},{1,3},{3,1},{4,6},{6,4},{5,7},{7,5},{8,10},{10,8},{9,1... | collective-permute-start | bytes 4915208 | tf_op jit(solution)/shard_map/ppermute | solution.py:651
  91.0 1.1 copy-start
  92.1 1.4 copy-start.2
  95.1 3.4 %copy-start.1 = (bf16[1536,512]{1,0:T(8,128)(2,1)}, bf16[1536,512]{1,0:T(8,128)(2,1)S(1)}, u32[]{:S(2)}) copy-start(bf16[1536,512]{1,0:T(8,128)(2,1)S(1)} %get-tuple-element.40.normed.normed_own) | copy-start | bytes 4718596
  95.1 36.2 %collective-permute-start.7 = (bf16[1536,512]{1,0:T(8,128)(2,1)S(1)}, bf16[1536,512]{1,0:T(8,128)(2,1)}, u32[]{:S(2)}, u32[]{:S(2)}) collective-permute-start(bf16[1536,512]{1,0:T(8,128)(2,1)S(1)} %get-tuple-element.40.normed.normed_own), channel_id=1, source_target_pairs={{0,2},{2,0},{1,3},{3,1},{4,6},{6,4},{5,7},{7,5},{8,10},{10,8},{9,1... | collective-permute-start | bytes 4718600 | tf_op jit(solution)/shard_map/ppermute | solution.py:651
  98.5 21.6 %copy-start.8 = (f32[384]{0:T(512)S(1)}, f32[384]{0:T(512)}, u32[]{:S(2)}) copy-start(f32[384]{0:T(512)} %param.10) | copy-start | bytes 4612
  115.9 38.7 %collective-permute-start.4 = (bf16[400,512]{1,0:T(8,128)(2,1)}, bf16[400,512]{1,0:T(8,128)(2,1)}, u32[]{:S(2)}, u32[]{:S(2)}) collective-permute-start(bf16[400,512]{1,0:T(8,128)(2,1)} %get-tuple-element.43), channel_id=1, source_target_pairs={{0,4},{4,8},{8,12},{12,0},{1,5},{5,9},{9,13},{13,1},{2,6},{6,10},{... | collective-permute-start | bytes 1228808 | tf_op jit(solution)/shard_map/ppermute | solution.py:641
  116.3 38.2 %collective-permute-start.5 = (bf16[400,512]{1,0:T(8,128)(2,1)}, bf16[400,512]{1,0:T(8,128)(2,1)}, u32[]{:S(2)}, u32[]{:S(2)}) collective-permute-start(bf16[400,512]{1,0:T(8,128)(2,1)} %get-tuple-element.44), channel_id=1, source_target_pairs={{0,8},{4,12},{8,0},{12,4},{1,9},{5,13},{9,1},{13,5},{2,10},{6,14},... | collective-permute-start | bytes 1228808 | tf_op jit(solution)/shard_map/ppermute | solution.py:641
  117.7 36.8 %collective-permute-start.6 = (bf16[400,512]{1,0:T(8,128)(2,1)}, bf16[400,512]{1,0:T(8,128)(2,1)}, u32[]{:S(2)}, u32[]{:S(2)}) collective-permute-start(bf16[400,512]{1,0:T(8,128)(2,1)} %get-tuple-element.45), channel_id=1, source_target_pairs={{0,12},{4,0},{8,4},{12,8},{1,13},{5,1},{9,5},{13,9},{2,14},{6,2},{... | collective-permute-start | bytes 1228808 | tf_op jit(solution)/shard_map/ppermute | solution.py:641
  131.3 23.2 %copy-start.4 = (f32[384,512]{1,0:T(8,128)S(1)}, f32[384,512]{1,0:T(8,128)}, u32[]{:S(2)}) copy-start(f32[384,512]{1,0:T(8,128)} %copy-done.3) | copy-start | bytes 2359300
  154.6 1.0 copy-start.5
  158.7 24.8 %copy-start.6 = (bf16[384,4,128]{2,1,0:T(4,128)(2,1)S(1)}, bf16[384,4,128]{2,1,0:T(4,128)(2,1)}, u32[]{:S(2)}) copy-start(bf16[384,4,128]{2,1,0:T(4,128)(2,1)} %param.8) | copy-start | bytes 1179652
  158.7 37.0 %collective-permute-start.11 = (bf16[1536,1536]{1,0:T(8,128)(2,1)}, bf16[1536,1536]{1,0:T(8,128)(2,1)}, u32[]{:S(2)}, u32[]{:S(2)}) collective-permute-start(bf16[1536,1536]{1,0:T(8,128)(2,1)} %get-tuple-element.66.refs_0_), channel_id=1, source_target_pairs={{0,1},{1,0},{2,3},{3,2},{4,5},{5,4},{6,7},{7,6},{8,9},{9,8},{10,11... | collective-permute-start | bytes 14155784 | tf_op jit(solution)/shard_map/ppermute | solution.py:651
  158.8 43.4 %collective-permute-start.12 = (bf16[1536,1536]{1,0:T(8,128)(2,1)}, bf16[1536,1536]{1,0:T(8,128)(2,1)}, u32[]{:S(2)}, u32[]{:S(2)}) collective-permute-start(bf16[1536,1536]{1,0:T(8,128)(2,1)} %get-tuple-element.67.refs_0_), channel_id=1, source_target_pairs={{0,1},{1,0},{2,3},{3,2},{4,5},{5,4},{6,7},{7,6},{8,9},{9,8},{10,11... | collective-permute-start | bytes 14155784 | tf_op jit(solution)/shard_map/ppermute | solution.py:651
  159.3 34.4 %copy-start.7 = (f32[384]{0:T(512)S(1)}, f32[384]{0:T(512)}, u32[]{:S(2)}) copy-start(f32[384]{0:T(512)} %param.14) | copy-start | bytes 4612
  159.4 9.1 %collective-permute-start.8 = (bf16[3,384,128]{2,1,0:T(8,128)(2,1)S(1)}, bf16[3,384,128]{2,1,0:T(8,128)(2,1)S(1)}, u32[]{:S(2)}, u32[]{:S(2)}) collective-permute-start(bf16[3,384,128]{2,1,0:T(8,128)(2,1)S(1)} %slice_select_fusion), channel_id=1, source_target_pairs={{0,2},{2,0},{1,3},{3,1},{4,6},{6,4},{5,7},{7,5},{8,10},{10,8},{9,1... | collective-permute-start | bytes 884744 | tf_op jit(solution)/shard_map/ppermute | solution.py:58
  160.8 13.9 %collective-permute-start.9 = (bf16[4,384,128]{2,1,0:T(8,128)(2,1)S(1)}, bf16[4,384,128]{2,1,0:T(8,128)(2,1)S(1)}, u32[]{:S(2)}, u32[]{:S(2)}) collective-permute-start(bf16[4,384,128]{2,1,0:T(8,128)(2,1)S(1)} %norm_gradient.1.block.gradient), channel_id=1, source_target_pairs={{0,1},{1,0},{2,3},{3,2},{4,5},{5,4},{6,7},{7,6},{8,9},{9,8},{10,11... | collective-permute-start | bytes 1179656 | tf_op jit(solution)/shard_map/ppermute | solution.py:68
  168.4 6.2 %collective-permute-start.10 = (bf16[3,384,128]{2,1,0:T(8,128)(2,1)S(1)}, bf16[3,384,128]{2,1,0:T(8,128)(2,1)S(1)}, u32[]{:S(2)}, u32[]{:S(2)}) collective-permute-start(bf16[3,384,128]{2,1,0:T(8,128)(2,1)S(1)} %collective-permute-done.8.above.below), channel_id=1, source_target_pairs={{0,1},{1,0},{2,3},{3,2},{4,5},{5,4},{6,7},{7,6},{8,9},{9,8},{10,11... | collective-permute-start | bytes 884744 | tf_op jit(solution)/shard_map/ppermute | solution.py:68
  180.4 1.6 collective-permute-start.13
  182.1 7.2 %collective-permute-start.14 = (f32[384,128]{1,0:T(8,128)S(1)}, f32[384,128]{1,0:T(8,128)S(1)}, u32[]{:S(2)}, u32[]{:S(2)}) collective-permute-start(f32[384,128]{1,0:T(8,128)S(1)} %add.12), channel_id=1, source_target_pairs={{0,2},{2,0},{1,3},{3,1},{4,6},{6,4},{5,7},{7,5},{8,10},{10,8},{9,1... | collective-permute-start | bytes 589832 | tf_op jit(solution)/shard_map/ppermute | solution.py:651
Sparse Core Ops, SparseCore 0:
  10.9 40.8 all-gather.6
  54.0 37.0 all-gather.4
  159.5 34.2 reduce-scatter.1

commit v3 on v2

--- a/solution.py
+++ b/solution.py
@@ -72,10 +72,12 @@
     return jnp.where(lane < width // 2, high, low)
 
 
-def surroundings(block):
+def surroundings(block, before_corner=None):
     rows = block.shape[0]
     above, below = from_sides(block[rows - HALF :], block[:HALF], "rows")
     side = edges(block, "cols")
+    if before_corner is not None:
+        above, below = after((above, below), before_corner)
     if lax.axis_size("rows") == 2:
         corner = edges(above, "cols")
         return block, above, below, side, corner, corner
@@ -319,29 +321,41 @@
     ]
 
 
-def gain_kernel(cot_all, gain, tails, sem):
+def cot_kernel(cot_all, w_reduce, bias, gain, wide_bias, back, matrix):
     count, padded, pixels = cot_all.shape
     channels = padded - PAD
-    copy = pltpu.make_async_copy(cot_all.at[:, channels:, :], tails, sem)
-    copy.start()
-    copy.wait()
-    ones = jnp.ones((PAD, gain.shape[1]), BF16)
-    for k in range(count):
-        gain[k * channels : (k + 1) * channels, :] = dot(tails[k], ones, COLS_BY_COLS)[:channels, :]
-
-
-def gain_stage(cot_all):
-    count, padded, pixels = cot_all.shape
-    return pl.pallas_call(
-        gain_kernel,
-        out_shape=shape((count * (padded - PAD), 128), F32),
-        in_specs=[anywhere],
-        out_specs=whole,
-        scratch_shapes=[pltpu.VMEM((count, PAD, pixels), BF16), pltpu.SemaphoreType.DMA],
+
+    @pl.when(pl.program_id(0) == 0)
+    def _():
+        ones = jnp.ones((PAD, gain.shape[1]), BF16)
+        wide_bias[...] = dot(stacked_rows(bias[...]), ones, COLS_BY_COLS)
+        for k in range(count):
+            cut = slice(k * channels, (k + 1) * channels)
+            matrix[cut, :] = cot_all[k, :channels, :]
+            gain[cut, :] = dot(cot_all[k, channels:, :], ones, COLS_BY_COLS)[:channels, :]
+
+    back[...] = dot(w_reduce[...], matrix[...], COLS_BY_COLS)
+
+
+def cot_stage(cot_all, w_reduce, bias):
+    pixels = cot_all.shape[2]
+    every, units = w_reduce.shape
+    tile = tile_of(units)
+    return pl.pallas_call(
+        cot_kernel,
+        grid=(units // tile,),
+        out_shape=(shape((every, 128), F32), shape((units, 128), F32), shape((units, pixels), F32)),
+        in_specs=[fixed(cot_all.shape), columns_of(every, tile), fixed((1, units))],
+        out_specs=(fixed((every, 128)), fixed((units, 128)), rows_of(tile, pixels)),
+        scratch_shapes=[pltpu.VMEM((every, pixels), BF16)],
         compiler_params=params(60),
         cost_estimate=LIGHT,
-        name="gains",
-    )(cot_all)
+        name="cotangent_stage",
+    )(cot_all, w_reduce, bias[None, :])
+
+
+def widened(values, pixels):
+    return jnp.concatenate([values] * (pixels // values.shape[1]), axis=1)
 
 
 def normalise(conv_all, gain, normed):
@@ -401,37 +415,28 @@
     )(conv_all, gain)
 
 
-def block_kernel(steps, normed, cot_all, gain, w_expand, bias, w_reduce, hidden, grad_pre, reduced, *refs):
-    blocks, (cot, reduce_sum, normed_sum) = refs[:-3], refs[-3:]
+def block_kernel(steps, normed, gain, w_expand, bias, back, hidden, grad_pre, *refs):
+    blocks, normed_sum = refs[:-1], refs[-1]
     at = pl.program_id(0)
 
     @pl.when(at == 0)
     def _():
-        channels = cot_all.shape[1] - PAD
-        for k in range(cot_all.shape[0]):
-            cot[k * channels : (k + 1) * channels, :] = cot_all[k, :channels, :]
-        reduce_sum[...] = jnp.zeros_like(reduce_sum)
         normed_sum[...] = jnp.zeros_like(normed_sum)
 
-    pre = dot(w_expand[...], normed[...], ROWS_BY_COLS) + bias[...]
-    back = dot(w_reduce[...], cot[...], COLS_BY_COLS)
+    pre = dot(w_expand[...], normed[...], ROWS_BY_COLS) + widened(bias[...], normed.shape[1])
     active, slope = gelu_parts(pre)
-    active = active.astype(BF16)
-    hidden[...] = active
-    grad = (back * slope).astype(BF16)
+    hidden[...] = active.astype(BF16)
+    grad = (back[...] * slope).astype(BF16)
     grad_pre[...] = grad
-    reduce_sum[...] += dot(w_reduce[...], active, ROWS_BY_COLS)
     normed_sum[...] += dot(w_expand[...], grad, COLS_BY_COLS)
 
     @pl.when(at == steps - 1)
     def _():
         every, pixels = normed.shape
-        reduced[...] = reduce_sum[...].astype(BF16)
-
         def step(index, totals):
             cut = pl.ds(pl.multiple_of(index * PAD, PAD), PAD)
             value = normed_sum[cut, :]
-            first = value * jnp.concatenate([gain[cut, :]] * (pixels // gain.shape[1]), axis=1)
+            first = value * widened(gain[cut, :], pixels)
             cross = value * normed[cut, :].astype(F32)
             return totals[0] + first[:8] + first[8:], totals[1] + cross[:8] + cross[8:]
 
@@ -444,7 +449,7 @@
             block[height:, :] = moments
 
 
-def block_stage(normed, cot_all, gain, w_expand, bias, w_reduce):
+def block_stage(normed, gain, w_expand, bias, back):
     count = lax.axis_size("chan")
     units, every = w_expand.shape
     pixels = normed.shape[1]
@@ -455,104 +460,116 @@
         functools.partial(block_kernel, steps),
         grid=(steps,),
         out_shape=(shape((units, pixels), BF16),) * 2
-        + (shape((every, pixels), BF16),)
         + (shape((every // blocks + PAD, pixels), BF16),) * blocks,
         in_specs=[
             fixed(normed.shape),
-            fixed(cot_all.shape),
             fixed(gain.shape),
             rows_of(tile, every),
-            rows_of(tile, 1),
+            rows_of(tile, 128),
+            rows_of(tile, pixels),
+        ],
+        out_specs=(rows_of(tile, pixels),) * 2 + (fixed((every // blocks + PAD, pixels)),) * blocks,
+        scratch_shapes=[pltpu.VMEM((every, pixels), F32)],
+        compiler_params=params(60),
+        cost_estimate=LIGHT,
+        name="pointwise_block",
+    )(normed, gain, w_expand, bias, back)
+
+
+def reduced_kernel(weight, hidden, result):
+    result[...] = dot(weight[...], hidden[...], ROWS_BY_COLS).astype(BF16)
+
+
+def reduce_product(w_reduce, hidden):
+    every, units = w_reduce.shape
+    pixels = hidden.shape[1]
+    tile = 512 if every % 512 == 0 else tile_of(every)
+    return pl.pallas_call(
+        reduced_kernel,
+        grid=(every // tile,),
+        out_shape=shape((every, pixels), BF16),
+        in_specs=[rows_of(tile, units), fixed(hidden.shape)],
+        out_specs=rows_of(tile, pixels),
+        compiler_params=params(60),
+        cost_estimate=LIGHT,
+        name="reduced_product",
+    )(w_reduce, hidden)
+
+
+def unpack(cot_all, target):
+    channels = cot_all.shape[1] - PAD
+    for k in range(cot_all.shape[0]):
+        target[k * channels : (k + 1) * channels, :] = cot_all[k, :channels, :]
+
+
+def own_tile_kernel(normed, cot_all, hidden, grad_pre, grad_reduce, grad_expand, cot):
+    @pl.when(pl.program_id(0) == 0)
+    def _():
+        unpack(cot_all, cot)
+
+    grad_reduce[...] = dot(cot[...], hidden[...], ROWS_BY_ROWS).astype(BF16)
+    grad_expand[...] = dot(grad_pre[...], normed[...], ROWS_BY_ROWS).astype(BF16)
+
+
+def own_tile_gradients(normed, cot_all, hidden, grad_pre):
+    every, pixels = normed.shape
+    units = hidden.shape[0]
+    tile = tile_of(units)
+    return pl.pallas_call(
+        own_tile_kernel,
+        grid=(units // tile,),
+        out_shape=(shape((every, units), BF16), shape((units, every), BF16)),
+        in_specs=[fixed(normed.shape), fixed(cot_all.shape), rows_of(tile, pixels), rows_of(tile, pixels)],
+        out_specs=(columns_of(every, tile), rows_of(tile, every)),
+        scratch_shapes=[pltpu.VMEM((every, pixels), BF16)],
+        compiler_params=params(60),
+        cost_estimate=LIGHT,
+        name="own_tile_gradients",
+    )(normed, cot_all, hidden, grad_pre)
+
+
+def plus(first, product):
+    return (first.astype(F32) + product.astype(BF16).astype(F32)).astype(BF16)
+
+
+def other_tile_kernel(
+    normed, cot_all, reduce_own, expand_own, w_expand, bias, w_reduce, grad_reduce, grad_expand, cot
+):
+    @pl.when(pl.program_id(0) == 0)
+    def _():
+        unpack(cot_all, cot)
+
+    pre = dot(w_expand[...], normed[...], ROWS_BY_COLS) + widened(bias[...], normed.shape[1])
+    back = dot(w_reduce[...], cot[...], COLS_BY_COLS)
+    active, slope = gelu_parts(pre)
+    grad_pre = (back * slope).astype(BF16)
+    grad_reduce[...] = plus(reduce_own[...], dot(cot[...], active.astype(BF16), ROWS_BY_ROWS))
+    grad_expand[...] = plus(expand_own[...], dot(grad_pre, normed[...], ROWS_BY_ROWS))
+
+
+def two_tile_gradients(normed, cot_all, reduce_own, expand_own, w_expand, bias, w_reduce):
+    every, pixels = normed.shape
+    units = w_expand.shape[0]
+    tile = tile_of(units)
+    return pl.pallas_call(
+        other_tile_kernel,
+        grid=(units // tile,),
+        out_shape=(shape((every, units), BF16), shape((units, every), BF16)),
+        in_specs=[
+            fixed(normed.shape),
+            fixed(cot_all.shape),
+            columns_of(every, tile),
+            rows_of(tile, every),
+            rows_of(tile, every),
+            rows_of(tile, 128),
             columns_of(every, tile),
         ],
-        out_specs=(rows_of(tile, pixels),) * 2
-        + (fixed((every, pixels)),)
-        + (fixed((every // blocks + PAD, pixels)),) * blocks,
-        scratch_shapes=[
-            pltpu.VMEM((every, pixels), BF16),
-            pltpu.VMEM((every, pixels), F32),
-            pltpu.VMEM((every, pixels), F32),
-        ],
+        out_specs=(columns_of(every, tile), rows_of(tile, every)),
+        scratch_shapes=[pltpu.VMEM((every, pixels), BF16)],
         compiler_params=params(60),
         cost_estimate=LIGHT,
-        name="pointwise_block",
-    )(normed, cot_all, gain, w_expand, bias, w_reduce)
-
-
-def side_by_side(pixels):
-    index = lax.axis_index("rows")
-    own = pl.ds(pl.multiple_of(index * pixels, pixels), pixels)
-    other = pl.ds(pl.multiple_of((1 - index) * pixels, pixels), pixels)
-    return own, other
-
-
-def weight_kernel(
-    normed_own, normed_other, cot_own, cot_other, hidden_own, pre_own, w_expand, bias, w_reduce,
-    grad_reduce, grad_expand, normed, cot, hidden, grad_pre, sems,
-):
-    pixels = normed_own.shape[1]
-    own, other = side_by_side(pixels)
-
-    @pl.when(pl.program_id(0) == 0)
-    def _():
-        copies = [
-            pltpu.make_async_copy(normed_other, normed.at[:, other], sems.at[0]),
-            pltpu.make_async_copy(normed_own, normed.at[:, own], sems.at[1]),
-        ]
-        count, padded, _ = cot_own.shape
-        channels = padded - PAD
-        for k in range(count):
-            rows = slice(k * channels, (k + 1) * channels)
-            for x, (source, cut) in enumerate(((cot_own, own), (cot_other, other))):
-                copies.append(
-                    pltpu.make_async_copy(source.at[k, :channels, :], cot.at[rows, cut], sems.at[2 + 2 * k + x])
-                )
-        for copy in copies:
-            copy.start()
-        for copy in copies:
-            copy.wait()
-
-    pre = dot(w_expand[...], normed[:, other], ROWS_BY_COLS) + bias[...]
-    back = dot(w_reduce[...], cot[:, other], COLS_BY_COLS)
-    active, slope = gelu_parts(pre)
-    hidden[:, own] = hidden_own[...]
-    hidden[:, other] = active.astype(BF16)
-    grad_pre[:, own] = pre_own[...]
-    grad_pre[:, other] = (back * slope).astype(BF16)
-    grad_reduce[...] = dot(cot[...], hidden[...], ROWS_BY_ROWS).astype(BF16)
-    grad_expand[...] = dot(grad_pre[...], normed[...], ROWS_BY_ROWS).astype(BF16)
-
-
-def weight_gradients(part, parts, normed_own, normed_other, cot_own, cot_other, hidden, grad_pre, w_expand, bias, w_reduce):
-    every, pixels = normed_own.shape
-    units = w_expand.shape[0]
-    tile = tile_of(units)
-    steps = units // tile // parts
-    first = part * steps
-    return pl.pallas_call(
-        weight_kernel,
-        grid=(steps,),
-        out_shape=(shape((every, steps * tile), BF16), shape((steps * tile, every), BF16)),
-        in_specs=[anywhere] * 4
-        + [
-            rows_of(tile, pixels, first),
-            rows_of(tile, pixels, first),
-            rows_of(tile, every, first),
-            rows_of(tile, 1, first),
-            columns_of(every, tile, first),
-        ],
-        out_specs=(columns_of(every, tile), rows_of(tile, every)),
-        scratch_shapes=[
-            pltpu.VMEM((every, 2 * pixels), BF16),
-            pltpu.VMEM((every, 2 * pixels), BF16),
-            pltpu.VMEM((tile, 2 * pixels), BF16),
-            pltpu.VMEM((tile, 2 * pixels), BF16),
-            pltpu.SemaphoreType.DMA((2 + 2 * cot_own.shape[0],)),
-        ],
-        compiler_params=params(60),
-        cost_estimate=LIGHT,
-        name="weight_gradients",
-    )(normed_own, normed_other, cot_own, cot_other, hidden, grad_pre, w_expand, bias, w_reduce)
+        name="two_tile_gradients",
+    )(normed, cot_all, reduce_own, expand_own, w_expand, bias, w_reduce)
 
 
 def pair_kernel(*refs):
@@ -597,6 +614,7 @@
         cross = cross + unstacked(tail, 1)
     first, cross = first / every, cross / every
     shift = local[0:1, :] - mean
+    own = lax.axis_index("chan") * channels
 
     def step(index, carry):
         at = pl.multiple_of(index * PAD, PAD)
@@ -605,7 +623,7 @@
         value = blocks[0][cut, :].astype(F32)
         for block in blocks[1:]:
             value = value + block[cut, :].astype(F32)
-        value = value * gain[cut, :]
+        value = value * widened(gain[pl.ds(pl.multiple_of(own + at, PAD), PAD), :], value.shape[1])
         value = ((value - first - hat * cross) * deviation).astype(BF16)
         for k in range(rows):
             result[k, cut] = value[:, k * width : (k + 1) * width]
@@ -665,38 +683,40 @@
     packed_cot = pack_cotangent(cot_rows, layer_scale[:, None], layer_norm_weight[None, :])
     cot_all = lax.all_gather(packed_cot, "chan")
 
-    bias = bias_expand[:, None]
     packed_conv, centered, local = forward_conv(around, kernel)
     conv_all = lax.all_gather(packed_conv, "chan")
-    cot_all = after(cot_all, packed_conv)
-    gain = gain_stage(cot_all)
+    cot_all, bias = after((cot_all, bias_expand), packed_conv)
+    gain, bias, back = cot_stage(cot_all, w_reduce, bias)
     normed, stats = norm_stage(conv_all, gain)
     ready = normed
     if two_tiles:
         cot_other = swap(cot_all, "rows")
         normed_other = swap(normed, "rows")
         ready = after(normed, cot_other)
-    hidden, grad_pre, reduced, *blocks = block_stage(ready, cot_all, gain, w_expand, bias, w_reduce)
+    hidden, grad_pre, *blocks = block_stage(ready, gain, w_expand, bias, back)
     norm_inputs = (scattered(blocks), centered, local, stats)
+    product = reduce_product(w_reduce, hidden)
+    reduced = lax.psum_scatter(product, "chan", scatter_dimension=0, tiled=True)
 
     if two_tiles:
-        weight_inputs = (normed, normed_other, cot_all, cot_other, hidden, grad_pre, w_expand, bias, w_reduce)
-        found = weight_gradients(0, 1, *weight_inputs)
+        own = own_tile_gradients(normed, cot_all, after(hidden, product), grad_pre)
+        found = two_tile_gradients(normed_other, cot_other, *own, w_expand, bias, w_reduce)
         norm_inputs = after(norm_inputs, found)
-    reduced = lax.psum_scatter(reduced, "chan", scatter_dimension=0, tiled=True).astype(F32)
-    gradient = norm_gradient(every, image_rows.shape, *norm_inputs, layer_norm_weight[:, None])
-    grad_around = surroundings(gradient)
+    gradient = norm_gradient(every, image_rows.shape, *norm_inputs, gain)
     taps = kernel_gradient(around, gradient)
+    grad_around = surroundings(gradient, taps if two_tiles else None)
     if two_tiles:
-        grad_around = after(grad_around, reduced)
+        theirs = [swap(after(mine, gradient), "cols") for mine in found]
+        grad_reduce = add_pair(0, 1, 0, found[0], theirs[0], None)
+        grad_around = after(grad_around, grad_reduce)
     grad_rows = backward_conv(grad_around, kernel, cot_rows)
     grad_input = jnp.transpose(grad_rows, (1, 0, 2))
     if two_tiles:
         taps = after(taps, grad_rows)
         taps = taps + swap(taps, "cols")
         taps = taps + swap(taps, "rows")
-        theirs = [swap(after(mine, gradient), "cols") for mine in found]
-        grad_reduce, grad_expand = [add_pair(0, 1, 0, *pair, None) for pair in zip(found, theirs)]
+        grad_expand = add_pair(0, 1, 0, found[1], theirs[1], None)
+        reduced = after(reduced, grad_expand, taps)
     else:
         taps = lax.psum(taps, ("rows", "cols"))
         cot = cot_all[:, :channels, :].reshape(every, pixels)
@@ -706,7 +726,7 @@
     taps = taps[:, : KS * KS]
 
     output = (
-        image.reshape(channels, pixels).astype(F32) + layer_scale[:, None] * reduced
+        image.reshape(channels, pixels).astype(F32) + layer_scale[:, None] * reduced.astype(F32)
     ).astype(BF16).reshape(image.shape)
     return output, grad_input, grad_expand, grad_reduce, taps
 

time: 216 us -> 198 us (0.917)
  waiting for transfers between devices: 92 us -> 62.5 us
  Pallas kernels: 79.8 us -> 91.1 us
    pallas_call x2 -> x4, Pallas kernels: 25.3 us -> 42.2 us  [the longest x1 17.2 us: two_tile_gradients(): pl.pallas_call(other_tile_kernel, grid=(units // tile,), out_shape=(shape...]
    ppermute x6, waiting for transfers between devices: 16.8 us -> 1.79 us  [swap(): return lax.ppermute(values, axis, [(0, 1), (1, 0)])]
    all_gather x1, waiting for transfers between devices: 35.6 us -> 28.8 us  [on_device(): conv_all = lax.all_gather(packed_conv, 'chan')]
    ppermute x2, waiting for transfers between devices: 14.6 us -> 8.28 us  [from_sides(): got = lax.ppermute(sent, axis, [(0, 1), (1, 0)])]
    pallas_call x1, Pallas kernels: 17.4 us -> 13.1 us  [block_stage(): pl.pallas_call(functools.partial(block_kernel, steps), grid=(steps,), out...]
    unnamed x23 -> x29, local copies, waits for them, and re-layouts: 9.42 us -> 10.2 us
  transfers between devices with their start and end apart: 18 -> 18, of which waited for: 9 -> 8; matrix products, arithmetic and copies ran while one was open for 4% -> 2% of each run, Pallas kernels for 32% -> 45%
where the time goes in v3:
time: 198 us; the launch traced here: 197 us
  Pallas kernels  91.1 us (46%)
  waiting for transfers between devices  62.5 us (32%)
  starting transfers between devices  14.5 us (7%)
  between operations  14 us (7%)
  local copies, waits for them, and re-layouts  13.1 us (7%)
    all_gather x1, waiting for transfers between devices, on_device(): conv_all = lax.all_gather(packed_conv, 'chan')  28.8 us
    all_gather x1, waiting for transfers between devices, on_device(): cot_all = lax.all_gather(packed_cot, 'chan')  20.6 us
    pallas_call x1, Pallas kernels, two_tile_gradients(): pl.pallas_call(other_tile_kernel, grid=(units // tile,), out_shape=(shape...  17.2 us
    pallas_call x1, Pallas kernels, block_stage(): pl.pallas_call(functools.partial(block_kernel, steps), grid=(steps,), out...  13.1 us
    pallas_call x2, Pallas kernels, add_pair(): pl.pallas_call(pair_kernel, grid=(steps,), out_shape=shape(dims, BF16), i...  13 us
    pallas_call x1, Pallas kernels, own_tile_gradients(): pl.pallas_call(own_tile_kernel, grid=(units // tile,), out_shape=(shape((...  10.4 us
    unnamed x29, local copies, waits for them, and re-layouts  10.2 us
    ppermute x2, waiting for transfers between devices, from_sides(): got = lax.ppermute(sent, axis, [(0, 1), (1, 0)])  8.28 us
  transfers between devices with their start and end apart: 18, of which 8 were waited for; matrix products, arithmetic and copies ran while one was open for 2% of the time, Pallas kernels for 45%

profile of v3, /device:TPU:0, one launch (start us, length us, event | category | flops | bytes accessed | tf_op | source)
XLA Modules:
  0.0 196.6 jit_solution(6789486046161953649)
XLA Ops:
  7.2 0.0 all-gather.7.cloned.1.call-start
  7.2 0.7 broadcast_in_dim.11.gain
  7.9 0.8 broadcast_in_dim.13.scale
  8.7 1.1 copy.30
  9.8 1.0 pack_cotangent.1
  10.8 0.0 all-gather.7.cloned.1.call-update
  10.8 0.0 all-gather.5.cloned.1.call-start
  10.9 1.1 copy.31
  12.0 3.0 %collective-permute-start = (bf16[3,384,128]{2,1,0:T(8,128)(2,1)S(1)}, bf16[3,384,128]{2,1,0:T(8,128)(2,1)S(1)}, u32[]{:S(2)}, u32[]{:S(2)}) collective-permute-start(bf16[3,384,128]{2,1,0:T(8,128)(2,1)S(1)} %slice_select_fusion.1), channel_id=1, source_target_pairs={{0,2},{2,0},{1,3},{3,1},{4,6},{6,4},{5,7},{7,5},{8,10},{10,8},{9,1... | collective-permute-start | bytes 884744 | tf_op jit(solution)/shard_map/ppermute | solution.py:58
  15.0 0.0 collective-permute-start.1
  15.0 7.0 %collective-permute-done.above.below = bf16[3,384,128]{2,1,0:T(8,128)(2,1)S(1)} collective-permute-done((bf16[3,384,128]{2,1,0:T(8,128)(2,1)S(1)}, bf16[3,384,128]{2,1,0:T(8,128)(2,1)S(1)}, u32[]{:S(2)}, u32[]{:S(2)}) %collective-permute-start) | collective-permute-done | bytes 294944 | tf_op jit(solution)/shard_map/ppermute | solution.py:58
  22.0 0.0 collective-permute-start.2
  22.0 1.0 copy.20.kernel
  23.0 0.0 collective-permute-done.1.side
  23.0 0.5 collective-permute-done.2.above_side.below_side
  23.6 6.6 %conv_forward.1 = (bf16[400,512]{1,0:T(8,128)(2,1)}, f32[384,512]{1,0:T(8,128)S(1)}, f32[8,512]{1,0:T(8,128)S(1)}) custom-call(bf16[4,384,128]{2,1,0:T(8,128)(2,1)S(1)} %bitcast.18, bf16[3,384,128]{2,1,0:T(8,128)(2,1)S(1)} %collective-permute-done.above.below, bf16[3,384,128]{2,1,0:T(8,128)(2,1)S(1)} %collective-permute-done.above.below, ...), custom_call_target="tpu_custom_call" | custom-call | flops 1000 | bytes 1000 | tf_op jit(solution)/shard_map/conv_forward/pallas_call | solution.py:174
  30.2 0.9 copy-done.4
  31.1 0.0 all-gather.5.cloned.1.call-update
  31.1 0.0 reduce-scatter.2.cloned.1.call-start
  31.2 20.6 %all-gather.7.cloned.1.call-done = bf16[1600,512]{1,0:T(8,128)(2,1)} async-done(((bf16[400,512]{1,0:T(8,128)(2,1)}), bf16[1600,512]{1,0:T(8,128)(2,1)}) %all-gather.7.cloned.1.call-update) | async-done | bytes 1638416 | tf_op jit(solution)/shard_map/all_gather | solution.py:684
  51.8 1.5 collective-permute-start.3
  53.3 0.6 broadcast_in_dim.12.bias
  53.9 8.3 %cotangent_stage.1 = (f32[1536,128]{1,0:T(8,128)}, f32[1536,128]{1,0:T(8,128)}, f32[1536,512]{1,0:T(8,128)}) custom-call(bf16[4,400,512]{2,1,0:T(8,128)(2,1)} %bitcast.25, bf16[1536,1536]{1,0:T(8,128)(2,1)} %w_reduce.3, f32[1,1536]{1,0:T(1,128)} %broadcast_in_dim.12.bias), custom_call_target="tpu_custom_call" | custom-call | flops 1000 | bytes 1000 | tf_op jit(solution)/shard_map/cotangent_stage/pallas_call | solution.py:344
  62.2 28.8 %all-gather.5.cloned.1.call-done = bf16[1600,512]{1,0:T(8,128)(2,1)} async-done(((bf16[400,512]{1,0:T(8,128)(2,1)}), bf16[1600,512]{1,0:T(8,128)(2,1)}) %all-gather.5.cloned.1.call-update) | async-done | bytes 1638416 | tf_op jit(solution)/shard_map/all_gather | solution.py:687
  91.0 1.1 copy-done
  92.2 1.4 copy-done.3
  93.6 1.5 norm.1
  95.1 0.0 copy-start.7
  95.1 0.6 copy-done.7
  95.7 1.5 collective-permute-start.4
  97.2 0.0 collective-permute-done.3.cot_all
  97.2 13.1 %pointwise_block.1 = (bf16[1536,512]{1,0:T(8,128)(2,1)}, bf16[1536,512]{1,0:T(8,128)(2,1)}, bf16[400,512]{1,0:T(8,128)(2,1)}, bf16[400,512]{1,0:T(8,128)(2,1)}, ...) custom-call(bf16[1536,512]{1,0:T(8,128)(2,1)} %copy-done.2, f32[1536,128]{1,0:T(8,128)} %get-tuple-element.49.gain, ...), custom_call_target="tpu_custom_call" | custom-call | flops 1000 | bytes 1000 | tf_op jit(solution)/shard_map/pointwise_block/pallas_call | solution.py:459
  110.3 0.5 collective-permute-start.5
  110.7 1.4 collective-permute-start.6
  112.1 2.4 %collective-permute-start.7 = (bf16[400,512]{1,0:T(8,128)(2,1)}, bf16[400,512]{1,0:T(8,128)(2,1)}, u32[]{:S(2)}, u32[]{:S(2)}) collective-permute-start(bf16[400,512]{1,0:T(8,128)(2,1)} %get-tuple-element.63), channel_id=1, source_target_pairs={{0,12},{4,0},{8,4},{12,8},{1,13},{5,1},{9,5},{13,9},{2,14},{6,2},{... | collective-permute-start | bytes 1228808 | tf_op jit(solution)/shard_map/ppermute | solution.py:659
  114.5 6.2 %reduced_product.1 = bf16[1536,512]{1,0:T(8,128)(2,1)} custom-call(bf16[1536,1536]{1,0:T(8,128)(2,1)} %w_reduce.3, bf16[1536,512]{1,0:T(8,128)(2,1)} %get-tuple-element.55.hidden), custom_call_target="tpu_custom_call" | custom-call | flops 1000 | bytes 1000 | tf_op jit(solution)/shard_map/reduced_product/pallas_call | solution.py:487
  120.7 10.4 %own_tile_gradients.1 = (bf16[1536,1536]{1,0:T(8,128)(2,1)}, bf16[1536,1536]{1,0:T(8,128)(2,1)}) custom-call(bf16[1536,512]{1,0:T(8,128)(2,1)} %copy-done.2, bf16[4,400,512]{2,1,0:T(8,128)(2,1)} %bitcast.26, bf16[1536,512]{1,0:T(8,128)(2,1)} %get-tuple-element.55.hidden, bf16[1536,512]{1,0:T(8,128)(2,1)} %get-tuple-element.56.grad_pre), custom_call_target="tpu_custom_call" | custom-call | flops 1000 | bytes 1000 | tf_op jit(solution)/shard_map/own_tile_gradients/pallas_call | solution.py:518
  131.2 0.7 collective-permute-done.4.normed
  131.9 17.2 %two_tile_gradients.1 = (bf16[1536,1536]{1,0:T(8,128)(2,1)}, bf16[1536,1536]{1,0:T(8,128)(2,1)}) custom-call(bf16[1536,512]{1,0:T(8,128)(2,1)} %collective-permute-done.4.normed, bf16[4,400,512]{2,1,0:T(8,128)(2,1)} %collective-permute-done.3.cot_all, bf16[1536,1536]{1,0:T(8,128)(2,1)} %get-tuple-element.57.reduce_own, ...), custom_call_target="tpu_custom_call" | custom-call | flops 1000 | bytes 1000 | tf_op jit(solution)/shard_map/two_tile_gradients/pallas_call | solution.py:554
  149.1 0.0 collective-permute-done.6.refs_2_
  149.2 1.1 copy-done.5
  150.3 1.9 norm_gradient.1.gradient.block
  152.1 0.1 collective-permute-start.12
  152.2 0.5 collective-permute-start.8
  152.7 0.0 reduce-scatter.2.cloned.1.call-update
  152.8 1.5 collective-permute-start.9
  154.3 0.0 collective-permute-start.10
  154.3 6.2 %kernel_gradient.1 = f32[384,128]{1,0:T(8,128)S(1)} custom-call(bf16[4,384,128]{2,1,0:T(8,128)(2,1)S(1)} %bitcast.19, bf16[3,384,128]{2,1,0:T(8,128)(2,1)S(1)} %collective-permute-done.above.below, bf16[3,384,128]{2,1,0:T(8,128)(2,1)S(1)} %collective-permute-done.above.below, bf16[4,384,128]{2,1,0:T(8,128)(2,1)S(1)} %collective-permute-done.1.side, ...), custom_call_target="tpu_custom_call" | custom-call | flops 1000 | bytes 1000 | tf_op jit(solution)/shard_map/kernel_gradient/pallas_call | solution.py:248
  160.6 0.0 copy-start.9
  160.6 1.3 collective-permute-done.9.above.below
  161.8 0.0 collective-permute-start.11
  161.8 6.5 %add_pair.3 = bf16[1536,1536]{1,0:T(8,128)(2,1)} custom-call(bf16[1536,1536]{1,0:T(8,128)(2,1)} %get-tuple-element.78.refs_0_, bf16[1536,1536]{1,0:T(8,128)(2,1)} %collective-permute-done.12.refs_1_), custom_call_target="tpu_custom_call" | custom-call | flops 1000 | bytes 1000 | tf_op jit(solution)/shard_map/add_pair/pallas_call | solution.py:593
  168.3 5.7 %conv_backward.1 = bf16[4,384,128]{2,1,0:T(8,128)(2,1)S(1)} custom-call(bf16[4,384,128]{2,1,0:T(8,128)(2,1)S(1)} %norm_gradient.1.gradient.block, bf16[3,384,128]{2,1,0:T(8,128)(2,1)S(1)} %collective-permute-done.9.above.below, bf16[3,384,128]{2,1,0:T(8,128)(2,1)S(1)} %collective-permute-done.9.above.below, ...), custom_call_target="tpu_custom_call" | custom-call | flops 1000 | bytes 1000 | tf_op jit(solution)/shard_map/conv_backward/pallas_call | solution.py:206
  174.1 0.6 collective-permute-start.13
  174.6 1.1 collective-permute-done.13
  175.7 1.5 collective-permute-start.14
  177.3 0.1 convert.1
  177.4 0.0 copy-start.10
  177.4 6.5 %add_pair.2 = bf16[1536,1536]{1,0:T(8,128)(2,1)} custom-call(bf16[1536,1536]{1,0:T(8,128)(2,1)} %get-tuple-element.75.refs_0_, bf16[1536,1536]{1,0:T(8,128)(2,1)} %collective-permute-done.8.refs_1_), custom_call_target="tpu_custom_call" | custom-call | flops 1000 | bytes 1000 | tf_op jit(solution)/shard_map/add_pair/pallas_call | solution.py:593
  183.9 1.1 copy.24
  185.0 2.3 %reduce-scatter.2.cloned.1.call-done = bf16[384,512]{1,0:T(8,128)(2,1)} async-done(((bf16[1536,512]{1,0:T(8,128)(2,1)}), bf16[384,512]{1,0:T(8,128)(2,1)}) %reduce-scatter.2.cloned.1.call-update) | async-done | bytes 393232 | tf_op jit(solution)/shard_map/reduce_scatter | solution.py:699
  187.3 1.1 fusion
  188.4 0.8 reshape.17
  189.3 0.8 copy.25
  (27 shorter events, 0.1 us)
Async XLA Ops:
  7.2 46.1 %copy-start.11 = (f32[1536]{0:T(1024)S(1)}, f32[1536]{0:T(1024)}, u32[]{:S(2)}) copy-start(f32[1536]{0:T(1024)} %param.12) | copy-start | bytes 18436
  7.2 44.7 %all-gather.7.cloned.1.call-start = ((), (), s32[]{:S(2)}) async-start(), calls=%async_computation.3 | async-start | bytes 2048000 | tf_op jit(solution)/shard_map/all_gather | solution.py:684
  10.8 80.2 %all-gather.5.cloned.1.call-start = ((), (), s32[]{:S(2)}) async-start(), calls=%async_computation.2 | async-start | bytes 2048000 | tf_op jit(solution)/shard_map/all_gather | solution.py:687
  12.0 10.0 %collective-permute-start = (bf16[3,384,128]{2,1,0:T(8,128)(2,1)S(1)}, bf16[3,384,128]{2,1,0:T(8,128)(2,1)S(1)}, u32[]{:S(2)}, u32[]{:S(2)}) collective-permute-start(bf16[3,384,128]{2,1,0:T(8,128)(2,1)S(1)} %slice_select_fusion.1), channel_id=1, source_target_pairs={{0,2},{2,0},{1,3},{3,1},{4,6},{6,4},{5,7},{7,5},{8,10},{10,8},{9,1... | collective-permute-start | bytes 884744 | tf_op jit(solution)/shard_map/ppermute | solution.py:58
  15.0 8.0 %collective-permute-start.1 = (bf16[4,384,128]{2,1,0:T(8,128)(2,1)S(1)}, bf16[4,384,128]{2,1,0:T(8,128)(2,1)S(1)}, u32[]{:S(2)}, u32[]{:S(2)}) collective-permute-start(bf16[4,384,128]{2,1,0:T(8,128)(2,1)S(1)} %bitcast.17), channel_id=1, source_target_pairs={{0,1},{1,0},{2,3},{3,2},{4,5},{5,4},{6,7},{7,6},{8,9},{9,8},{10,11... | collective-permute-start | bytes 1179656 | tf_op jit(solution)/shard_map/ppermute | solution.py:68
  22.0 1.6 collective-permute-start.2
  30.2 0.9 copy-start.4
  31.1 156.1 %reduce-scatter.2.cloned.1.call-start = ((), (), s32[]{:S(2)}) async-start(), calls=%async_computation.1 | async-start | bytes 1966080 | tf_op jit(solution)/shard_map/reduce_scatter | solution.py:699
  51.8 45.3 %collective-permute-start.3 = (bf16[4,400,512]{2,1,0:T(8,128)(2,1)}, bf16[4,400,512]{2,1,0:T(8,128)(2,1)}, u32[]{:S(2)}, u32[]{:S(2)}) collective-permute-start(bf16[4,400,512]{2,1,0:T(8,128)(2,1)} %bitcast.24), channel_id=1, source_target_pairs={{0,2},{2,0},{1,3},{3,1},{4,6},{6,4},{5,7},{7,5},{8,10},{10,8},{9,1... | collective-permute-start | bytes 4915208 | tf_op jit(solution)/shard_map/ppermute | solution.py:669
  91.0 1.1 copy-start
  92.2 1.4 copy-start.3
  95.1 0.6 copy-start.7
  95.7 1.5 copy-start.2
  95.7 36.2 %collective-permute-start.4 = (bf16[1536,512]{1,0:T(8,128)(2,1)S(1)}, bf16[1536,512]{1,0:T(8,128)(2,1)}, u32[]{:S(2)}, u32[]{:S(2)}) collective-permute-start(bf16[1536,512]{1,0:T(8,128)(2,1)S(1)} %get-tuple-element.51.normed), channel_id=1, source_target_pairs={{0,2},{2,0},{1,3},{3,1},{4,6},{6,4},{5,7},{7,5},{8,10},{10,8},{9,1... | collective-permute-start | bytes 4718600 | tf_op jit(solution)/shard_map/ppermute | solution.py:669
  110.3 38.8 %collective-permute-start.5 = (bf16[400,512]{1,0:T(8,128)(2,1)}, bf16[400,512]{1,0:T(8,128)(2,1)}, u32[]{:S(2)}, u32[]{:S(2)}) collective-permute-start(bf16[400,512]{1,0:T(8,128)(2,1)} %get-tuple-element.61), channel_id=1, source_target_pairs={{0,4},{4,8},{8,12},{12,0},{1,5},{5,9},{9,13},{13,1},{2,6},{6,10},{... | collective-permute-start | bytes 1228808 | tf_op jit(solution)/shard_map/ppermute | solution.py:659
  110.7 38.4 %collective-permute-start.6 = (bf16[400,512]{1,0:T(8,128)(2,1)}, bf16[400,512]{1,0:T(8,128)(2,1)}, u32[]{:S(2)}, u32[]{:S(2)}) collective-permute-start(bf16[400,512]{1,0:T(8,128)(2,1)} %get-tuple-element.62), channel_id=1, source_target_pairs={{0,8},{4,12},{8,0},{12,4},{1,9},{5,13},{9,1},{13,5},{2,10},{6,14},... | collective-permute-start | bytes 1228808 | tf_op jit(solution)/shard_map/ppermute | solution.py:659
  112.1 37.0 %collective-permute-start.7 = (bf16[400,512]{1,0:T(8,128)(2,1)}, bf16[400,512]{1,0:T(8,128)(2,1)}, u32[]{:S(2)}, u32[]{:S(2)}) collective-permute-start(bf16[400,512]{1,0:T(8,128)(2,1)} %get-tuple-element.63), channel_id=1, source_target_pairs={{0,12},{4,0},{8,4},{12,8},{1,13},{5,1},{9,5},{13,9},{2,14},{6,2},{... | collective-permute-start | bytes 1228808 | tf_op jit(solution)/shard_map/ppermute | solution.py:659
  131.9 17.2 %copy-start.1 = (f32[1536,128]{1,0:T(8,128)S(1)}, f32[1536,128]{1,0:T(8,128)}, u32[]{:S(2)}) copy-start(f32[1536,128]{1,0:T(8,128)} %get-tuple-element.49.gain) | copy-start | bytes 2359300
  131.9 17.3 %copy-start.6 = (bf16[400,512]{1,0:T(8,128)(2,1)S(1)}, bf16[400,512]{1,0:T(8,128)(2,1)}, u32[]{:S(2)}) copy-start(bf16[400,512]{1,0:T(8,128)(2,1)} %get-tuple-element.71.refs_0_) | copy-start | bytes 1228804
  131.9 17.3 %copy-start.8 = (f32[8,512]{1,0:T(8,128)S(1)}, f32[8,512]{1,0:T(8,128)}, u32[]{:S(2)}) copy-start(f32[8,512]{1,0:T(8,128)} %copy-done.7) | copy-start | bytes 49156
  149.2 1.1 copy-start.5
  152.1 9.7 %collective-permute-start.12 = (bf16[1536,1536]{1,0:T(8,128)(2,1)}, bf16[1536,1536]{1,0:T(8,128)(2,1)}, u32[]{:S(2)}, u32[]{:S(2)}) collective-permute-start(bf16[1536,1536]{1,0:T(8,128)(2,1)} %get-tuple-element.78.refs_0_), channel_id=1, source_target_pairs={{0,1},{1,0},{2,3},{3,2},{4,5},{5,4},{6,7},{7,6},{8,9},{9,8},{10,11... | collective-permute-start | bytes 14155784 | tf_op jit(solution)/shard_map/ppermute | solution.py:669
  152.2 25.2 %collective-permute-start.8 = (bf16[1536,1536]{1,0:T(8,128)(2,1)}, bf16[1536,1536]{1,0:T(8,128)(2,1)}, u32[]{:S(2)}, u32[]{:S(2)}) collective-permute-start(bf16[1536,1536]{1,0:T(8,128)(2,1)} %get-tuple-element.75.refs_0_), channel_id=1, source_target_pairs={{0,1},{1,0},{2,3},{3,2},{4,5},{5,4},{6,7},{7,6},{8,9},{9,8},{10,11... | collective-permute-start | bytes 14155784 | tf_op jit(solution)/shard_map/ppermute | solution.py:669
  152.8 9.1 %collective-permute-start.9 = (bf16[3,384,128]{2,1,0:T(8,128)(2,1)S(1)}, bf16[3,384,128]{2,1,0:T(8,128)(2,1)S(1)}, u32[]{:S(2)}, u32[]{:S(2)}) collective-permute-start(bf16[3,384,128]{2,1,0:T(8,128)(2,1)S(1)} %slice_select_fusion), channel_id=1, source_target_pairs={{0,2},{2,0},{1,3},{3,1},{4,6},{6,4},{5,7},{7,5},{8,10},{10,8},{9,1... | collective-permute-start | bytes 884744 | tf_op jit(solution)/shard_map/ppermute | solution.py:58
  154.3 14.0 %collective-permute-start.10 = (bf16[4,384,128]{2,1,0:T(8,128)(2,1)S(1)}, bf16[4,384,128]{2,1,0:T(8,128)(2,1)S(1)}, u32[]{:S(2)}, u32[]{:S(2)}) collective-permute-start(bf16[4,384,128]{2,1,0:T(8,128)(2,1)S(1)} %norm_gradient.1.gradient.block), channel_id=1, source_target_pairs={{0,1},{1,0},{2,3},{3,2},{4,5},{5,4},{6,7},{7,6},{8,9},{9,8},{10,11... | collective-permute-start | bytes 1179656 | tf_op jit(solution)/shard_map/ppermute | solution.py:68
  160.6 16.7 %copy-start.9 = (bf16[384,4,128]{2,1,0:T(4,128)(2,1)S(1)}, bf16[384,4,128]{2,1,0:T(4,128)(2,1)}, u32[]{:S(2)}) copy-start(bf16[384,4,128]{2,1,0:T(4,128)(2,1)} %param.8) | copy-start | bytes 1179652
  161.8 6.5 %collective-permute-start.11 = (bf16[3,384,128]{2,1,0:T(8,128)(2,1)S(1)}, bf16[3,384,128]{2,1,0:T(8,128)(2,1)S(1)}, u32[]{:S(2)}, u32[]{:S(2)}) collective-permute-start(bf16[3,384,128]{2,1,0:T(8,128)(2,1)S(1)} %collective-permute-done.9.above.below), channel_id=1, source_target_pairs={{0,1},{1,0},{2,3},{3,2},{4,5},{5,4},{6,7},{7,6},{8,9},{9,8},{10,11... | collective-permute-start | bytes 884744 | tf_op jit(solution)/shard_map/ppermute | solution.py:68
  174.1 1.7 collective-permute-start.13
  175.7 9.2 %collective-permute-start.14 = (f32[384,128]{1,0:T(8,128)S(1)}, f32[384,128]{1,0:T(8,128)S(1)}, u32[]{:S(2)}, u32[]{:S(2)}) collective-permute-start(f32[384,128]{1,0:T(8,128)S(1)} %add.11), channel_id=1, source_target_pairs={{0,2},{2,0},{1,3},{3,1},{4,6},{6,4},{5,7},{7,5},{8,10},{10,8},{9,1... | collective-permute-start | bytes 589832 | tf_op jit(solution)/shard_map/ppermute | solution.py:669
  177.4 9.9 %copy-start.10 = (f32[384]{0:T(512)S(1)}, f32[384]{0:T(512)}, u32[]{:S(2)}) copy-start(f32[384]{0:T(512)} %param.14) | copy-start | bytes 4612
Sparse Core Ops, SparseCore 0:
  10.9 40.8 all-gather.6
  54.0 37.0 all-gather.4
  152.9 34.3 reduce-scatter.1

commit v4 on v3

--- a/solution.py
+++ b/solution.py
@@ -257,24 +257,24 @@
     )(*around, gradient)
 
 
-def pack_kernel(cotangent, scale, gain, packed):
+def pack_kernel(cotangent, scale, gain, packed, gain_rows):
     rows, channels, width = cotangent.shape
+    ones = jnp.ones((PAD, width), BF16)
+    wide = dot(stacked_rows(scale[...].reshape(1, channels)), ones, COLS_BY_COLS)
     for k in range(rows):
-        packed[:channels, k * width : (k + 1) * width] = (
-            cotangent[k].astype(F32) * scale[...]
-        ).astype(BF16)
-    packed[channels:, :] = jnp.zeros((PAD, rows * width), BF16)
-    packed[channels:, :channels] = stacked_rows(gain[...])
+        packed[:, k * width : (k + 1) * width] = (cotangent[k].astype(F32) * wide).astype(BF16)
+    gain_rows[...] = stacked_rows(gain[...].reshape(1, channels))
 
 
 def pack_cotangent(cotangent, scale, gain):
     rows, channels, width = cotangent.shape
     return pl.pallas_call(
         pack_kernel,
-        out_shape=shape((channels + PAD, rows * width), BF16),
+        out_shape=(shape((channels, rows * width), BF16), shape((PAD, channels), BF16)),
         in_specs=[whole] * 3,
-        out_specs=whole,
+        out_specs=(whole, whole),
         compiler_params=params(32),
+        cost_estimate=LIGHT,
         name="pack_cotangent",
     )(cotangent, scale, gain)
 
@@ -321,23 +321,27 @@
     ]
 
 
-def cot_kernel(cot_all, w_reduce, bias, gain, wide_bias, back, matrix):
-    count, padded, pixels = cot_all.shape
-    channels = padded - PAD
+def cot_kernel(cot_all, w_reduce, bias, *refs):
+    shares, (gain, wide_bias, back, matrix) = refs[:-4], refs[-4:]
+    count, channels, _ = cot_all.shape
 
     @pl.when(pl.program_id(0) == 0)
     def _():
         ones = jnp.ones((PAD, gain.shape[1]), BF16)
         wide_bias[...] = dot(stacked_rows(bias[...]), ones, COLS_BY_COLS)
+        unpack(cot_all, matrix)
         for k in range(count):
-            cut = slice(k * channels, (k + 1) * channels)
-            matrix[cut, :] = cot_all[k, :channels, :]
-            gain[cut, :] = dot(cot_all[k, channels:, :], ones, COLS_BY_COLS)[:channels, :]
+            if len(shares) == 1:
+                place, share = k, shares[0][k]
+            else:
+                place, share = lax.rem(lax.axis_index("chan") + count - k, count), shares[k][...]
+            at = pl.multiple_of(place * channels, PAD)
+            gain[pl.ds(at, channels), :] = dot(share, ones, COLS_BY_COLS)
 
     back[...] = dot(w_reduce[...], matrix[...], COLS_BY_COLS)
 
 
-def cot_stage(cot_all, w_reduce, bias):
+def cot_stage(cot_all, w_reduce, bias, shares):
     pixels = cot_all.shape[2]
     every, units = w_reduce.shape
     tile = tile_of(units)
@@ -345,13 +349,14 @@
         cot_kernel,
         grid=(units // tile,),
         out_shape=(shape((every, 128), F32), shape((units, 128), F32), shape((units, pixels), F32)),
-        in_specs=[fixed(cot_all.shape), columns_of(every, tile), fixed((1, units))],
+        in_specs=[fixed(cot_all.shape), columns_of(every, tile), fixed((1, units))]
+        + [fixed(share.shape) for share in shares],
         out_specs=(fixed((every, 128)), fixed((units, 128)), rows_of(tile, pixels)),
         scratch_shapes=[pltpu.VMEM((every, pixels), BF16)],
         compiler_params=params(60),
         cost_estimate=LIGHT,
         name="cotangent_stage",
-    )(cot_all, w_reduce, bias[None, :])
+    )(cot_all, w_reduce, bias[None, :], *shares)
 
 
 def widened(values, pixels):
@@ -453,7 +458,7 @@
     count = lax.axis_size("chan")
     units, every = w_expand.shape
     pixels = normed.shape[1]
-    tile = tile_of(units)
+    tile = 512 if units % 512 == 0 else tile_of(units)
     steps = units // tile
     blocks = count if count <= 4 else 1
     return pl.pallas_call(
@@ -497,9 +502,9 @@
 
 
 def unpack(cot_all, target):
-    channels = cot_all.shape[1] - PAD
+    channels = cot_all.shape[1]
     for k in range(cot_all.shape[0]):
-        target[k * channels : (k + 1) * channels, :] = cot_all[k, :channels, :]
+        target[k * channels : (k + 1) * channels, :] = cot_all[k]
 
 
 def own_tile_kernel(normed, cot_all, hidden, grad_pre, grad_reduce, grad_expand, cot):
@@ -572,35 +577,8 @@
     )(normed, cot_all, reduce_own, expand_own, w_expand, bias, w_reduce)
 
 
-def pair_kernel(*refs):
-    mine, theirs, result = refs[0], refs[1], refs[-1]
-    result[...] = (mine[...].astype(F32) + theirs[...].astype(F32)).astype(BF16)
-
-
-def add_pair(part, parts, axis, mine, theirs, target):
-    height, width = mine.shape
-    if axis == 0:
-        tile = 384 if height % 384 == 0 else tile_of(height)
-        steps = height // tile
-        block, dims = rows_of(tile, width), (height * parts, width)
-        placed = rows_of(tile, width, part * steps)
-    else:
-        tile = 384 if height % 384 == 0 else tile_of(height)
-        steps = height // tile
-        block, dims = rows_of(tile, width), (height, width * parts)
-        placed = pl.BlockSpec((tile, width), lambda t: (t, part))
-    known = () if target is None else (target,)
-    return pl.pallas_call(
-        pair_kernel,
-        grid=(steps,),
-        out_shape=shape(dims, BF16),
-        in_specs=[block, block] + [anywhere] * len(known),
-        out_specs=placed,
-        input_output_aliases={2: 0} if known else {},
-        compiler_params=params(60),
-        cost_estimate=LIGHT,
-        name="add_pair",
-    )(mine, theirs, *known)
+def pair_sum(mine, theirs):
+    return (mine.astype(F32) + theirs.astype(F32)).astype(BF16)
 
 
 def norm_gradient_kernel(every, centered, local, stats, gain, *refs):
@@ -680,13 +658,19 @@
     image_rows = jnp.transpose(image, (1, 0, 2))
     around = surroundings(image_rows)
     cot_rows = jnp.transpose(cotangent, (1, 0, 2))
-    packed_cot = pack_cotangent(cot_rows, layer_scale[:, None], layer_norm_weight[None, :])
+    packed_cot, gain_rows = pack_cotangent(cot_rows, layer_scale, layer_norm_weight)
     cot_all = lax.all_gather(packed_cot, "chan")
 
     packed_conv, centered, local = forward_conv(around, kernel)
     conv_all = lax.all_gather(packed_conv, "chan")
     cot_all, bias = after((cot_all, bias_expand), packed_conv)
-    gain, bias, back = cot_stage(cot_all, w_reduce, bias)
+    gain_rows = after(gain_rows, packed_conv)
+    count = lax.axis_size("chan")
+    shares = [lax.all_gather(gain_rows, "chan")]
+    if count <= 4:
+        turns = [[(i, (i + k) % count) for i in range(count)] for k in range(1, count)]
+        shares = [gain_rows] + [lax.ppermute(gain_rows, "chan", turn) for turn in turns]
+    gain, bias, back = cot_stage(cot_all, w_reduce, bias, shares)
     normed, stats = norm_stage(conv_all, gain)
     ready = normed
     if two_tiles:
@@ -707,7 +691,7 @@
     grad_around = surroundings(gradient, taps if two_tiles else None)
     if two_tiles:
         theirs = [swap(after(mine, gradient), "cols") for mine in found]
-        grad_reduce = add_pair(0, 1, 0, found[0], theirs[0], None)
+        grad_reduce = pair_sum(found[0], theirs[0])
         grad_around = after(grad_around, grad_reduce)
     grad_rows = backward_conv(grad_around, kernel, cot_rows)
     grad_input = jnp.transpose(grad_rows, (1, 0, 2))
@@ -715,7 +699,7 @@
         taps = after(taps, grad_rows)
         taps = taps + swap(taps, "cols")
         taps = taps + swap(taps, "rows")
-        grad_expand = add_pair(0, 1, 0, found[1], theirs[1], None)
+        grad_expand = pair_sum(found[1], theirs[1])
         reduced = after(reduced, grad_expand, taps)
     else:
         taps = lax.psum(taps, ("rows", "cols"))

time: 198 us -> 197 us (level)
  Pallas kernels: 91.1 us -> 76.9 us
  other arithmetic: 1.33 us -> 14.4 us
  starting transfers between devices: 14.5 us -> 17.6 us
  waiting for transfers between devices: 62.5 us -> 59.6 us
    convert_element_type x0 -> x2, other arithmetic: none -> 13.1 us  [pair_sum(): return (mine.astype(F32) + theirs.astype(F32)).astype(BF16)]
    pallas_call x3 -> x1, Pallas kernels: 14 us -> 1.03 us  [pack_cotangent(): pl.pallas_call(pack_kernel, out_shape=(shape((channels, rows * width), BF...]
    all_gather x1, waiting for transfers between devices: 28.8 us -> 21.6 us  [on_device(): conv_all = lax.all_gather(packed_conv, 'chan')]
    ppermute x0 -> x3, waiting for transfers between devices: none -> 3.52 us  [on_device(): lax.ppermute(gain_rows, 'chan', turn)]
    ppermute x0 -> x3, starting transfers between devices: none -> 3.31 us  [on_device(): lax.ppermute(gain_rows, 'chan', turn)]
    unnamed x29 -> x45, local copies, waits for them, and re-layouts: 10.2 us -> 12.1 us
  transfers between devices with their start and end apart: 18 -> 21, of which waited for: 8 -> 10; matrix products, arithmetic and copies ran while one was open for 2% -> 9% of each run, Pallas kernels for 45% -> 38%
where the time goes in v4:
time: 197 us; the launch traced here: 196 us
  Pallas kernels  76.9 us (39%)
  waiting for transfers between devices  59.6 us (30%)
  starting transfers between devices  17.6 us (9%)
  other arithmetic  14.4 us (7%)
  between operations  14 us (7%)
  local copies, waits for them, and re-layouts  13.5 us (7%)
    all_gather x1, waiting for transfers between devices, on_device(): conv_all = lax.all_gather(packed_conv, 'chan')  21.6 us
    all_gather x1, waiting for transfers between devices, on_device(): cot_all = lax.all_gather(packed_cot, 'chan')  19.6 us
    pallas_call x1, Pallas kernels, two_tile_gradients(): pl.pallas_call(other_tile_kernel, grid=(units // tile,), out_shape=(shape...  17.2 us
    convert_element_type x2, other arithmetic, pair_sum(): return (mine.astype(F32) + theirs.astype(F32)).astype(BF16)  13.1 us
    unnamed x45, local copies, waits for them, and re-layouts  12.1 us
    pallas_call x1, Pallas kernels, block_stage(): pl.pallas_call(functools.partial(block_kernel, steps), grid=(steps,), out...  11.9 us
    pallas_call x1, Pallas kernels, own_tile_gradients(): pl.pallas_call(own_tile_kernel, grid=(units // tile,), out_shape=(shape((...  10.4 us
    ppermute x2, waiting for transfers between devices, from_sides(): got = lax.ppermute(sent, axis, [(0, 1), (1, 0)])  8.3 us
  transfers between devices with their start and end apart: 21, of which 10 were waited for; matrix products, arithmetic and copies ran while one was open for 9% of the time, Pallas kernels for 38%

profile of v4, /device:TPU:0, one launch (start us, length us, event | category | flops | bytes accessed | tf_op | source)
XLA Modules:
  0.0 196.0 jit_solution(1732218910812112108)
XLA Ops:
  7.2 0.0 all-gather.7.cloned.1.call-start
  7.2 1.0 copy.23
  8.3 0.7 copy-done.10
  9.0 0.7 copy-done.12
  9.6 1.0 pack_cotangent.1
  10.7 0.0 all-gather.7.cloned.1.call-update
  10.7 0.0 all-gather.5.cloned.1.call-start
  10.8 1.1 copy.24
  11.8 3.0 %collective-permute-start = (bf16[3,384,128]{2,1,0:T(8,128)(2,1)S(1)}, bf16[3,384,128]{2,1,0:T(8,128)(2,1)S(1)}, u32[]{:S(2)}, u32[]{:S(2)}) collective-permute-start(bf16[3,384,128]{2,1,0:T(8,128)(2,1)S(1)} %slice_select_fusion.1), channel_id=1, source_target_pairs={{0,2},{2,0},{1,3},{3,1},{4,6},{6,4},{5,7},{7,5},{8,10},{10,8},{9,1... | collective-permute-start | bytes 884744 | tf_op jit(solution)/shard_map/ppermute | solution.py:58
  14.9 7.0 %collective-permute-done.above.below = bf16[3,384,128]{2,1,0:T(8,128)(2,1)S(1)} collective-permute-done((bf16[3,384,128]{2,1,0:T(8,128)(2,1)S(1)}, bf16[3,384,128]{2,1,0:T(8,128)(2,1)S(1)}, u32[]{:S(2)}, u32[]{:S(2)}) %collective-permute-start) | collective-permute-done | bytes 294944 | tf_op jit(solution)/shard_map/ppermute | solution.py:58
  21.9 1.0 copy.14.kernel
  22.9 0.5 collective-permute-done.2.above_side.below_side
  23.4 6.6 %conv_forward.1 = (bf16[400,512]{1,0:T(8,128)(2,1)}, f32[384,512]{1,0:T(8,128)S(1)}, f32[8,512]{1,0:T(8,128)S(1)}) custom-call(bf16[4,384,128]{2,1,0:T(8,128)(2,1)S(1)} %bitcast.18, bf16[3,384,128]{2,1,0:T(8,128)(2,1)S(1)} %collective-permute-done.above.below, bf16[3,384,128]{2,1,0:T(8,128)(2,1)S(1)} %collective-permute-done.above.below, ...), custom_call_target="tpu_custom_call" | custom-call | flops 1000 | bytes 1000 | tf_op jit(solution)/shard_map/conv_forward/pallas_call | solution.py:174
  30.1 0.9 copy-done.4
  30.9 0.0 all-gather.5.cloned.1.call-update
  31.0 0.0 reduce-scatter.2.cloned.1.call-start
  31.0 19.6 %all-gather.7.cloned.1.call-done = bf16[1536,512]{1,0:T(8,128)(2,1)} async-done(((bf16[384,512]{1,0:T(8,128)(2,1)}), bf16[1536,512]{1,0:T(8,128)(2,1)}) %all-gather.7.cloned.1.call-update) | async-done | bytes 1572880 | tf_op jit(solution)/shard_map/all_gather | solution.py:662
  50.6 1.5 collective-permute-start.6
  52.1 1.3 collective-permute-start.5
  53.4 0.7 collective-permute-start.4
  54.0 1.4 collective-permute-start.3
  55.4 0.6 broadcast_in_dim.4.bias
  56.0 1.9 collective-permute-done.4.refs_2_
  58.0 1.6 collective-permute-done.3.refs_1_
  59.5 0.0 copy-start.16
  59.6 0.6 copy-done.16
  60.2 8.2 %cotangent_stage.1 = (f32[1536,128]{1,0:T(8,128)}, f32[1536,128]{1,0:T(8,128)}, f32[1536,512]{1,0:T(8,128)}) custom-call(bf16[4,384,512]{2,1,0:T(8,128)(2,1)} %bitcast.25, bf16[1536,1536]{1,0:T(8,128)(2,1)} %w_reduce.3, f32[1,1536]{1,0:T(1,128)} %broadcast_in_dim.4.bias, bf16[16,384]{1,0:T(8,128)(2,1)} %copy-done.9, bf16[16,384]{1,0:T(8,128)(2,1)} %copy-done.16, ...), custom_call_target="tpu_custom_call" | custom-call | flops 1000 | bytes 1000 | tf_op jit(solution)/shard_map/cotangent_stage/pallas_call | solution.py:348
  68.3 21.6 %all-gather.5.cloned.1.call-done = bf16[1600,512]{1,0:T(8,128)(2,1)} async-done(((bf16[400,512]{1,0:T(8,128)(2,1)}), bf16[1600,512]{1,0:T(8,128)(2,1)}) %all-gather.5.cloned.1.call-update) | async-done | bytes 1638416 | tf_op jit(solution)/shard_map/all_gather | solution.py:665
  89.9 1.1 copy-done
  91.0 1.4 copy-done.3
  92.5 1.5 norm.1
  94.0 0.0 copy-start.7
  94.0 0.6 copy-done.7
  94.6 1.4 collective-permute-start.7
  96.0 11.9 %pointwise_block.1 = (bf16[1536,512]{1,0:T(8,128)(2,1)}, bf16[1536,512]{1,0:T(8,128)(2,1)}, bf16[400,512]{1,0:T(8,128)(2,1)}, bf16[400,512]{1,0:T(8,128)(2,1)}, ...) custom-call(bf16[1536,512]{1,0:T(8,128)(2,1)} %copy-done.2, f32[1536,128]{1,0:T(8,128)} %get-tuple-element.55.gain, ...), custom_call_target="tpu_custom_call" | custom-call | flops 1000 | bytes 1000 | tf_op jit(solution)/shard_map/pointwise_block/pallas_call | solution.py:464
  107.9 0.5 collective-permute-start.8
  108.4 1.4 collective-permute-start.9
  109.8 2.4 %collective-permute-start.10 = (bf16[400,512]{1,0:T(8,128)(2,1)}, bf16[400,512]{1,0:T(8,128)(2,1)}, u32[]{:S(2)}, u32[]{:S(2)}) collective-permute-start(bf16[400,512]{1,0:T(8,128)(2,1)} %get-tuple-element.69), channel_id=1, source_target_pairs={{0,12},{4,0},{8,4},{12,8},{1,13},{5,1},{9,5},{13,9},{2,14},{6,2},{... | collective-permute-start | bytes 1228808 | tf_op jit(solution)/shard_map/ppermute | solution.py:637
  112.2 6.2 %reduced_product.1 = bf16[1536,512]{1,0:T(8,128)(2,1)} custom-call(bf16[1536,1536]{1,0:T(8,128)(2,1)} %w_reduce.3, bf16[1536,512]{1,0:T(8,128)(2,1)} %get-tuple-element.61.hidden), custom_call_target="tpu_custom_call" | custom-call | flops 1000 | bytes 1000 | tf_op jit(solution)/shard_map/reduced_product/pallas_call | solution.py:492
  118.4 10.4 %own_tile_gradients.1 = (bf16[1536,1536]{1,0:T(8,128)(2,1)}, bf16[1536,1536]{1,0:T(8,128)(2,1)}) custom-call(bf16[1536,512]{1,0:T(8,128)(2,1)} %copy-done.2, bf16[4,384,512]{2,1,0:T(8,128)(2,1)} %bitcast.26, bf16[1536,512]{1,0:T(8,128)(2,1)} %get-tuple-element.61.hidden, bf16[1536,512]{1,0:T(8,128)(2,1)} %get-tuple-element.62.grad_pre), custom_call_target="tpu_custom_call" | custom-call | flops 1000 | bytes 1000 | tf_op jit(solution)/shard_map/own_tile_gradients/pallas_call | solution.py:523
  128.8 2.1 %collective-permute-done.7.normed = bf16[1536,512]{1,0:T(8,128)(2,1)} collective-permute-done((bf16[1536,512]{1,0:T(8,128)(2,1)S(1)}, bf16[1536,512]{1,0:T(8,128)(2,1)}, u32[]{:S(2)}, u32[]{:S(2)}) %collective-permute-start.7) | collective-permute-done | bytes 1572896 | tf_op jit(solution)/shard_map/ppermute | solution.py:647
  130.9 17.2 %two_tile_gradients.1 = (bf16[1536,1536]{1,0:T(8,128)(2,1)}, bf16[1536,1536]{1,0:T(8,128)(2,1)}) custom-call(bf16[1536,512]{1,0:T(8,128)(2,1)} %collective-permute-done.7.normed, bf16[4,384,512]{2,1,0:T(8,128)(2,1)} %collective-permute-done.6.cot_all, bf16[1536,1536]{1,0:T(8,128)(2,1)} %get-tuple-element.63.reduce_own, ...), custom_call_target="tpu_custom_call" | custom-call | flops 1000 | bytes 1000 | tf_op jit(solution)/shard_map/two_tile_gradients/pallas_call | solution.py:559
  148.1 1.1 copy-done.5
  149.2 1.9 norm_gradient.1.gradient.block
  151.1 0.1 collective-permute-start.15
  151.2 0.5 collective-permute-start.11
  151.7 1.4 collective-permute-start.12
  153.1 0.0 reduce-scatter.2.cloned.1.call-update
  153.1 0.1 collective-permute-start.13
  153.2 6.2 %kernel_gradient.1 = f32[384,128]{1,0:T(8,128)S(1)} custom-call(bf16[4,384,128]{2,1,0:T(8,128)(2,1)S(1)} %bitcast.19, bf16[3,384,128]{2,1,0:T(8,128)(2,1)S(1)} %collective-permute-done.above.below, bf16[3,384,128]{2,1,0:T(8,128)(2,1)S(1)} %collective-permute-done.above.below, bf16[4,384,128]{2,1,0:T(8,128)(2,1)S(1)} %collective-permute-done.1.side, ...), custom_call_target="tpu_custom_call" | custom-call | flops 1000 | bytes 1000 | tf_op jit(solution)/shard_map/kernel_gradient/pallas_call | solution.py:248
  159.4 0.0 copy-start.13
  159.5 1.3 collective-permute-done.12.above.below
  160.8 7.3 %add_convert_fusion = bf16[1536,1536]{1,0:T(8,128)(2,1)} fusion(bf16[1536,1536]{1,0:T(8,128)(2,1)} %collective-permute-done.15, bf16[1536,1536]{1,0:T(8,128)(2,1)} %get-tuple-element.84), kind=kLoop, calls=%fused_computation | loop fusion | flops 9437184 | bytes 14155776 | tf_op jit(solution)/shard_map/convert_element_type | solution.py:581
  168.1 5.7 %conv_backward.1 = bf16[4,384,128]{2,1,0:T(8,128)(2,1)S(1)} custom-call(bf16[4,384,128]{2,1,0:T(8,128)(2,1)S(1)} %norm_gradient.1.gradient.block, bf16[3,384,128]{2,1,0:T(8,128)(2,1)S(1)} %collective-permute-done.12.above.below, bf16[3,384,128]{2,1,0:T(8,128)(2,1)S(1)} %collective-permute-done.12.above.below, ...), custom_call_target="tpu_custom_call" | custom-call | flops 1000 | bytes 1000 | tf_op jit(solution)/shard_map/conv_backward/pallas_call | solution.py:206
  173.8 0.6 collective-permute-start.16
  174.3 0.1 convert.1
  174.4 1.0 collective-permute-done.16
  175.5 1.4 collective-permute-start.17
  176.9 5.8 %add_convert_fusion.1 = bf16[1536,1536]{1,0:T(8,128)(2,1)} fusion(bf16[1536,1536]{1,0:T(8,128)(2,1)} %collective-permute-done.11, bf16[1536,1536]{1,0:T(8,128)(2,1)S(1)} %bitcast.28), kind=kLoop, calls=%fused_computation.1 | loop fusion | flops 9437184 | bytes 14155776 | tf_op jit(solution)/shard_map/convert_element_type | solution.py:581
  182.7 1.1 copy.17
  183.8 2.9 %reduce-scatter.2.cloned.1.call-done = bf16[384,512]{1,0:T(8,128)(2,1)} async-done(((bf16[1536,512]{1,0:T(8,128)(2,1)}), bf16[384,512]{1,0:T(8,128)(2,1)}) %reduce-scatter.2.cloned.1.call-update) | async-done | bytes 393232 | tf_op jit(solution)/shard_map/reduce_scatter | solution.py:683
  186.7 1.1 fusion
  187.9 0.8 reshape.17
  188.7 0.8 copy.18
  (48 shorter events, 0.2 us)
Async XLA Ops:
  7.2 48.3 %copy-start.17 = (f32[1536]{0:T(1024)S(1)}, f32[1536]{0:T(1024)}, u32[]{:S(2)}) copy-start(f32[1536]{0:T(1024)} %param.12) | copy-start | bytes 18436
  7.2 43.5 %all-gather.7.cloned.1.call-start = ((), (), s32[]{:S(2)}) async-start(), calls=%async_computation.3 | async-start | bytes 1966080 | tf_op jit(solution)/shard_map/all_gather | solution.py:662
  8.3 0.7 copy-start.10
  9.0 0.7 copy-start.12
  10.7 48.9 %copy-start.9 = (bf16[16,384]{1,0:T(8,128)(2,1)}, bf16[16,384]{1,0:T(8,128)(2,1)S(1)}, u32[]{:S(2)}) copy-start(bf16[16,384]{1,0:T(8,128)(2,1)S(1)} %get-tuple-element.54.refs_0_) | copy-start | bytes 36868
  10.7 79.2 %all-gather.5.cloned.1.call-start = ((), (), s32[]{:S(2)}) async-start(), calls=%async_computation.2 | async-start | bytes 2048000 | tf_op jit(solution)/shard_map/all_gather | solution.py:665
  11.8 10.0 %collective-permute-start = (bf16[3,384,128]{2,1,0:T(8,128)(2,1)S(1)}, bf16[3,384,128]{2,1,0:T(8,128)(2,1)S(1)}, u32[]{:S(2)}, u32[]{:S(2)}) collective-permute-start(bf16[3,384,128]{2,1,0:T(8,128)(2,1)S(1)} %slice_select_fusion.1), channel_id=1, source_target_pairs={{0,2},{2,0},{1,3},{3,1},{4,6},{6,4},{5,7},{7,5},{8,10},{10,8},{9,1... | collective-permute-start | bytes 884744 | tf_op jit(solution)/shard_map/ppermute | solution.py:58
  14.8 8.0 %collective-permute-start.1 = (bf16[4,384,128]{2,1,0:T(8,128)(2,1)S(1)}, bf16[4,384,128]{2,1,0:T(8,128)(2,1)S(1)}, u32[]{:S(2)}, u32[]{:S(2)}) collective-permute-start(bf16[4,384,128]{2,1,0:T(8,128)(2,1)S(1)} %bitcast.17), channel_id=1, source_target_pairs={{0,1},{1,0},{2,3},{3,2},{4,5},{5,4},{6,7},{7,6},{8,9},{9,8},{10,11... | collective-permute-start | bytes 1179656 | tf_op jit(solution)/shard_map/ppermute | solution.py:68
  21.9 1.6 collective-permute-start.2
  30.1 0.9 copy-start.4
  31.0 155.7 %reduce-scatter.2.cloned.1.call-start = ((), (), s32[]{:S(2)}) async-start(), calls=%async_computation.1 | async-start | bytes 1966080 | tf_op jit(solution)/shard_map/reduce_scatter | solution.py:683
  50.6 45.4 %collective-permute-start.6 = (bf16[4,384,512]{2,1,0:T(8,128)(2,1)}, bf16[4,384,512]{2,1,0:T(8,128)(2,1)}, u32[]{:S(2)}, u32[]{:S(2)}) collective-permute-start(bf16[4,384,512]{2,1,0:T(8,128)(2,1)} %bitcast.24), channel_id=1, source_target_pairs={{0,2},{2,0},{1,3},{3,1},{4,6},{6,4},{5,7},{7,5},{8,10},{10,8},{9,1... | collective-permute-start | bytes 4718600 | tf_op jit(solution)/shard_map/ppermute | solution.py:647
  52.1 3.9 %collective-permute-start.5 = (bf16[16,384]{1,0:T(8,128)(2,1)S(1)}, bf16[16,384]{1,0:T(8,128)(2,1)S(1)}, u32[]{:S(2)}, u32[]{:S(2)}) collective-permute-start(bf16[16,384]{1,0:T(8,128)(2,1)S(1)} %get-tuple-element.54.refs_0_), channel_id=1, source_target_pairs={{0,12},{4,0},{8,4},{12,8},{1,13},{5,1},{9,5},{13,9},{2,14},{6,2},{... | collective-permute-start | bytes 36872 | tf_op jit(solution)/shard_map/ppermute | solution.py:672
  53.4 4.6 %collective-permute-start.4 = (bf16[16,384]{1,0:T(8,128)(2,1)S(1)}, bf16[16,384]{1,0:T(8,128)(2,1)S(1)}, u32[]{:S(2)}, u32[]{:S(2)}) collective-permute-start(bf16[16,384]{1,0:T(8,128)(2,1)S(1)} %get-tuple-element.54.refs_0_), channel_id=1, source_target_pairs={{0,8},{4,12},{8,0},{12,4},{1,9},{5,13},{9,1},{13,5},{2,10},{6,14},... | collective-permute-start | bytes 36872 | tf_op jit(solution)/shard_map/ppermute | solution.py:672
  54.0 5.5 %collective-permute-start.3 = (bf16[16,384]{1,0:T(8,128)(2,1)S(1)}, bf16[16,384]{1,0:T(8,128)(2,1)S(1)}, u32[]{:S(2)}, u32[]{:S(2)}) collective-permute-start(bf16[16,384]{1,0:T(8,128)(2,1)S(1)} %get-tuple-element.54.refs_0_), channel_id=1, source_target_pairs={{0,4},{4,8},{8,12},{12,0},{1,5},{5,9},{9,13},{13,1},{2,6},{6,10},{... | collective-permute-start | bytes 36872 | tf_op jit(solution)/shard_map/ppermute | solution.py:672
  56.0 3.5 %copy-start.14 = (bf16[16,384]{1,0:T(8,128)(2,1)}, bf16[16,384]{1,0:T(8,128)(2,1)S(1)}, u32[]{:S(2)}) copy-start(bf16[16,384]{1,0:T(8,128)(2,1)S(1)} %collective-permute-done.5.refs_3_) | copy-start | bytes 36868
  58.0 1.6 copy-start.15
  59.5 0.6 copy-start.16
  89.9 1.1 copy-start
  91.0 1.4 copy-start.3
  94.0 0.6 copy-start.7
  94.6 1.4 copy-start.2
  94.6 36.3 %collective-permute-start.7 = (bf16[1536,512]{1,0:T(8,128)(2,1)S(1)}, bf16[1536,512]{1,0:T(8,128)(2,1)}, u32[]{:S(2)}, u32[]{:S(2)}) collective-permute-start(bf16[1536,512]{1,0:T(8,128)(2,1)S(1)} %get-tuple-element.57.normed), channel_id=1, source_target_pairs={{0,2},{2,0},{1,3},{3,1},{4,6},{6,4},{5,7},{7,5},{8,10},{10,8},{9,1... | collective-permute-start | bytes 4718600 | tf_op jit(solution)/shard_map/ppermute | solution.py:647
  107.9 40.1 %collective-permute-start.8 = (bf16[400,512]{1,0:T(8,128)(2,1)}, bf16[400,512]{1,0:T(8,128)(2,1)}, u32[]{:S(2)}, u32[]{:S(2)}) collective-permute-start(bf16[400,512]{1,0:T(8,128)(2,1)} %get-tuple-element.67), channel_id=1, source_target_pairs={{0,4},{4,8},{8,12},{12,0},{1,5},{5,9},{9,13},{13,1},{2,6},{6,10},{... | collective-permute-start | bytes 1228808 | tf_op jit(solution)/shard_map/ppermute | solution.py:637
  108.4 39.7 %collective-permute-start.9 = (bf16[400,512]{1,0:T(8,128)(2,1)}, bf16[400,512]{1,0:T(8,128)(2,1)}, u32[]{:S(2)}, u32[]{:S(2)}) collective-permute-start(bf16[400,512]{1,0:T(8,128)(2,1)} %get-tuple-element.68), channel_id=1, source_target_pairs={{0,8},{4,12},{8,0},{12,4},{1,9},{5,13},{9,1},{13,5},{2,10},{6,14},... | collective-permute-start | bytes 1228808 | tf_op jit(solution)/shard_map/ppermute | solution.py:637
  109.8 38.3 %collective-permute-start.10 = (bf16[400,512]{1,0:T(8,128)(2,1)}, bf16[400,512]{1,0:T(8,128)(2,1)}, u32[]{:S(2)}, u32[]{:S(2)}) collective-permute-start(bf16[400,512]{1,0:T(8,128)(2,1)} %get-tuple-element.69), channel_id=1, source_target_pairs={{0,12},{4,0},{8,4},{12,8},{1,13},{5,1},{9,5},{13,9},{2,14},{6,2},{... | collective-permute-start | bytes 1228808 | tf_op jit(solution)/shard_map/ppermute | solution.py:637
  130.9 17.2 %copy-start.1 = (f32[1536,128]{1,0:T(8,128)S(1)}, f32[1536,128]{1,0:T(8,128)}, u32[]{:S(2)}) copy-start(f32[1536,128]{1,0:T(8,128)} %get-tuple-element.55.gain) | copy-start | bytes 2359300
  130.9 17.2 %copy-start.6 = (bf16[400,512]{1,0:T(8,128)(2,1)S(1)}, bf16[400,512]{1,0:T(8,128)(2,1)}, u32[]{:S(2)}) copy-start(bf16[400,512]{1,0:T(8,128)(2,1)} %get-tuple-element.77.refs_0_) | copy-start | bytes 1228804
  130.9 17.2 %copy-start.8 = (f32[8,512]{1,0:T(8,128)S(1)}, f32[8,512]{1,0:T(8,128)}, u32[]{:S(2)}) copy-start(f32[8,512]{1,0:T(8,128)} %copy-done.7) | copy-start | bytes 49156
  148.1 1.1 copy-start.5
  151.1 9.7 %collective-permute-start.15 = (bf16[1536,1536]{1,0:T(8,128)(2,1)}, bf16[1536,1536]{1,0:T(8,128)(2,1)}, u32[]{:S(2)}, u32[]{:S(2)}) collective-permute-start(bf16[1536,1536]{1,0:T(8,128)(2,1)} %get-tuple-element.84), channel_id=1, source_target_pairs={{0,1},{1,0},{2,3},{3,2},{4,5},{5,4},{6,7},{7,6},{8,9},{9,8},{10,11... | collective-permute-start | bytes 14155784 | tf_op jit(solution)/shard_map/ppermute | solution.py:647
  151.2 25.7 %collective-permute-start.11 = (bf16[1536,1536]{1,0:T(8,128)(2,1)}, bf16[1536,1536]{1,0:T(8,128)(2,1)}, u32[]{:S(2)}, u32[]{:S(2)}) collective-permute-start(bf16[1536,1536]{1,0:T(8,128)(2,1)} %get-tuple-element.81), channel_id=1, source_target_pairs={{0,1},{1,0},{2,3},{3,2},{4,5},{5,4},{6,7},{7,6},{8,9},{9,8},{10,11... | collective-permute-start | bytes 14155784 | tf_op jit(solution)/shard_map/ppermute | solution.py:647
  151.7 9.1 %collective-permute-start.12 = (bf16[3,384,128]{2,1,0:T(8,128)(2,1)S(1)}, bf16[3,384,128]{2,1,0:T(8,128)(2,1)S(1)}, u32[]{:S(2)}, u32[]{:S(2)}) collective-permute-start(bf16[3,384,128]{2,1,0:T(8,128)(2,1)S(1)} %slice_select_fusion), channel_id=1, source_target_pairs={{0,2},{2,0},{1,3},{3,1},{4,6},{6,4},{5,7},{7,5},{8,10},{10,8},{9,1... | collective-permute-start | bytes 884744 | tf_op jit(solution)/shard_map/ppermute | solution.py:58
  153.1 14.9 %collective-permute-start.13 = (bf16[4,384,128]{2,1,0:T(8,128)(2,1)S(1)}, bf16[4,384,128]{2,1,0:T(8,128)(2,1)S(1)}, u32[]{:S(2)}, u32[]{:S(2)}) collective-permute-start(bf16[4,384,128]{2,1,0:T(8,128)(2,1)S(1)} %norm_gradient.1.gradient.block), channel_id=1, source_target_pairs={{0,1},{1,0},{2,3},{3,2},{4,5},{5,4},{6,7},{7,6},{8,9},{9,8},{10,11... | collective-permute-start | bytes 1179656 | tf_op jit(solution)/shard_map/ppermute | solution.py:68
  153.2 23.7 %slice-start = ((s8[4718592]{0:T(1024)(128)(4,1)}), s8[4194304]{0:T(1024)(128)(4,1)S(1)}, s32[]{:S(2)}) async-start(s8[4718592]{0:T(1024)(128)(4,1)} %bitcast.27), calls=%async_computation.4 | async-start | bytes 8388608
  159.4 14.9 %copy-start.13 = (bf16[384,4,128]{2,1,0:T(4,128)(2,1)S(1)}, bf16[384,4,128]{2,1,0:T(4,128)(2,1)}, u32[]{:S(2)}) copy-start(bf16[384,4,128]{2,1,0:T(4,128)(2,1)} %param.8) | copy-start | bytes 1179652
  159.4 17.4 %slice-start.1 = ((s8[4718592]{0:T(1024)(128)(4,1)}), s8[524288]{0:T(1024)(128)(4,1)S(1)}, s32[]{:S(2)}) async-start(s8[4718592]{0:T(1024)(128)(4,1)} %bitcast.27), calls=%async_computation.5 | async-start | bytes 1048576
  160.8 7.3 %collective-permute-start.14 = (bf16[3,384,128]{2,1,0:T(8,128)(2,1)S(1)}, bf16[3,384,128]{2,1,0:T(8,128)(2,1)S(1)}, u32[]{:S(2)}, u32[]{:S(2)}) collective-permute-start(bf16[3,384,128]{2,1,0:T(8,128)(2,1)S(1)} %collective-permute-done.12.above.below), channel_id=1, source_target_pairs={{0,1},{1,0},{2,3},{3,2},{4,5},{5,4},{6,7},{7,6},{8,9},{9,8},{10,11... | collective-permute-start | bytes 884744 | tf_op jit(solution)/shard_map/ppermute | solution.py:68
  173.8 1.6 collective-permute-start.16
  175.4 11.3 %copy-start.11 = (f32[384]{0:T(512)S(1)}, f32[384]{0:T(512)}, u32[]{:S(2)}) copy-start(f32[384]{0:T(512)} %scale.1) | copy-start | bytes 4612
  175.5 8.3 %collective-permute-start.17 = (f32[384,128]{1,0:T(8,128)S(1)}, f32[384,128]{1,0:T(8,128)S(1)}, u32[]{:S(2)}, u32[]{:S(2)}) collective-permute-start(f32[384,128]{1,0:T(8,128)S(1)} %add.19), channel_id=1, source_target_pairs={{0,2},{2,0},{1,3},{3,1},{4,6},{6,4},{5,7},{7,5},{8,10},{10,8},{9,1... | collective-permute-start | bytes 589832 | tf_op jit(solution)/shard_map/ppermute | solution.py:647
Sparse Core Ops, SparseCore 0:
  10.8 39.7 all-gather.6
  52.8 37.0 all-gather.4
  153.2 33.4 reduce-scatter.1

commit v5 on v4

--- a/solution.py
+++ b/solution.py
@@ -47,7 +47,7 @@
 
 
 def unstacked(block, first):
-    return jnp.sum(block[3 * first : 3 * first + 3, :].astype(F32), axis=0, keepdims=True)
+    return jnp.sum(block.astype(F32)[3 * first : 3 * first + 3, :], axis=0, keepdims=True)
 
 
 def from_sides(low_source, high_source, axis):
@@ -519,7 +519,7 @@
 def own_tile_gradients(normed, cot_all, hidden, grad_pre):
     every, pixels = normed.shape
     units = hidden.shape[0]
-    tile = tile_of(units)
+    tile = 512 if units % 512 == 0 else tile_of(units)
     return pl.pallas_call(
         own_tile_kernel,
         grid=(units // tile,),
@@ -555,7 +555,7 @@
 def two_tile_gradients(normed, cot_all, reduce_own, expand_own, w_expand, bias, w_reduce):
     every, pixels = normed.shape
     units = w_expand.shape[0]
-    tile = tile_of(units)
+    tile = 384 if units % 384 == 0 else tile_of(units)
     return pl.pallas_call(
         other_tile_kernel,
         grid=(units // tile,),

time: 197 us -> 196 us (level)
  Pallas kernels: 76.9 us -> 74.9 us
  transfers between devices with their start and end apart: 21 -> 21, of which waited for: 10 -> 10; matrix products, arithmetic and copies ran while one was open for 9% -> 9% of each run, Pallas kernels for 38% -> 37%
where the time goes in v5:
time: 196 us; the launch traced here: 195 us
  Pallas kernels  74.9 us (38%)
  waiting for transfers between devices  61 us (31%)
  starting transfers between devices  17.6 us (9%)
  other arithmetic  14.4 us (7%)
  between operations  14 us (7%)
  local copies, waits for them, and re-layouts  13.5 us (7%)
    all_gather x1, waiting for transfers between devices, on_device(): conv_all = lax.all_gather(packed_conv, 'chan')  21.6 us
    all_gather x1, waiting for transfers between devices, on_device(): cot_all = lax.all_gather(packed_cot, 'chan')  19.6 us
    pallas_call x1, Pallas kernels, two_tile_gradients(): pl.pallas_call(other_tile_kernel, grid=(units // tile,), out_shape=(shape...  16.6 us
    convert_element_type x2, other arithmetic, pair_sum(): return (mine.astype(F32) + theirs.astype(F32)).astype(BF16)  13.1 us
    unnamed x45, local copies, waits for them, and re-layouts  12.1 us
    pallas_call x1, Pallas kernels, block_stage(): pl.pallas_call(functools.partial(block_kernel, steps), grid=(steps,), out...  11.9 us
    pallas_call x1, Pallas kernels, own_tile_gradients(): pl.pallas_call(own_tile_kernel, grid=(units // tile,), out_shape=(shape((...  9.02 us
    ppermute x2, waiting for transfers between devices, from_sides(): got = lax.ppermute(sent, axis, [(0, 1), (1, 0)])  8.3 us
  transfers between devices with their start and end apart: 21, of which 10 were waited for; matrix products, arithmetic and copies ran while one was open for 9% of the time, Pallas kernels for 37%

profile of v5, /device:TPU:0, one launch (start us, length us, event | category | flops | bytes accessed | tf_op | source)
XLA Modules:
  0.0 195.4 jit_solution(837351319612156808)
XLA Ops:
  7.2 0.0 all-gather.7.cloned.1.call-start
  7.2 1.0 copy.23
  8.3 0.7 copy-done.10
  9.0 0.7 copy-done.12
  9.6 1.0 pack_cotangent.1
  10.7 0.0 all-gather.7.cloned.1.call-update
  10.7 0.0 all-gather.5.cloned.1.call-start
  10.8 1.1 copy.24
  11.8 3.0 %collective-permute-start = (bf16[3,384,128]{2,1,0:T(8,128)(2,1)S(1)}, bf16[3,384,128]{2,1,0:T(8,128)(2,1)S(1)}, u32[]{:S(2)}, u32[]{:S(2)}) collective-permute-start(bf16[3,384,128]{2,1,0:T(8,128)(2,1)S(1)} %slice_select_fusion.1), channel_id=1, source_target_pairs={{0,2},{2,0},{1,3},{3,1},{4,6},{6,4},{5,7},{7,5},{8,10},{10,8},{9,1... | collective-permute-start | bytes 884744 | tf_op jit(solution)/shard_map/ppermute | solution.py:58
  14.9 7.0 %collective-permute-done.above.below = bf16[3,384,128]{2,1,0:T(8,128)(2,1)S(1)} collective-permute-done((bf16[3,384,128]{2,1,0:T(8,128)(2,1)S(1)}, bf16[3,384,128]{2,1,0:T(8,128)(2,1)S(1)}, u32[]{:S(2)}, u32[]{:S(2)}) %collective-permute-start) | collective-permute-done | bytes 294944 | tf_op jit(solution)/shard_map/ppermute | solution.py:58
  21.9 1.0 copy.14.kernel
  22.9 0.5 collective-permute-done.2.above_side.below_side
  23.4 6.6 %conv_forward.1 = (bf16[400,512]{1,0:T(8,128)(2,1)}, f32[384,512]{1,0:T(8,128)S(1)}, f32[8,512]{1,0:T(8,128)S(1)}) custom-call(bf16[4,384,128]{2,1,0:T(8,128)(2,1)S(1)} %bitcast.18, bf16[3,384,128]{2,1,0:T(8,128)(2,1)S(1)} %collective-permute-done.above.below, bf16[3,384,128]{2,1,0:T(8,128)(2,1)S(1)} %collective-permute-done.above.below, ...), custom_call_target="tpu_custom_call" | custom-call | flops 1000 | bytes 1000 | tf_op jit(solution)/shard_map/conv_forward/pallas_call | solution.py:174
  30.1 0.9 copy-done.4
  30.9 0.0 all-gather.5.cloned.1.call-update
  31.0 0.0 reduce-scatter.2.cloned.1.call-start
  31.0 19.6 %all-gather.7.cloned.1.call-done = bf16[1536,512]{1,0:T(8,128)(2,1)} async-done(((bf16[384,512]{1,0:T(8,128)(2,1)}), bf16[1536,512]{1,0:T(8,128)(2,1)}) %all-gather.7.cloned.1.call-update) | async-done | bytes 1572880 | tf_op jit(solution)/shard_map/all_gather | solution.py:662
  50.6 1.5 collective-permute-start.6
  52.1 1.3 collective-permute-start.5
  53.4 0.7 collective-permute-start.4
  54.0 1.4 collective-permute-start.3
  55.4 0.6 broadcast_in_dim.4.bias
  56.0 1.9 collective-permute-done.4.refs_2_
  58.0 1.6 collective-permute-done.3.refs_1_
  59.5 0.0 copy-start.16
  59.6 0.6 copy-done.16
  60.2 8.2 %cotangent_stage.1 = (f32[1536,128]{1,0:T(8,128)}, f32[1536,128]{1,0:T(8,128)}, f32[1536,512]{1,0:T(8,128)}) custom-call(bf16[4,384,512]{2,1,0:T(8,128)(2,1)} %bitcast.25, bf16[1536,1536]{1,0:T(8,128)(2,1)} %w_reduce.3, f32[1,1536]{1,0:T(1,128)} %broadcast_in_dim.4.bias, bf16[16,384]{1,0:T(8,128)(2,1)} %copy-done.9, bf16[16,384]{1,0:T(8,128)(2,1)} %copy-done.16, ...), custom_call_target="tpu_custom_call" | custom-call | flops 1000 | bytes 1000 | tf_op jit(solution)/shard_map/cotangent_stage/pallas_call | solution.py:348
  68.3 21.6 %all-gather.5.cloned.1.call-done = bf16[1600,512]{1,0:T(8,128)(2,1)} async-done(((bf16[400,512]{1,0:T(8,128)(2,1)}), bf16[1600,512]{1,0:T(8,128)(2,1)}) %all-gather.5.cloned.1.call-update) | async-done | bytes 1638416 | tf_op jit(solution)/shard_map/all_gather | solution.py:665
  89.9 1.1 copy-done
  91.0 1.4 copy-done.3
  92.5 1.5 norm.1
  94.0 0.0 copy-start.7
  94.0 0.6 copy-done.7
  94.6 1.4 collective-permute-start.7
  96.0 11.9 %pointwise_block.1 = (bf16[1536,512]{1,0:T(8,128)(2,1)}, bf16[1536,512]{1,0:T(8,128)(2,1)}, bf16[400,512]{1,0:T(8,128)(2,1)}, bf16[400,512]{1,0:T(8,128)(2,1)}, ...) custom-call(bf16[1536,512]{1,0:T(8,128)(2,1)} %copy-done.2, f32[1536,128]{1,0:T(8,128)} %get-tuple-element.55.gain, ...), custom_call_target="tpu_custom_call" | custom-call | flops 1000 | bytes 1000 | tf_op jit(solution)/shard_map/pointwise_block/pallas_call | solution.py:464
  107.9 0.5 collective-permute-start.8
  108.4 1.4 collective-permute-start.9
  109.8 2.4 %collective-permute-start.10 = (bf16[400,512]{1,0:T(8,128)(2,1)}, bf16[400,512]{1,0:T(8,128)(2,1)}, u32[]{:S(2)}, u32[]{:S(2)}) collective-permute-start(bf16[400,512]{1,0:T(8,128)(2,1)} %get-tuple-element.69), channel_id=1, source_target_pairs={{0,12},{4,0},{8,4},{12,8},{1,13},{5,1},{9,5},{13,9},{2,14},{6,2},{... | collective-permute-start | bytes 1228808 | tf_op jit(solution)/shard_map/ppermute | solution.py:637
  112.2 6.2 %reduced_product.1 = bf16[1536,512]{1,0:T(8,128)(2,1)} custom-call(bf16[1536,1536]{1,0:T(8,128)(2,1)} %w_reduce.3, bf16[1536,512]{1,0:T(8,128)(2,1)} %get-tuple-element.61.hidden), custom_call_target="tpu_custom_call" | custom-call | flops 1000 | bytes 1000 | tf_op jit(solution)/shard_map/reduced_product/pallas_call | solution.py:492
  118.4 9.0 %own_tile_gradients.1 = (bf16[1536,1536]{1,0:T(8,128)(2,1)}, bf16[1536,1536]{1,0:T(8,128)(2,1)}) custom-call(bf16[1536,512]{1,0:T(8,128)(2,1)} %copy-done.2, bf16[4,384,512]{2,1,0:T(8,128)(2,1)} %bitcast.26, bf16[1536,512]{1,0:T(8,128)(2,1)} %get-tuple-element.61.hidden, bf16[1536,512]{1,0:T(8,128)(2,1)} %get-tuple-element.62.grad_pre), custom_call_target="tpu_custom_call" | custom-call | flops 1000 | bytes 1000 | tf_op jit(solution)/shard_map/own_tile_gradients/pallas_call | solution.py:523
  127.4 3.4 %collective-permute-done.7.normed = bf16[1536,512]{1,0:T(8,128)(2,1)} collective-permute-done((bf16[1536,512]{1,0:T(8,128)(2,1)S(1)}, bf16[1536,512]{1,0:T(8,128)(2,1)}, u32[]{:S(2)}, u32[]{:S(2)}) %collective-permute-start.7) | collective-permute-done | bytes 1572896 | tf_op jit(solution)/shard_map/ppermute | solution.py:647
  130.9 16.6 %two_tile_gradients.1 = (bf16[1536,1536]{1,0:T(8,128)(2,1)}, bf16[1536,1536]{1,0:T(8,128)(2,1)}) custom-call(bf16[1536,512]{1,0:T(8,128)(2,1)} %collective-permute-done.7.normed, bf16[4,384,512]{2,1,0:T(8,128)(2,1)} %collective-permute-done.6.cot_all, bf16[1536,1536]{1,0:T(8,128)(2,1)} %get-tuple-element.63.reduce_own, ...), custom_call_target="tpu_custom_call" | custom-call | flops 1000 | bytes 1000 | tf_op jit(solution)/shard_map/two_tile_gradients/pallas_call | solution.py:559
  147.5 1.1 copy-done.5
  148.6 1.9 norm_gradient.1.gradient.block
  150.5 0.1 collective-permute-start.15
  150.6 0.5 collective-permute-start.11
  151.1 1.4 collective-permute-start.12
  152.5 0.0 reduce-scatter.2.cloned.1.call-update
  152.5 0.1 collective-permute-start.13
  152.6 6.2 %kernel_gradient.1 = f32[384,128]{1,0:T(8,128)S(1)} custom-call(bf16[4,384,128]{2,1,0:T(8,128)(2,1)S(1)} %bitcast.19, bf16[3,384,128]{2,1,0:T(8,128)(2,1)S(1)} %collective-permute-done.above.below, bf16[3,384,128]{2,1,0:T(8,128)(2,1)S(1)} %collective-permute-done.above.below, bf16[4,384,128]{2,1,0:T(8,128)(2,1)S(1)} %collective-permute-done.1.side, ...), custom_call_target="tpu_custom_call" | custom-call | flops 1000 | bytes 1000 | tf_op jit(solution)/shard_map/kernel_gradient/pallas_call | solution.py:248
  158.9 1.3 collective-permute-done.12.above.below
  160.2 7.3 %add_convert_fusion = bf16[1536,1536]{1,0:T(8,128)(2,1)} fusion(bf16[1536,1536]{1,0:T(8,128)(2,1)} %collective-permute-done.15, bf16[1536,1536]{1,0:T(8,128)(2,1)} %get-tuple-element.84), kind=kLoop, calls=%fused_computation | loop fusion | flops 9437184 | bytes 14155776 | tf_op jit(solution)/shard_map/convert_element_type | solution.py:581
  167.5 5.7 %conv_backward.1 = bf16[4,384,128]{2,1,0:T(8,128)(2,1)S(1)} custom-call(bf16[4,384,128]{2,1,0:T(8,128)(2,1)S(1)} %norm_gradient.1.gradient.block, bf16[3,384,128]{2,1,0:T(8,128)(2,1)S(1)} %collective-permute-done.12.above.below, bf16[3,384,128]{2,1,0:T(8,128)(2,1)S(1)} %collective-permute-done.12.above.below, ...), custom_call_target="tpu_custom_call" | custom-call | flops 1000 | bytes 1000 | tf_op jit(solution)/shard_map/conv_backward/pallas_call | solution.py:206
  173.2 0.6 collective-permute-start.16
  173.8 0.1 convert.1
  173.9 1.0 collective-permute-done.16
  174.9 0.0 copy-start.11
  174.9 1.4 collective-permute-start.17
  176.3 5.8 %add_convert_fusion.1 = bf16[1536,1536]{1,0:T(8,128)(2,1)} fusion(bf16[1536,1536]{1,0:T(8,128)(2,1)} %collective-permute-done.11, bf16[1536,1536]{1,0:T(8,128)(2,1)S(1)} %bitcast.28), kind=kLoop, calls=%fused_computation.1 | loop fusion | flops 9437184 | bytes 14155776 | tf_op jit(solution)/shard_map/convert_element_type | solution.py:581
  182.1 1.1 copy.17
  183.2 2.9 %reduce-scatter.2.cloned.1.call-done = bf16[384,512]{1,0:T(8,128)(2,1)} async-done(((bf16[1536,512]{1,0:T(8,128)(2,1)}), bf16[384,512]{1,0:T(8,128)(2,1)}) %reduce-scatter.2.cloned.1.call-update) | async-done | bytes 393232 | tf_op jit(solution)/shard_map/reduce_scatter | solution.py:683
  186.1 1.1 fusion
  187.3 0.8 reshape.17
  188.1 0.8 copy.18
  (48 shorter events, 0.2 us)
Async XLA Ops:
  7.2 48.3 %copy-start.17 = (f32[1536]{0:T(1024)S(1)}, f32[1536]{0:T(1024)}, u32[]{:S(2)}) copy-start(f32[1536]{0:T(1024)} %param.12) | copy-start | bytes 18436
  7.2 43.5 %all-gather.7.cloned.1.call-start = ((), (), s32[]{:S(2)}) async-start(), calls=%async_computation.3 | async-start | bytes 1966080 | tf_op jit(solution)/shard_map/all_gather | solution.py:662
  8.3 0.7 copy-start.10
  9.0 0.7 copy-start.12
  10.7 48.9 %copy-start.9 = (bf16[16,384]{1,0:T(8,128)(2,1)}, bf16[16,384]{1,0:T(8,128)(2,1)S(1)}, u32[]{:S(2)}) copy-start(bf16[16,384]{1,0:T(8,128)(2,1)S(1)} %get-tuple-element.54.refs_0_) | copy-start | bytes 36868
  10.7 79.2 %all-gather.5.cloned.1.call-start = ((), (), s32[]{:S(2)}) async-start(), calls=%async_computation.2 | async-start | bytes 2048000 | tf_op jit(solution)/shard_map/all_gather | solution.py:665
  11.8 10.0 %collective-permute-start = (bf16[3,384,128]{2,1,0:T(8,128)(2,1)S(1)}, bf16[3,384,128]{2,1,0:T(8,128)(2,1)S(1)}, u32[]{:S(2)}, u32[]{:S(2)}) collective-permute-start(bf16[3,384,128]{2,1,0:T(8,128)(2,1)S(1)} %slice_select_fusion.1), channel_id=1, source_target_pairs={{0,2},{2,0},{1,3},{3,1},{4,6},{6,4},{5,7},{7,5},{8,10},{10,8},{9,1... | collective-permute-start | bytes 884744 | tf_op jit(solution)/shard_map/ppermute | solution.py:58
  14.8 8.0 %collective-permute-start.1 = (bf16[4,384,128]{2,1,0:T(8,128)(2,1)S(1)}, bf16[4,384,128]{2,1,0:T(8,128)(2,1)S(1)}, u32[]{:S(2)}, u32[]{:S(2)}) collective-permute-start(bf16[4,384,128]{2,1,0:T(8,128)(2,1)S(1)} %bitcast.17), channel_id=1, source_target_pairs={{0,1},{1,0},{2,3},{3,2},{4,5},{5,4},{6,7},{7,6},{8,9},{9,8},{10,11... | collective-permute-start | bytes 1179656 | tf_op jit(solution)/shard_map/ppermute | solution.py:68
  21.9 1.6 collective-permute-start.2
  30.1 0.9 copy-start.4
  31.0 155.1 %reduce-scatter.2.cloned.1.call-start = ((), (), s32[]{:S(2)}) async-start(), calls=%async_computation.1 | async-start | bytes 1966080 | tf_op jit(solution)/shard_map/reduce_scatter | solution.py:683
  50.6 45.4 %collective-permute-start.6 = (bf16[4,384,512]{2,1,0:T(8,128)(2,1)}, bf16[4,384,512]{2,1,0:T(8,128)(2,1)}, u32[]{:S(2)}, u32[]{:S(2)}) collective-permute-start(bf16[4,384,512]{2,1,0:T(8,128)(2,1)} %bitcast.24), channel_id=1, source_target_pairs={{0,2},{2,0},{1,3},{3,1},{4,6},{6,4},{5,7},{7,5},{8,10},{10,8},{9,1... | collective-permute-start | bytes 4718600 | tf_op jit(solution)/shard_map/ppermute | solution.py:647
  52.1 3.9 %collective-permute-start.5 = (bf16[16,384]{1,0:T(8,128)(2,1)S(1)}, bf16[16,384]{1,0:T(8,128)(2,1)S(1)}, u32[]{:S(2)}, u32[]{:S(2)}) collective-permute-start(bf16[16,384]{1,0:T(8,128)(2,1)S(1)} %get-tuple-element.54.refs_0_), channel_id=1, source_target_pairs={{0,12},{4,0},{8,4},{12,8},{1,13},{5,1},{9,5},{13,9},{2,14},{6,2},{... | collective-permute-start | bytes 36872 | tf_op jit(solution)/shard_map/ppermute | solution.py:672
  53.4 4.6 %collective-permute-start.4 = (bf16[16,384]{1,0:T(8,128)(2,1)S(1)}, bf16[16,384]{1,0:T(8,128)(2,1)S(1)}, u32[]{:S(2)}, u32[]{:S(2)}) collective-permute-start(bf16[16,384]{1,0:T(8,128)(2,1)S(1)} %get-tuple-element.54.refs_0_), channel_id=1, source_target_pairs={{0,8},{4,12},{8,0},{12,4},{1,9},{5,13},{9,1},{13,5},{2,10},{6,14},... | collective-permute-start | bytes 36872 | tf_op jit(solution)/shard_map/ppermute | solution.py:672
  54.0 5.5 %collective-permute-start.3 = (bf16[16,384]{1,0:T(8,128)(2,1)S(1)}, bf16[16,384]{1,0:T(8,128)(2,1)S(1)}, u32[]{:S(2)}, u32[]{:S(2)}) collective-permute-start(bf16[16,384]{1,0:T(8,128)(2,1)S(1)} %get-tuple-element.54.refs_0_), channel_id=1, source_target_pairs={{0,4},{4,8},{8,12},{12,0},{1,5},{5,9},{9,13},{13,1},{2,6},{6,10},{... | collective-permute-start | bytes 36872 | tf_op jit(solution)/shard_map/ppermute | solution.py:672
  56.0 3.5 %copy-start.14 = (bf16[16,384]{1,0:T(8,128)(2,1)}, bf16[16,384]{1,0:T(8,128)(2,1)S(1)}, u32[]{:S(2)}) copy-start(bf16[16,384]{1,0:T(8,128)(2,1)S(1)} %collective-permute-done.5.refs_3_) | copy-start | bytes 36868
  58.0 1.6 copy-start.15
  59.5 0.6 copy-start.16
  89.9 1.1 copy-start
  91.0 1.4 copy-start.3
  94.0 0.6 copy-start.7
  94.6 1.4 copy-start.2
  94.6 36.3 %collective-permute-start.7 = (bf16[1536,512]{1,0:T(8,128)(2,1)S(1)}, bf16[1536,512]{1,0:T(8,128)(2,1)}, u32[]{:S(2)}, u32[]{:S(2)}) collective-permute-start(bf16[1536,512]{1,0:T(8,128)(2,1)S(1)} %get-tuple-element.57.normed), channel_id=1, source_target_pairs={{0,2},{2,0},{1,3},{3,1},{4,6},{6,4},{5,7},{7,5},{8,10},{10,8},{9,1... | collective-permute-start | bytes 4718600 | tf_op jit(solution)/shard_map/ppermute | solution.py:647
  107.9 39.5 %collective-permute-start.8 = (bf16[400,512]{1,0:T(8,128)(2,1)}, bf16[400,512]{1,0:T(8,128)(2,1)}, u32[]{:S(2)}, u32[]{:S(2)}) collective-permute-start(bf16[400,512]{1,0:T(8,128)(2,1)} %get-tuple-element.67), channel_id=1, source_target_pairs={{0,4},{4,8},{8,12},{12,0},{1,5},{5,9},{9,13},{13,1},{2,6},{6,10},{... | collective-permute-start | bytes 1228808 | tf_op jit(solution)/shard_map/ppermute | solution.py:637
  108.4 39.1 %collective-permute-start.9 = (bf16[400,512]{1,0:T(8,128)(2,1)}, bf16[400,512]{1,0:T(8,128)(2,1)}, u32[]{:S(2)}, u32[]{:S(2)}) collective-permute-start(bf16[400,512]{1,0:T(8,128)(2,1)} %get-tuple-element.68), channel_id=1, source_target_pairs={{0,8},{4,12},{8,0},{12,4},{1,9},{5,13},{9,1},{13,5},{2,10},{6,14},... | collective-permute-start | bytes 1228808 | tf_op jit(solution)/shard_map/ppermute | solution.py:637
  109.8 37.7 %collective-permute-start.10 = (bf16[400,512]{1,0:T(8,128)(2,1)}, bf16[400,512]{1,0:T(8,128)(2,1)}, u32[]{:S(2)}, u32[]{:S(2)}) collective-permute-start(bf16[400,512]{1,0:T(8,128)(2,1)} %get-tuple-element.69), channel_id=1, source_target_pairs={{0,12},{4,0},{8,4},{12,8},{1,13},{5,1},{9,5},{13,9},{2,14},{6,2},{... | collective-permute-start | bytes 1228808 | tf_op jit(solution)/shard_map/ppermute | solution.py:637
  130.9 16.6 %copy-start.1 = (f32[1536,128]{1,0:T(8,128)S(1)}, f32[1536,128]{1,0:T(8,128)}, u32[]{:S(2)}) copy-start(f32[1536,128]{1,0:T(8,128)} %get-tuple-element.55.gain) | copy-start | bytes 2359300
  130.9 16.6 %copy-start.6 = (bf16[400,512]{1,0:T(8,128)(2,1)S(1)}, bf16[400,512]{1,0:T(8,128)(2,1)}, u32[]{:S(2)}) copy-start(bf16[400,512]{1,0:T(8,128)(2,1)} %get-tuple-element.77.refs_0_) | copy-start | bytes 1228804
  130.9 16.6 %copy-start.8 = (f32[8,512]{1,0:T(8,128)S(1)}, f32[8,512]{1,0:T(8,128)}, u32[]{:S(2)}) copy-start(f32[8,512]{1,0:T(8,128)} %copy-done.7) | copy-start | bytes 49156
  147.5 1.1 copy-start.5
  150.5 9.7 %collective-permute-start.15 = (bf16[1536,1536]{1,0:T(8,128)(2,1)}, bf16[1536,1536]{1,0:T(8,128)(2,1)}, u32[]{:S(2)}, u32[]{:S(2)}) collective-permute-start(bf16[1536,1536]{1,0:T(8,128)(2,1)} %get-tuple-element.84), channel_id=1, source_target_pairs={{0,1},{1,0},{2,3},{3,2},{4,5},{5,4},{6,7},{7,6},{8,9},{9,8},{10,11... | collective-permute-start | bytes 14155784 | tf_op jit(solution)/shard_map/ppermute | solution.py:647
  150.6 25.7 %collective-permute-start.11 = (bf16[1536,1536]{1,0:T(8,128)(2,1)}, bf16[1536,1536]{1,0:T(8,128)(2,1)}, u32[]{:S(2)}, u32[]{:S(2)}) collective-permute-start(bf16[1536,1536]{1,0:T(8,128)(2,1)} %get-tuple-element.81), channel_id=1, source_target_pairs={{0,1},{1,0},{2,3},{3,2},{4,5},{5,4},{6,7},{7,6},{8,9},{9,8},{10,11... | collective-permute-start | bytes 14155784 | tf_op jit(solution)/shard_map/ppermute | solution.py:647
  151.1 9.1 %collective-permute-start.12 = (bf16[3,384,128]{2,1,0:T(8,128)(2,1)S(1)}, bf16[3,384,128]{2,1,0:T(8,128)(2,1)S(1)}, u32[]{:S(2)}, u32[]{:S(2)}) collective-permute-start(bf16[3,384,128]{2,1,0:T(8,128)(2,1)S(1)} %slice_select_fusion), channel_id=1, source_target_pairs={{0,2},{2,0},{1,3},{3,1},{4,6},{6,4},{5,7},{7,5},{8,10},{10,8},{9,1... | collective-permute-start | bytes 884744 | tf_op jit(solution)/shard_map/ppermute | solution.py:58
  152.5 14.9 %collective-permute-start.13 = (bf16[4,384,128]{2,1,0:T(8,128)(2,1)S(1)}, bf16[4,384,128]{2,1,0:T(8,128)(2,1)S(1)}, u32[]{:S(2)}, u32[]{:S(2)}) collective-permute-start(bf16[4,384,128]{2,1,0:T(8,128)(2,1)S(1)} %norm_gradient.1.gradient.block), channel_id=1, source_target_pairs={{0,1},{1,0},{2,3},{3,2},{4,5},{5,4},{6,7},{7,6},{8,9},{9,8},{10,11... | collective-permute-start | bytes 1179656 | tf_op jit(solution)/shard_map/ppermute | solution.py:68
  152.6 23.7 %slice-start = ((s8[4718592]{0:T(1024)(128)(4,1)}), s8[4194304]{0:T(1024)(128)(4,1)S(1)}, s32[]{:S(2)}) async-start(s8[4718592]{0:T(1024)(128)(4,1)} %bitcast.27), calls=%async_computation.4 | async-start | bytes 8388608
  158.8 14.9 %copy-start.13 = (bf16[384,4,128]{2,1,0:T(4,128)(2,1)S(1)}, bf16[384,4,128]{2,1,0:T(4,128)(2,1)}, u32[]{:S(2)}) copy-start(bf16[384,4,128]{2,1,0:T(4,128)(2,1)} %param.8) | copy-start | bytes 1179652
  158.8 17.4 %slice-start.1 = ((s8[4718592]{0:T(1024)(128)(4,1)}), s8[524288]{0:T(1024)(128)(4,1)S(1)}, s32[]{:S(2)}) async-start(s8[4718592]{0:T(1024)(128)(4,1)} %bitcast.27), calls=%async_computation.5 | async-start | bytes 1048576
  160.2 7.3 %collective-permute-start.14 = (bf16[3,384,128]{2,1,0:T(8,128)(2,1)S(1)}, bf16[3,384,128]{2,1,0:T(8,128)(2,1)S(1)}, u32[]{:S(2)}, u32[]{:S(2)}) collective-permute-start(bf16[3,384,128]{2,1,0:T(8,128)(2,1)S(1)} %collective-permute-done.12.above.below), channel_id=1, source_target_pairs={{0,1},{1,0},{2,3},{3,2},{4,5},{5,4},{6,7},{7,6},{8,9},{9,8},{10,11... | collective-permute-start | bytes 884744 | tf_op jit(solution)/shard_map/ppermute | solution.py:68
  173.2 1.7 collective-permute-start.16
  174.9 11.3 %copy-start.11 = (f32[384]{0:T(512)S(1)}, f32[384]{0:T(512)}, u32[]{:S(2)}) copy-start(f32[384]{0:T(512)} %scale.1) | copy-start | bytes 4612
  174.9 8.3 %collective-permute-start.17 = (f32[384,128]{1,0:T(8,128)S(1)}, f32[384,128]{1,0:T(8,128)S(1)}, u32[]{:S(2)}, u32[]{:S(2)}) collective-permute-start(f32[384,128]{1,0:T(8,128)S(1)} %add.19), channel_id=1, source_target_pairs={{0,2},{2,0},{1,3},{3,1},{4,6},{6,4},{5,7},{7,5},{8,10},{10,8},{9,1... | collective-permute-start | bytes 589832 | tf_op jit(solution)/shard_map/ppermute | solution.py:647
Sparse Core Ops, SparseCore 0:
  10.8 39.7 all-gather.6
  52.8 37.0 all-gather.4
  152.6 33.4 reduce-scatter.1

commit v6 on v5

--- a/solution.py
+++ b/solution.py
@@ -273,7 +273,7 @@
         out_shape=(shape((channels, rows * width), BF16), shape((PAD, channels), BF16)),
         in_specs=[whole] * 3,
         out_specs=(whole, whole),
-        compiler_params=params(32),
+        compiler_params=params(60),
         cost_estimate=LIGHT,
         name="pack_cotangent",
     )(cotangent, scale, gain)

time: 196 us -> 196 us (level)
    unnamed x45 -> x47, local copies, waits for them, and re-layouts: 12.1 us -> 12.1 us
where the time goes in v6:
time: 196 us
  Pallas kernels  75.8 us (39%)
  waiting for transfers between devices  60.3 us (31%)
  starting transfers between devices  17.6 us (9%)
  other arithmetic  14.4 us (7%)
  between operations  14 us (7%)
  local copies, waits for them, and re-layouts  13.5 us (7%)
    all_gather x1, waiting for transfers between devices, on_device(): conv_all = lax.all_gather(packed_conv, 'chan')  21.6 us
    all_gather x1, waiting for transfers between devices, on_device(): cot_all = lax.all_gather(packed_cot, 'chan')  19 us
    pallas_call x1, Pallas kernels, two_tile_gradients(): pl.pallas_call(other_tile_kernel, grid=(units // tile,), out_shape=(shape...  16.6 us
    convert_element_type x2, other arithmetic, pair_sum(): return (mine.astype(F32) + theirs.astype(F32)).astype(BF16)  13.1 us
    unnamed x47, local copies, waits for them, and re-layouts  12.1 us
    pallas_call x1, Pallas kernels, block_stage(): pl.pallas_call(functools.partial(block_kernel, steps), grid=(steps,), out...  11.9 us
    pallas_call x1, Pallas kernels, own_tile_gradients(): pl.pallas_call(own_tile_kernel, grid=(units // tile,), out_shape=(shape((...  9.02 us
    ppermute x2, waiting for transfers between devices, from_sides(): got = lax.ppermute(sent, axis, [(0, 1), (1, 0)])  8.3 us
  transfers between devices with their start and end apart: 21, of which 10 were waited for; matrix products, arithmetic and copies ran while one was open for 9% of the time, Pallas kernels for 37%

profile of v6, /device:TPU:0, one launch (start us, length us, event | category | flops | bytes accessed | tf_op | source)
XLA Modules:
  0.0 195.7 jit_solution(8880976452987121987)
XLA Ops:
  7.2 0.0 all-gather.7.cloned.1.call-start
  7.2 1.8 copy.23
  9.0 2.0 %pack_cotangent.1 = (bf16[384,512]{1,0:T(8,128)(2,1)}, bf16[16,384]{1,0:T(8,128)(2,1)}) custom-call(bf16[4,384,128]{2,1,0:T(8,128)(2,1)} %bitcast.20, f32[384]{0:T(512)} %scale.1, f32[384]{0:T(512)} %gain.1), custom_call_target="tpu_custom_call" | custom-call | flops 1000 | bytes 1000 | tf_op jit(solution)/shard_map/pack_cotangent/pallas_call | solution.py:271
  11.1 0.0 all-gather.7.cloned.1.call-update
  11.1 0.0 all-gather.5.cloned.1.call-start
  11.1 1.1 copy.24
  12.2 3.0 %collective-permute-start = (bf16[3,384,128]{2,1,0:T(8,128)(2,1)S(1)}, bf16[3,384,128]{2,1,0:T(8,128)(2,1)S(1)}, u32[]{:S(2)}, u32[]{:S(2)}) collective-permute-start(bf16[3,384,128]{2,1,0:T(8,128)(2,1)S(1)} %slice_select_fusion.1), channel_id=1, source_target_pairs={{0,2},{2,0},{1,3},{3,1},{4,6},{6,4},{5,7},{7,5},{8,10},{10,8},{9,1... | collective-permute-start | bytes 884744 | tf_op jit(solution)/shard_map/ppermute | solution.py:58
  15.2 7.0 %collective-permute-done.above.below = bf16[3,384,128]{2,1,0:T(8,128)(2,1)S(1)} collective-permute-done((bf16[3,384,128]{2,1,0:T(8,128)(2,1)S(1)}, bf16[3,384,128]{2,1,0:T(8,128)(2,1)S(1)}, u32[]{:S(2)}, u32[]{:S(2)}) %collective-permute-start) | collective-permute-done | bytes 294944 | tf_op jit(solution)/shard_map/ppermute | solution.py:58
  22.3 1.0 copy.14.kernel
  23.3 0.5 collective-permute-done.2.above_side.below_side
  23.8 6.6 %conv_forward.1 = (bf16[400,512]{1,0:T(8,128)(2,1)}, f32[384,512]{1,0:T(8,128)S(1)}, f32[8,512]{1,0:T(8,128)S(1)}) custom-call(bf16[4,384,128]{2,1,0:T(8,128)(2,1)S(1)} %bitcast.18, bf16[3,384,128]{2,1,0:T(8,128)(2,1)S(1)} %collective-permute-done.above.below, bf16[3,384,128]{2,1,0:T(8,128)(2,1)S(1)} %collective-permute-done.above.below, ...), custom_call_target="tpu_custom_call" | custom-call | flops 1000 | bytes 1000 | tf_op jit(solution)/shard_map/conv_forward/pallas_call | solution.py:174
  30.5 0.9 copy-done.5
  31.3 0.6 copy-done.8
  32.0 0.0 all-gather.5.cloned.1.call-update
  32.0 0.0 reduce-scatter.2.cloned.1.call-start
  32.0 19.0 %all-gather.7.cloned.1.call-done = bf16[1536,512]{1,0:T(8,128)(2,1)} async-done(((bf16[384,512]{1,0:T(8,128)(2,1)}), bf16[1536,512]{1,0:T(8,128)(2,1)}) %all-gather.7.cloned.1.call-update) | async-done | bytes 1572880 | tf_op jit(solution)/shard_map/all_gather | solution.py:662
  51.0 1.5 collective-permute-start.6
  52.5 1.3 collective-permute-start.5
  53.8 0.7 collective-permute-start.4
  54.4 1.4 collective-permute-start.3
  55.8 0.6 broadcast_in_dim.4.bias
  56.4 1.9 collective-permute-done.4.refs_2_
  58.4 1.6 collective-permute-done.3.refs_1_
  59.9 0.6 copy-done.16
  60.5 8.2 %cotangent_stage.1 = (f32[1536,128]{1,0:T(8,128)}, f32[1536,128]{1,0:T(8,128)}, f32[1536,512]{1,0:T(8,128)}) custom-call(bf16[4,384,512]{2,1,0:T(8,128)(2,1)} %bitcast.25, bf16[1536,1536]{1,0:T(8,128)(2,1)} %w_reduce.3, f32[1,1536]{1,0:T(1,128)} %broadcast_in_dim.4.bias, bf16[16,384]{1,0:T(8,128)(2,1)} %get-tuple-element.54.refs_0_, ...), custom_call_target="tpu_custom_call" | custom-call | flops 1000 | bytes 1000 | tf_op jit(solution)/shard_map/cotangent_stage/pallas_call | solution.py:348
  68.7 21.6 %all-gather.5.cloned.1.call-done = bf16[1600,512]{1,0:T(8,128)(2,1)} async-done(((bf16[400,512]{1,0:T(8,128)(2,1)}), bf16[1600,512]{1,0:T(8,128)(2,1)}) %all-gather.5.cloned.1.call-update) | async-done | bytes 1638416 | tf_op jit(solution)/shard_map/all_gather | solution.py:665
  90.3 1.1 copy-done
  91.4 1.4 copy-done.4
  92.8 1.5 norm.1
  94.3 0.0 copy-start.10
  94.4 0.6 copy-done.10
  95.0 1.4 collective-permute-start.7
  96.4 11.9 %pointwise_block.1 = (bf16[1536,512]{1,0:T(8,128)(2,1)}, bf16[1536,512]{1,0:T(8,128)(2,1)}, bf16[400,512]{1,0:T(8,128)(2,1)}, bf16[400,512]{1,0:T(8,128)(2,1)}, ...) custom-call(bf16[1536,512]{1,0:T(8,128)(2,1)} %copy-done.2, f32[1536,128]{1,0:T(8,128)} %get-tuple-element.55.gain, ...), custom_call_target="tpu_custom_call" | custom-call | flops 1000 | bytes 1000 | tf_op jit(solution)/shard_map/pointwise_block/pallas_call | solution.py:464
  108.3 0.5 collective-permute-start.8
  108.8 1.4 collective-permute-start.9
  110.2 2.4 %collective-permute-start.10 = (bf16[400,512]{1,0:T(8,128)(2,1)}, bf16[400,512]{1,0:T(8,128)(2,1)}, u32[]{:S(2)}, u32[]{:S(2)}) collective-permute-start(bf16[400,512]{1,0:T(8,128)(2,1)} %get-tuple-element.69), channel_id=1, source_target_pairs={{0,12},{4,0},{8,4},{12,8},{1,13},{5,1},{9,5},{13,9},{2,14},{6,2},{... | collective-permute-start | bytes 1228808 | tf_op jit(solution)/shard_map/ppermute | solution.py:637
  112.6 6.2 %reduced_product.1 = bf16[1536,512]{1,0:T(8,128)(2,1)} custom-call(bf16[1536,1536]{1,0:T(8,128)(2,1)} %w_reduce.3, bf16[1536,512]{1,0:T(8,128)(2,1)} %get-tuple-element.61.hidden), custom_call_target="tpu_custom_call" | custom-call | flops 1000 | bytes 1000 | tf_op jit(solution)/shard_map/reduced_product/pallas_call | solution.py:492
  118.8 9.0 %own_tile_gradients.1 = (bf16[1536,1536]{1,0:T(8,128)(2,1)}, bf16[1536,1536]{1,0:T(8,128)(2,1)}) custom-call(bf16[1536,512]{1,0:T(8,128)(2,1)} %copy-done.2, bf16[4,384,512]{2,1,0:T(8,128)(2,1)} %bitcast.26, bf16[1536,512]{1,0:T(8,128)(2,1)} %get-tuple-element.61.hidden, bf16[1536,512]{1,0:T(8,128)(2,1)} %get-tuple-element.62.grad_pre), custom_call_target="tpu_custom_call" | custom-call | flops 1000 | bytes 1000 | tf_op jit(solution)/shard_map/own_tile_gradients/pallas_call | solution.py:523
  127.8 3.4 %collective-permute-done.7.normed = bf16[1536,512]{1,0:T(8,128)(2,1)} collective-permute-done((bf16[1536,512]{1,0:T(8,128)(2,1)S(1)}, bf16[1536,512]{1,0:T(8,128)(2,1)}, u32[]{:S(2)}, u32[]{:S(2)}) %collective-permute-start.7) | collective-permute-done | bytes 1572896 | tf_op jit(solution)/shard_map/ppermute | solution.py:647
  131.3 16.6 %two_tile_gradients.1 = (bf16[1536,1536]{1,0:T(8,128)(2,1)}, bf16[1536,1536]{1,0:T(8,128)(2,1)}) custom-call(bf16[1536,512]{1,0:T(8,128)(2,1)} %collective-permute-done.7.normed, bf16[4,384,512]{2,1,0:T(8,128)(2,1)} %collective-permute-done.6.cot_all, bf16[1536,1536]{1,0:T(8,128)(2,1)} %get-tuple-element.63.reduce_own, ...), custom_call_target="tpu_custom_call" | custom-call | flops 1000 | bytes 1000 | tf_op jit(solution)/shard_map/two_tile_gradients/pallas_call | solution.py:559
  147.9 1.1 copy-done.6
  149.1 1.7 norm_gradient.1.gradient.block
  150.8 0.1 collective-permute-start.15
  150.9 0.5 collective-permute-start.11
  151.4 1.4 collective-permute-start.12
  152.8 0.0 reduce-scatter.2.cloned.1.call-update
  152.8 0.1 collective-permute-start.13
  152.9 6.2 %kernel_gradient.1 = f32[384,128]{1,0:T(8,128)S(1)} custom-call(bf16[4,384,128]{2,1,0:T(8,128)(2,1)S(1)} %bitcast.19, bf16[3,384,128]{2,1,0:T(8,128)(2,1)S(1)} %collective-permute-done.above.below, bf16[3,384,128]{2,1,0:T(8,128)(2,1)S(1)} %collective-permute-done.above.below, bf16[4,384,128]{2,1,0:T(8,128)(2,1)S(1)} %collective-permute-done.1.side, ...), custom_call_target="tpu_custom_call" | custom-call | flops 1000 | bytes 1000 | tf_op jit(solution)/shard_map/kernel_gradient/pallas_call | solution.py:248
  159.1 0.0 copy-start.3
  159.1 0.0 copy-start.12
  159.2 1.3 collective-permute-done.12.above.below
  160.5 7.3 %add_convert_fusion = bf16[1536,1536]{1,0:T(8,128)(2,1)} fusion(bf16[1536,1536]{1,0:T(8,128)(2,1)} %collective-permute-done.15, bf16[1536,1536]{1,0:T(8,128)(2,1)} %get-tuple-element.84), kind=kLoop, calls=%fused_computation | loop fusion | flops 9437184 | bytes 14155776 | tf_op jit(solution)/shard_map/convert_element_type | solution.py:581
  167.8 5.7 %conv_backward.1 = bf16[4,384,128]{2,1,0:T(8,128)(2,1)S(1)} custom-call(bf16[4,384,128]{2,1,0:T(8,128)(2,1)S(1)} %norm_gradient.1.gradient.block, bf16[3,384,128]{2,1,0:T(8,128)(2,1)S(1)} %collective-permute-done.12.above.below, bf16[3,384,128]{2,1,0:T(8,128)(2,1)S(1)} %collective-permute-done.12.above.below, ...), custom_call_target="tpu_custom_call" | custom-call | flops 1000 | bytes 1000 | tf_op jit(solution)/shard_map/conv_backward/pallas_call | solution.py:206
  173.5 0.6 collective-permute-start.16
  174.0 0.1 convert.1
  174.1 1.0 collective-permute-done.16
  175.1 0.0 copy-start.17
  175.1 1.4 collective-permute-start.17
  176.5 5.8 %add_convert_fusion.1 = bf16[1536,1536]{1,0:T(8,128)(2,1)} fusion(bf16[1536,1536]{1,0:T(8,128)(2,1)} %collective-permute-done.11, bf16[1536,1536]{1,0:T(8,128)(2,1)S(1)} %bitcast.28), kind=kLoop, calls=%fused_computation.1 | loop fusion | flops 9437184 | bytes 14155776 | tf_op jit(solution)/shard_map/convert_element_type | solution.py:581
  182.4 1.1 copy.17
  183.4 3.0 %reduce-scatter.2.cloned.1.call-done = bf16[384,512]{1,0:T(8,128)(2,1)} async-done(((bf16[1536,512]{1,0:T(8,128)(2,1)}), bf16[384,512]{1,0:T(8,128)(2,1)}) %reduce-scatter.2.cloned.1.call-update) | async-done | bytes 393232 | tf_op jit(solution)/shard_map/reduce_scatter | solution.py:683
  186.4 1.1 fusion
  187.6 0.8 reshape.17
  188.4 0.8 copy.18
  (50 shorter events, 0.2 us)
Async XLA Ops:
  7.2 48.7 %copy-start.18 = (f32[1536]{0:T(1024)S(1)}, f32[1536]{0:T(1024)}, u32[]{:S(2)}) copy-start(f32[1536]{0:T(1024)} %param.12) | copy-start | bytes 18436
  7.2 43.9 %all-gather.7.cloned.1.call-start = ((), (), s32[]{:S(2)}) async-start(), calls=%async_computation.3 | async-start | bytes 1966080 | tf_op jit(solution)/shard_map/all_gather | solution.py:662
  11.1 41.4 %copy-start.13 = (bf16[16,384]{1,0:T(8,128)(2,1)S(1)}, bf16[16,384]{1,0:T(8,128)(2,1)}, u32[]{:S(2)}) copy-start(bf16[16,384]{1,0:T(8,128)(2,1)} %get-tuple-element.54.refs_0_) | copy-start | bytes 36868
  11.1 79.2 %all-gather.5.cloned.1.call-start = ((), (), s32[]{:S(2)}) async-start(), calls=%async_computation.2 | async-start | bytes 2048000 | tf_op jit(solution)/shard_map/all_gather | solution.py:665
  12.2 10.0 %collective-permute-start = (bf16[3,384,128]{2,1,0:T(8,128)(2,1)S(1)}, bf16[3,384,128]{2,1,0:T(8,128)(2,1)S(1)}, u32[]{:S(2)}, u32[]{:S(2)}) collective-permute-start(bf16[3,384,128]{2,1,0:T(8,128)(2,1)S(1)} %slice_select_fusion.1), channel_id=1, source_target_pairs={{0,2},{2,0},{1,3},{3,1},{4,6},{6,4},{5,7},{7,5},{8,10},{10,8},{9,1... | collective-permute-start | bytes 884744 | tf_op jit(solution)/shard_map/ppermute | solution.py:58
  15.2 8.0 %collective-permute-start.1 = (bf16[4,384,128]{2,1,0:T(8,128)(2,1)S(1)}, bf16[4,384,128]{2,1,0:T(8,128)(2,1)S(1)}, u32[]{:S(2)}, u32[]{:S(2)}) collective-permute-start(bf16[4,384,128]{2,1,0:T(8,128)(2,1)S(1)} %bitcast.17), channel_id=1, source_target_pairs={{0,1},{1,0},{2,3},{3,2},{4,5},{5,4},{6,7},{7,6},{8,9},{9,8},{10,11... | collective-permute-start | bytes 1179656 | tf_op jit(solution)/shard_map/ppermute | solution.py:68
  22.2 1.6 collective-permute-start.2
  30.5 0.9 copy-start.5
  31.3 0.6 copy-start.8
  32.0 154.5 %reduce-scatter.2.cloned.1.call-start = ((), (), s32[]{:S(2)}) async-start(), calls=%async_computation.1 | async-start | bytes 1966080 | tf_op jit(solution)/shard_map/reduce_scatter | solution.py:683
  51.0 45.4 %collective-permute-start.6 = (bf16[4,384,512]{2,1,0:T(8,128)(2,1)}, bf16[4,384,512]{2,1,0:T(8,128)(2,1)}, u32[]{:S(2)}, u32[]{:S(2)}) collective-permute-start(bf16[4,384,512]{2,1,0:T(8,128)(2,1)} %bitcast.24), channel_id=1, source_target_pairs={{0,2},{2,0},{1,3},{3,1},{4,6},{6,4},{5,7},{7,5},{8,10},{10,8},{9,1... | collective-permute-start | bytes 4718600 | tf_op jit(solution)/shard_map/ppermute | solution.py:647
  52.5 3.9 %collective-permute-start.5 = (bf16[16,384]{1,0:T(8,128)(2,1)S(1)}, bf16[16,384]{1,0:T(8,128)(2,1)S(1)}, u32[]{:S(2)}, u32[]{:S(2)}) collective-permute-start(bf16[16,384]{1,0:T(8,128)(2,1)S(1)} %copy-done.13), channel_id=1, source_target_pairs={{0,12},{4,0},{8,4},{12,8},{1,13},{5,1},{9,5},{13,9},{2,14},{6,2},{... | collective-permute-start | bytes 36872 | tf_op jit(solution)/shard_map/ppermute | solution.py:672
  53.8 4.6 %collective-permute-start.4 = (bf16[16,384]{1,0:T(8,128)(2,1)S(1)}, bf16[16,384]{1,0:T(8,128)(2,1)S(1)}, u32[]{:S(2)}, u32[]{:S(2)}) collective-permute-start(bf16[16,384]{1,0:T(8,128)(2,1)S(1)} %copy-done.13), channel_id=1, source_target_pairs={{0,8},{4,12},{8,0},{12,4},{1,9},{5,13},{9,1},{13,5},{2,10},{6,14},... | collective-permute-start | bytes 36872 | tf_op jit(solution)/shard_map/ppermute | solution.py:672
  54.4 5.5 %collective-permute-start.3 = (bf16[16,384]{1,0:T(8,128)(2,1)S(1)}, bf16[16,384]{1,0:T(8,128)(2,1)S(1)}, u32[]{:S(2)}, u32[]{:S(2)}) collective-permute-start(bf16[16,384]{1,0:T(8,128)(2,1)S(1)} %copy-done.13), channel_id=1, source_target_pairs={{0,4},{4,8},{8,12},{12,0},{1,5},{5,9},{9,13},{13,1},{2,6},{6,10},{... | collective-permute-start | bytes 36872 | tf_op jit(solution)/shard_map/ppermute | solution.py:672
  56.4 3.5 %copy-start.14 = (bf16[16,384]{1,0:T(8,128)(2,1)}, bf16[16,384]{1,0:T(8,128)(2,1)S(1)}, u32[]{:S(2)}) copy-start(bf16[16,384]{1,0:T(8,128)(2,1)S(1)} %collective-permute-done.5.refs_3_) | copy-start | bytes 36868
  58.4 1.6 copy-start.15
  59.9 0.6 copy-start.16
  90.3 1.1 copy-start
  91.4 1.4 copy-start.4
  94.3 0.6 copy-start.10
  95.0 1.4 copy-start.2
  95.0 36.3 %collective-permute-start.7 = (bf16[1536,512]{1,0:T(8,128)(2,1)S(1)}, bf16[1536,512]{1,0:T(8,128)(2,1)}, u32[]{:S(2)}, u32[]{:S(2)}) collective-permute-start(bf16[1536,512]{1,0:T(8,128)(2,1)S(1)} %get-tuple-element.57.normed), channel_id=1, source_target_pairs={{0,2},{2,0},{1,3},{3,1},{4,6},{6,4},{5,7},{7,5},{8,10},{10,8},{9,1... | collective-permute-start | bytes 4718600 | tf_op jit(solution)/shard_map/ppermute | solution.py:647
  108.3 39.5 %collective-permute-start.8 = (bf16[400,512]{1,0:T(8,128)(2,1)}, bf16[400,512]{1,0:T(8,128)(2,1)S(1)}, u32[]{:S(2)}, u32[]{:S(2)}) collective-permute-start(bf16[400,512]{1,0:T(8,128)(2,1)} %get-tuple-element.67), channel_id=1, source_target_pairs={{0,4},{4,8},{8,12},{12,0},{1,5},{5,9},{9,13},{13,1},{2,6},{6,10},{... | collective-permute-start | bytes 1228808 | tf_op jit(solution)/shard_map/ppermute | solution.py:637
  108.8 39.1 %collective-permute-start.9 = (bf16[400,512]{1,0:T(8,128)(2,1)}, bf16[400,512]{1,0:T(8,128)(2,1)}, u32[]{:S(2)}, u32[]{:S(2)}) collective-permute-start(bf16[400,512]{1,0:T(8,128)(2,1)} %get-tuple-element.68), channel_id=1, source_target_pairs={{0,8},{4,12},{8,0},{12,4},{1,9},{5,13},{9,1},{13,5},{2,10},{6,14},... | collective-permute-start | bytes 1228808 | tf_op jit(solution)/shard_map/ppermute | solution.py:637
  110.2 37.7 %collective-permute-start.10 = (bf16[400,512]{1,0:T(8,128)(2,1)}, bf16[400,512]{1,0:T(8,128)(2,1)}, u32[]{:S(2)}, u32[]{:S(2)}) collective-permute-start(bf16[400,512]{1,0:T(8,128)(2,1)} %get-tuple-element.69), channel_id=1, source_target_pairs={{0,12},{4,0},{8,4},{12,8},{1,13},{5,1},{9,5},{13,9},{2,14},{6,2},{... | collective-permute-start | bytes 1228808 | tf_op jit(solution)/shard_map/ppermute | solution.py:637
  131.2 16.6 %copy-start.1 = (f32[1536,128]{1,0:T(8,128)S(1)}, f32[1536,128]{1,0:T(8,128)}, u32[]{:S(2)}) copy-start(f32[1536,128]{1,0:T(8,128)} %get-tuple-element.55.gain) | copy-start | bytes 2359300
  131.2 16.7 %copy-start.7 = (bf16[400,512]{1,0:T(8,128)(2,1)S(1)}, bf16[400,512]{1,0:T(8,128)(2,1)}, u32[]{:S(2)}) copy-start(bf16[400,512]{1,0:T(8,128)(2,1)} %get-tuple-element.77.refs_0_) | copy-start | bytes 1228804
  131.2 16.7 %copy-start.9 = (f32[8,512]{1,0:T(8,128)S(1)}, f32[8,512]{1,0:T(8,128)}, u32[]{:S(2)}) copy-start(f32[8,512]{1,0:T(8,128)} %copy-done.8) | copy-start | bytes 49156
  131.2 16.7 %copy-start.11 = (f32[8,512]{1,0:T(8,128)S(1)}, f32[8,512]{1,0:T(8,128)}, u32[]{:S(2)}) copy-start(f32[8,512]{1,0:T(8,128)} %copy-done.10) | copy-start | bytes 49156
  147.9 1.1 copy-start.6
  150.8 9.7 %collective-permute-start.15 = (bf16[1536,1536]{1,0:T(8,128)(2,1)}, bf16[1536,1536]{1,0:T(8,128)(2,1)}, u32[]{:S(2)}, u32[]{:S(2)}) collective-permute-start(bf16[1536,1536]{1,0:T(8,128)(2,1)} %get-tuple-element.84), channel_id=1, source_target_pairs={{0,1},{1,0},{2,3},{3,2},{4,5},{5,4},{6,7},{7,6},{8,9},{9,8},{10,11... | collective-permute-start | bytes 14155784 | tf_op jit(solution)/shard_map/ppermute | solution.py:647
  150.9 25.7 %collective-permute-start.11 = (bf16[1536,1536]{1,0:T(8,128)(2,1)}, bf16[1536,1536]{1,0:T(8,128)(2,1)}, u32[]{:S(2)}, u32[]{:S(2)}) collective-permute-start(bf16[1536,1536]{1,0:T(8,128)(2,1)} %get-tuple-element.81), channel_id=1, source_target_pairs={{0,1},{1,0},{2,3},{3,2},{4,5},{5,4},{6,7},{7,6},{8,9},{9,8},{10,11... | collective-permute-start | bytes 14155784 | tf_op jit(solution)/shard_map/ppermute | solution.py:647
  151.4 9.1 %collective-permute-start.12 = (bf16[3,384,128]{2,1,0:T(8,128)(2,1)S(1)}, bf16[3,384,128]{2,1,0:T(8,128)(2,1)S(1)}, u32[]{:S(2)}, u32[]{:S(2)}) collective-permute-start(bf16[3,384,128]{2,1,0:T(8,128)(2,1)S(1)} %slice_select_fusion), channel_id=1, source_target_pairs={{0,2},{2,0},{1,3},{3,1},{4,6},{6,4},{5,7},{7,5},{8,10},{10,8},{9,1... | collective-permute-start | bytes 884744 | tf_op jit(solution)/shard_map/ppermute | solution.py:58
  152.8 14.9 %collective-permute-start.13 = (bf16[4,384,128]{2,1,0:T(8,128)(2,1)S(1)}, bf16[4,384,128]{2,1,0:T(8,128)(2,1)S(1)}, u32[]{:S(2)}, u32[]{:S(2)}) collective-permute-start(bf16[4,384,128]{2,1,0:T(8,128)(2,1)S(1)} %norm_gradient.1.gradient.block), channel_id=1, source_target_pairs={{0,1},{1,0},{2,3},{3,2},{4,5},{5,4},{6,7},{7,6},{8,9},{9,8},{10,11... | collective-permute-start | bytes 1179656 | tf_op jit(solution)/shard_map/ppermute | solution.py:68
  152.9 23.6 %slice-start = ((s8[4718592]{0:T(1024)(128)(4,1)}), s8[4194304]{0:T(1024)(128)(4,1)S(1)}, s32[]{:S(2)}) async-start(s8[4718592]{0:T(1024)(128)(4,1)} %bitcast.27), calls=%async_computation.4 | async-start | bytes 8388608
  159.1 8.6 %copy-start.3 = (bf16[384,4,128]{2,0,1:T(8,128)(2,1)S(1)}, bf16[384,4,128]{2,0,1:T(8,128)(2,1)}, u32[]{:S(2)}) copy-start(bf16[384,4,128]{2,0,1:T(8,128)(2,1)} %copy.23) | copy-start | bytes 1179652
  159.1 14.9 %copy-start.12 = (bf16[384,4,128]{2,1,0:T(4,128)(2,1)S(1)}, bf16[384,4,128]{2,1,0:T(4,128)(2,1)}, u32[]{:S(2)}) copy-start(bf16[384,4,128]{2,1,0:T(4,128)(2,1)} %param.8) | copy-start | bytes 1179652
  159.2 17.4 %slice-start.1 = ((s8[4718592]{0:T(1024)(128)(4,1)}), s8[524288]{0:T(1024)(128)(4,1)S(1)}, s32[]{:S(2)}) async-start(s8[4718592]{0:T(1024)(128)(4,1)} %bitcast.27), calls=%async_computation.5 | async-start | bytes 1048576
  160.5 7.3 %collective-permute-start.14 = (bf16[3,384,128]{2,1,0:T(8,128)(2,1)S(1)}, bf16[3,384,128]{2,1,0:T(8,128)(2,1)S(1)}, u32[]{:S(2)}, u32[]{:S(2)}) collective-permute-start(bf16[3,384,128]{2,1,0:T(8,128)(2,1)S(1)} %collective-permute-done.12.above.below), channel_id=1, source_target_pairs={{0,1},{1,0},{2,3},{3,2},{4,5},{5,4},{6,7},{7,6},{8,9},{9,8},{10,11... | collective-permute-start | bytes 884744 | tf_op jit(solution)/shard_map/ppermute | solution.py:68
  173.5 1.6 collective-permute-start.16
  175.1 11.3 %copy-start.17 = (f32[384]{0:T(512)S(1)}, f32[384]{0:T(512)}, u32[]{:S(2)}) copy-start(f32[384]{0:T(512)} %scale.1) | copy-start | bytes 4612
  175.1 8.3 %collective-permute-start.17 = (f32[384,128]{1,0:T(8,128)S(1)}, f32[384,128]{1,0:T(8,128)S(1)}, u32[]{:S(2)}, u32[]{:S(2)}) collective-permute-start(f32[384,128]{1,0:T(8,128)S(1)} %add.19), channel_id=1, source_target_pairs={{0,2},{2,0},{1,3},{3,1},{4,6},{6,4},{5,7},{7,5},{8,10},{10,8},{9,1... | collective-permute-start | bytes 589832 | tf_op jit(solution)/shard_map/ppermute | solution.py:647
Sparse Core Ops, SparseCore 0:
  11.2 39.7 all-gather.6
  53.2 37.0 all-gather.4
  152.9 33.4 reduce-scatter.1
